TPU v7x, 32 devices: a whole 2x2x4 slice. The times are simulated.
32 devices in a mesh: groups: 2 (over y), dp: 4 (over x, core), tensor: 4 (over z).
Axes of the slice: x: 2, y: 2, z: 4, core: 2. Of those that a mesh axis runs over, the one named last changes fastest.
Arguments:
- tokens: bfloat16 [1, 64, 8192], P(None, 'groups', 'dp'), parts along dimension 1, may hold values from -6 to 6
- parents: int32 [1, 64], P(None, 'groups'), parts along dimension 1, may hold values from 0 to 31, as said below
- norm_gains: float32 [2, 8192], P(None, 'dp'), may hold values from 0.1 to 1.9
- weight_xz: bfloat16 [8192, 2, 8192], P('dp', None, 'tensor'), may hold values from -0.0625 to 0.0625
- weight_bc: bfloat16 [8192, 2, 1024], P('dp', None, 'tensor'), may hold values from -0.0625 to 0.0625
- weight_dt: bfloat16 [8192, 128], P('dp', 'tensor'), may hold values from -0.0625 to 0.0625
- conv_inner: float32 [4, 8192], P(None, 'tensor'), may hold values from -3 to 3
- conv_groups: float32 [4, 2, 1024], P(None, None, 'tensor'), may hold values from -3 to 3
- dt_bias: float32 [128], P('tensor'), may hold values from -3 to 1
- rates: float32 [128], P('tensor'), may hold values from 0.05 to 4
- skip_gain: float32 [128], P('tensor'), may hold values from 0.5 to 2
- gate_gain: float32 [8192], P('tensor'), may hold values from 0.1 to 1.9
- weight_out: bfloat16 [8192, 8192], P('tensor', 'dp'), may hold values from -0.0625 to 0.0625
- weight_up: bfloat16 [8192, 16384], P('dp', 'tensor'), may hold values from -0.0625 to 0.0625
- weight_down: bfloat16 [16384, 8192], P('tensor', 'dp'), may hold values from -0.046875 to 0.046875
- ssm_state: bfloat16 [64, 128, 64, 128], P(('groups', 'dp'), 'tensor'), parts along dimension 0, may hold values from -4 to 4
- queue_inner: bfloat16 [64, 3, 8192], P(('groups', 'dp'), None, 'tensor'), parts along dimension 0, may hold values from -6 to 6
- queue_groups: bfloat16 [64, 3, 2, 1024], P(('groups', 'dp'), None, None, 'tensor'), parts along dimension 0, may hold values from -6 to 6
Outputs:
- beam_out: bfloat16 [1, 64, 8192], P(None, 'groups', 'dp'), parts along dimension 1
- final_state: bfloat16 [64, 128, 64, 128], P(('groups', 'dp'), 'tensor'), parts along dimension 0
- final_inner: bfloat16 [64, 3, 8192], P(('groups', 'dp'), None, 'tensor'), parts along dimension 0
- final_groups: bfloat16 [64, 3, 2, 1024], P(('groups', 'dp'), None, None, 'tensor'), parts along dimension 0
There are 2 independent parts, one for each index of `groups`. A program takes and returns all parts, laid end to end along the dimension named above; an argument that names none is the same for every part. Nothing has to cross between parts.
Inputs may be any that keep to these rules, and one draw needn't show every extreme that they name: At each step the 8 rows of one index of dp (rows i * 8 to (i + 1) * 8 - 1) take at most 4 parents from the rows of any one index of dp, its own included, and exactly 4 from some index.
All inputs are finite; a program needn't handle non-finite values.
Results may differ from a plain program's by a relative error of at most 0.01.
Values may be sent and summed in bfloat16 or wider, within the bound.
No kernel may reach another device: no remote copies, remote signals or barrier semaphores. Data moves between devices by JAX's collectives and lax.ppermute only.
A program may use at most 256 MiB of HBM per device.

v0:
```python
import functools

import jax
import jax.numpy as jnp
from jax import lax
from jax.experimental import pallas as pl
from jax.experimental.pallas import tpu as pltpu
from jax.sharding import PartitionSpec as P

D = 8192
H = 128
G = 8
EPS = 1e-05
LANES = 128
MIB = 1 << 20

F32 = jnp.float32
BF16 = jnp.bfloat16

VM = pl.BlockSpec(memory_space=pltpu.VMEM)
SM = pl.BlockSpec(memory_space=pltpu.SMEM)
ANY = pl.BlockSpec(memory_space=pl.ANY)


def dot(a, b):
    return jnp.dot(a, b, preferred_element_type=F32)


def dot_t(a, b):
    return lax.dot_general(a, b, (((1,), (1,)), ((), ())), preferred_element_type=F32)


def iota(shape, dim):
    return lax.broadcasted_iota(jnp.int32, shape, dim)


def one_hot(condition):
    return jnp.where(condition, 1.0, 0.0).astype(BF16)


def split_two(value):
    high = value.astype(BF16)
    low = (value - high.astype(F32)).astype(BF16)
    return high, low


def call(kernel, outs, in_specs, args, vmem, name, scratch=(), out_specs=None, cost=None):
    single = not isinstance(outs, (list, tuple))
    if out_specs is None:
        out_specs = VM if single else [VM] * len(outs)
    return pl.pallas_call(
        kernel,
        out_shape=outs,
        in_specs=in_specs,
        out_specs=out_specs,
        scratch_shapes=list(scratch),
        name=name,
        cost_estimate=cost,
        compiler_params=pltpu.CompilerParams(vmem_limit_bytes=vmem),
    )(*args)


def shape_of(shape, dtype):
    return jax.ShapeDtypeStruct(shape, dtype)


def in_proj_kernel(heads, tok_ref, gain_ref, xz_ref, bc_ref, dt_ref, out_ref, xz_buf, bc_buf, lhs, dt_buf, sem, sem_bc):
    rows, depth = tok_ref.shape
    tiles = xz_buf.shape[0]
    tiles_bc = bc_buf.shape[0]
    inner = tiles * LANES
    groups_width = tiles_bc * LANES
    copies = [pltpu.make_async_copy(xz_ref.at[:, t], xz_buf.at[t], sem.at[t]) for t in range(tiles)]
    copies_bc = [pltpu.make_async_copy(bc_ref.at[:, t], bc_buf.at[t], sem_bc.at[t]) for t in range(tiles_bc)]
    for one in copies:
        one.start()
    for one in copies_bc:
        one.start()
    inputs = tok_ref[...].astype(F32)
    squares = jnp.sum(inputs * inputs, axis=1, keepdims=True)
    scaled = (inputs * gain_ref[0:1, :]).astype(BF16)
    row = iota((LANES, 2 * LANES), 0)
    col = iota((LANES, 2 * LANES), 1)
    even = one_hot(col == 2 * row)
    odd = one_hot(col == 2 * row + 1)
    for i in range(depth // LANES):
        block = scaled[:, i * LANES : (i + 1) * LANES]
        where = slice(i * 2 * LANES, (i + 1) * 2 * LANES)
        lhs[0:rows, where] = dot(block, even).astype(BF16)
        lhs[rows : 2 * rows, where] = dot(block, odd).astype(BF16)
    dt_buf[...] = jnp.zeros_like(dt_buf)
    dt_buf[0:heads, :] = dt_ref[...]
    tail = dot_t(scaled, dt_buf[...])
    high, low = split_two(squares)
    lane = iota(tail.shape, 1)
    tail = jnp.where(lane == heads, high.astype(F32), jnp.where(lane == heads + 1, low.astype(F32), tail))
    base = 2 * inner + 2 * groups_width
    out_ref[:, base : base + LANES] = tail.astype(BF16)

    def project(copies, view, start, width):
        count = len(copies)
        step = 2 if count % 2 == 0 else 1
        for t in range(0, count, step):
            for u in range(t, t + step):
                copies[u].wait()
            if step == 2:
                weights = jnp.concatenate([view[t], view[t + 1]], axis=1)
            else:
                weights = view[t]
            product = dot(lhs[...], weights).astype(BF16)
            at = start + t * LANES
            out_ref[:, at : at + step * LANES] = product[0:rows]
            out_ref[:, at + width : at + width + step * LANES] = product[rows : 2 * rows]

    project(copies, xz_buf.reshape(tiles, 2 * depth, LANES), 0, inner)
    project(copies_bc, bc_buf.reshape(tiles_bc, 2 * depth, LANES), 2 * inner, groups_width)


def in_proj(tokens, gains, weight_xz, weight_bc, weight_dt):
    rows, depth = tokens.shape
    inner = weight_xz.shape[2]
    groups_width = weight_bc.shape[2]
    heads = weight_dt.shape[1]
    tiles, tiles_bc = inner // LANES, groups_width // LANES
    xz = weight_xz.reshape(depth, 2, tiles, LANES).transpose(0, 2, 1, 3)
    bc = weight_bc.reshape(depth, 2, tiles_bc, LANES).transpose(0, 2, 1, 3)
    width = 2 * inner + 2 * groups_width + LANES
    return call(
        functools.partial(in_proj_kernel, heads),
        shape_of((rows, width), BF16),
        [VM, VM, ANY, ANY, VM],
        (tokens, gains, xz, bc, weight_dt.T),
        32 * MIB,
        "in_proj",
        scratch=[
            pltpu.VMEM((tiles, depth, 2, LANES), BF16),
            pltpu.VMEM((tiles_bc, depth, 2, LANES), BF16),
            pltpu.VMEM((2 * rows, 2 * depth), BF16),
            pltpu.VMEM((LANES, depth), BF16),
            pltpu.SemaphoreType.DMA((tiles,)),
            pltpu.SemaphoreType.DMA((tiles_bc,)),
        ],
    )


def pick_rows_kernel(slots, ids_ref, own_ref, other_ref, code_ref, *out_refs):
    total = (own_ref[...].astype(F32) + other_ref[...].astype(F32)).astype(BF16)
    rows = total.shape[0]
    slot = iota((slots, rows), 0)
    for i, out_ref in enumerate(out_refs):
        pick = one_hot(code_ref[...] == ids_ref[i] * slots + slot)
        out_ref[...] = dot(pick, total).astype(BF16)


def pick_rows(targets, own, other, code_row, slots):
    width = own.shape[1]
    count = targets.shape[0]
    return call(
        functools.partial(pick_rows_kernel, slots),
        [shape_of((slots, width), BF16)] * count,
        [SM, VM, VM, VM],
        (targets, own, other, code_row),
        8 * MIB,
        "pick_rows",
    )


def chip_sum_kernel(own_ref, other_ref, out_ref):
    out_ref[...] = (own_ref[...].astype(F32) + other_ref[...].astype(F32)).astype(BF16)


def chip_sum(own, other):
    return call(chip_sum_kernel, shape_of(own.shape, BF16), [VM, VM], (own, other), 4 * MIB, "chip_sum")


def mixer_kernel(
    parts,
    heads,
    ids_ref,
    code_ref,
    local_ref,
    *refs,
):
    part_refs = refs[:parts]
    (
        conv_ref,
        conv_bc_ref,
        bias_ref,
        rates_ref,
        skip_ref,
        gain_ref,
        queue_ref,
        queue_bc_ref,
        state_ref,
        act_ref,
        message_ref,
    ) = refs[parts:]
    slots = part_refs[0].shape[0]
    inner = gain_ref.shape[1]
    lags, local_rows, _ = queue_ref.shape
    groups_width = queue_bc_ref.shape[3]
    state_size = state_ref.shape[3]
    head_size = state_ref.shape[2]
    groups_here = groups_width // state_size
    per_group = inner // groups_here
    proj = part_refs[0][...].astype(F32)
    for ref in part_refs[1:]:
        proj = proj + ref[...].astype(F32)
    base_bc = 2 * inner
    base = base_bc + 2 * groups_width
    tail = proj[:, base : base + LANES]
    lane = iota(tail.shape, 1)
    squares = jnp.sum(jnp.where((lane == heads) | (lane == heads + 1), tail, 0.0), axis=1, keepdims=True)
    scale = lax.rsqrt(squares / D + EPS)
    slot = iota((slots, code_ref.shape[1]), 0)
    mine = code_ref[...] == ids_ref[0] * slots + slot
    valid = jnp.sum(jnp.where(mine, 1.0, 0.0), axis=1, keepdims=True)
    parent = jnp.sum(jnp.where(mine, local_ref[...], 0), axis=1, keepdims=True)
    pick = jnp.where((iota((slots, local_rows), 1) == parent) & (valid > 0.0), 1.0, 0.0).astype(BF16)

    now = proj[:, 0:inner] * scale
    gate = proj[:, inner : 2 * inner] * scale
    conv = now * conv_ref[lags : lags + 1, :]
    for k in range(lags):
        held = dot(pick, queue_ref[k])
        conv = conv + held * conv_ref[k : k + 1, :]
        if k > 0:
            message_ref[:, (k - 1) * inner : k * inner] = held.astype(BF16)
    message_ref[:, (lags - 1) * inner : lags * inner] = now.astype(BF16)
    inner_vals = conv * jax.nn.sigmoid(conv)
    at = lags * inner
    keys = []
    for j in range(2):
        start = base_bc + j * groups_width
        now_bc = proj[:, start : start + groups_width] * scale
        conv_bc = now_bc * conv_bc_ref[lags, j : j + 1, :]
        for k in range(lags):
            held = dot(pick, queue_bc_ref[k, j])
            conv_bc = conv_bc + held * conv_bc_ref[k, j : j + 1, :]
            if k > 0:
                to = at + ((k - 1) * 2 + j) * groups_width
                message_ref[:, to : to + groups_width] = held.astype(BF16)
        to = at + ((lags - 1) * 2 + j) * groups_width
        message_ref[:, to : to + groups_width] = now_bc.astype(BF16)
        keys.append(conv_bc * jax.nn.sigmoid(conv_bc))
    at = at + lags * 2 * groups_width

    raw = tail * scale + bias_ref[...]
    steps = jnp.maximum(raw, 0.0) + jnp.log1p(jnp.exp(-jnp.abs(raw)))
    decays = jnp.exp(-steps * rates_ref[...])
    spread = one_hot(iota((LANES, inner), 0) == iota((LANES, inner), 1) // head_size)

    def expand(value):
        high, low = split_two(value)
        return dot(high, spread) + dot(low, spread)

    steps_wide = expand(steps)
    decays_wide = expand(decays)
    skip_wide = expand(jnp.broadcast_to(skip_ref[...], (8, LANES)))[0:1]
    update = steps_wide * inner_vals
    message_ref[:, at : at + inner] = update.astype(BF16)
    at = at + inner
    message_ref[:, at : at + groups_width] = keys[0].astype(BF16)
    at = at + groups_width
    decay_high, decay_low = split_two(decays)
    message_ref[:, at : at + LANES] = decay_high
    message_ref[:, at + LANES : at + 2 * LANES] = decay_low

    for g in range(groups_here):
        lanes = slice(g * state_size, (g + 1) * state_size)
        wide = slice(g * per_group, (g + 1) * per_group)
        b_vals, c_vals = keys[0][:, lanes], keys[1][:, lanes]
        high, low = split_two(c_vals)
        c_both = jnp.concatenate([high, low], axis=0)
        mixed = jnp.zeros((slots, per_group), F32)
        first_head = g * (per_group // head_size)
        for r in range(local_rows):
            block = state_ref[r, first_head : first_head + per_group // head_size]
            both = dot_t(c_both, block.reshape(per_group, state_size))
            mixed = mixed + jnp.where(parent == r, both[0:slots] + both[slots : 2 * slots], 0.0)
        inside = jnp.sum(b_vals * c_vals, axis=1, keepdims=True)
        mixed = decays_wide[:, wide] * mixed + update[:, wide] * inside + skip_wide[:, wide] * inner_vals[:, wide]
        gated = mixed * (gate[:, wide] * jax.nn.sigmoid(gate[:, wide]))
        mean = jnp.sum(gated * gated, axis=1, keepdims=True) / per_group
        out = gated * lax.rsqrt(mean + EPS) * gain_ref[:, wide]
        act_ref[:, wide] = jnp.where(valid > 0.0, out, 0.0).astype(BF16)


def mixer(ids, code_row, local_row, parts, params, queue, queue_bc, state):
    conv, conv_bc, bias, rates, skip, gain = params
    slots = parts[0].shape[0]
    inner = gain.shape[0]
    lags = queue.shape[0]
    groups_width = queue_bc.shape[3]
    heads = bias.shape[0]
    message = lags * (inner + 2 * groups_width) + inner + groups_width + 2 * LANES

    def lane_row(vector):
        return jnp.pad(vector, (0, LANES - heads)).reshape(1, LANES)

    return call(
        functools.partial(mixer_kernel, len(parts), heads),
        [shape_of((slots, inner), BF16), shape_of((slots, message), BF16)],
        [SM, VM, VM] + [VM] * len(parts) + [VM] * 9,
        (ids, code_row, local_row, *parts, conv, conv_bc, lane_row(bias), lane_row(rates), lane_row(skip), gain.reshape(1, inner), queue, queue_bc, state),
        12 * MIB,
        "mixer",
    )


def deal_kernel(capacity, ids_ref, message_ref, *out_refs):
    slots = message_ref.shape[0]
    count = len(out_refs)
    row = iota((slots, slots), 0)
    want = row
    for i in range(count):
        want = jnp.where(row // capacity == i, ids_ref[i] * capacity + row % capacity, want)
    order = one_hot(iota((slots, slots), 1) == want)
    dealt = dot(order, message_ref[...])
    for i, out_ref in enumerate(out_refs):
        out_ref[...] = dealt[i * capacity : (i + 1) * capacity].astype(BF16)


def deal(targets, message, capacity):
    count = targets.shape[0]
    return call(
        functools.partial(deal_kernel, capacity),
        [shape_of((capacity, message.shape[1]), BF16)] * count,
        [SM, VM],
        (targets, message),
        8 * MIB,
        "deal",
    )


def collect_kernel(capacity, slots, lags, groups_width, ids_ref, code_ref, *refs):
    in_refs, (inner_ref, groups_ref, update_ref, keys_ref, decay_ref) = refs[:-5], refs[-5:]
    rows = code_ref.shape[0]
    count = len(in_refs)
    inner = update_ref.shape[1]
    me = ids_ref[0]
    held = jnp.concatenate([ref[...].astype(F32) for ref in in_refs], axis=0).astype(BF16)
    col = iota((rows, count * capacity), 1)
    want = jnp.full(col.shape, -1, jnp.int32)
    for i in range(count):
        want = jnp.where(col // capacity == i, ids_ref[i] * slots + me * capacity + col % capacity, want)
    mine = dot(one_hot(code_ref[...] == want), held)
    for k in range(lags):
        inner_ref[k] = mine[:, k * inner : (k + 1) * inner].astype(BF16)
    at = lags * inner
    for k in range(lags):
        for j in range(2):
            start = at + (2 * k + j) * groups_width
            groups_ref[k, j] = mine[:, start : start + groups_width].astype(BF16)
    at = at + 2 * lags * groups_width
    update_ref[...] = mine[:, at : at + inner]
    at = at + inner
    keys_ref[...] = mine[:, at : at + groups_width]
    at = at + groups_width
    decay_ref[...] = mine[:, at : at + LANES] + mine[:, at + LANES : at + 2 * LANES]


def collect(sources, own_code, messages, slots, inner, groups_width, lags):
    capacity = messages[0].shape[0]
    rows = own_code.shape[0]
    return call(
        functools.partial(collect_kernel, capacity, slots, lags, groups_width),
        [
            shape_of((lags, rows, inner), BF16),
            shape_of((lags, 2, rows, groups_width), BF16),
            shape_of((rows, inner), F32),
            shape_of((rows, groups_width), F32),
            shape_of((rows, LANES), F32),
        ],
        [SM, VM] + [VM] * len(messages),
        (sources, own_code, *messages),
        8 * MIB,
        "collect",
    )


def update_kernel(sources, own_parents_ref, ids_ref, *refs):
    state_refs = refs[:sources]
    update_ref, keys_ref, decay_ref, out_ref, held, made, sem_in, sem_out = refs[sources:]
    rows, heads, head_size, state_size = held.shape
    local_rows = rows
    inner = update_ref.shape[1]
    groups_here = keys_ref.shape[1] // state_size
    per_group = inner // groups_here
    heads_group = heads // groups_here

    def fetch(j):
        parent = own_parents_ref[j]
        owner = parent // local_rows
        row = lax.rem(parent, local_rows)
        for i in range(sources):

            @pl.when(owner == ids_ref[i])
            def _(i=i):
                pltpu.make_async_copy(state_refs[i].at[row], held.at[j], sem_in.at[j]).start()

    for j in range(rows):
        fetch(j)
    spread = one_hot(iota((LANES, inner), 0) == iota((LANES, inner), 1) // head_size)
    high, low = split_two(decay_ref[...])
    decay_high, decay_low = dot(high, spread), dot(low, spread)
    columns = []
    for g in range(groups_here):
        wide = slice(g * per_group, (g + 1) * per_group)
        stacked = jnp.concatenate([update_ref[:, wide], decay_high[:, wide], decay_low[:, wide]], axis=0)
        columns.append(jnp.transpose(stacked).astype(BF16))
    row_id = iota((3 * rows, state_size), 0)
    for j in range(rows):
        pltpu.make_async_copy(state_refs[0].at[0], held.at[j], sem_in.at[j]).wait()
        for g in range(groups_here):
            keys = keys_ref[j : j + 1, g * state_size : (g + 1) * state_size]
            right_keys = jnp.where(row_id == j, keys, 0.0)
            right_ones = jnp.where((row_id == rows + j) | (row_id == 2 * rows + j), 1.0, 0.0)
            right = jnp.concatenate([right_keys, right_ones], axis=1).astype(BF16)
            both = dot(columns[g], right)
            which = slice(g * heads_group, (g + 1) * heads_group)
            before = held[j, which].reshape(per_group, state_size).astype(F32)
            after = both[:, state_size:] * before + both[:, :state_size]
            made[j, which] = after.astype(BF16).reshape(heads_group, head_size, state_size)
        pltpu.make_async_copy(made.at[j], out_ref.at[j], sem_out.at[j]).start()
    for j in range(rows):
        pltpu.make_async_copy(made.at[j], out_ref.at[j], sem_out.at[j]).wait()


def update_state(own_parents, ids, states, update, keys, decay):
    shape = states[0].shape
    return call(
        functools.partial(update_kernel, len(states)),
        shape_of(shape, BF16),
        [SM, SM] + [ANY] * len(states) + [VM] * 3,
        (own_parents, ids, *states, update, keys, decay),
        24 * MIB,
        "update_state",
        scratch=[
            pltpu.VMEM(shape, BF16),
            pltpu.VMEM(shape, BF16),
            pltpu.SemaphoreType.DMA((shape[0],)),
            pltpu.SemaphoreType.DMA((shape[0],)),
        ],
        out_specs=ANY,
    )


def out_proj_kernel(slots, ids_ref, code_ref, *refs):
    act_refs, (weight_ref, out_ref) = refs[:-2], refs[-2:]
    rows = code_ref.shape[0]
    count = len(act_refs)
    col = iota((rows, count * slots), 1)
    want = jnp.full(col.shape, -1, jnp.int32)
    for i in range(count):
        want = jnp.where(col // slots == i, ids_ref[i] * slots + col % slots, want)
    held = jnp.concatenate([ref[...] for ref in act_refs], axis=0)
    activity = dot(one_hot(code_ref[...] == want), held).astype(BF16)
    out_ref[...] = dot(activity, weight_ref[...]).astype(BF16)


def out_proj(sources, code_col, acts, weight):
    rows = code_col.shape[0]
    return call(
        functools.partial(out_proj_kernel, acts[0].shape[0]),
        shape_of((rows, weight.shape[1]), BF16),
        [SM, VM] + [VM] * (len(acts) + 1),
        (sources, code_col, *acts, weight),
        12 * MIB,
        "out_proj",
    )


def up_kernel(parts, tok_ref, gain_ref, *refs):
    part_refs = refs[:parts]
    weight_ref, residual_ref, out_ref = refs[parts:]
    residual = tok_ref[...].astype(F32)
    total = part_refs[0][...].astype(F32)
    for ref in part_refs[1:]:
        total = total + ref[...].astype(F32)
    residual = residual + total
    residual_ref[...] = residual
    squares = jnp.sum(residual * residual, axis=1, keepdims=True)
    scaled = (residual * gain_ref[1:2, :]).astype(BF16)
    width = weight_ref.shape[1]
    high, low = split_two(squares)
    lane = iota((scaled.shape[0], LANES), 1)
    out_ref[:, width : width + LANES] = jnp.where(
        lane == 0, high.astype(F32), jnp.where(lane == 1, low.astype(F32), 0.0)
    ).astype(BF16)
    out_ref[:, 0:width] = dot(scaled, weight_ref[...]).astype(BF16)


def up_proj(tokens, gains, parts, weight):
    rows, width = tokens.shape
    return call(
        functools.partial(up_kernel, len(parts)),
        [shape_of((rows, width), F32), shape_of((rows, weight.shape[1] + LANES), BF16)],
        [VM] * (len(parts) + 3),
        (tokens, gains, *parts, weight),
        20 * MIB,
        "up_proj",
    )


def down_kernel(*refs):
    part_refs, (weight_ref, out_ref) = refs[:-2], refs[-2:]
    total = part_refs[0][...].astype(F32)
    for ref in part_refs[1:]:
        total = total + ref[...].astype(F32)
    width = weight_ref.shape[0]
    squares = jnp.sum(total[:, width : width + LANES], axis=1, keepdims=True)
    hidden = jnp.maximum(total[:, 0:width] * lax.rsqrt(squares / D + EPS), 0.0)
    out_ref[...] = dot((hidden * hidden).astype(BF16), weight_ref[...]).astype(BF16)


def down_proj(parts, weight):
    rows = parts[0].shape[0]
    return call(
        down_kernel,
        shape_of((rows, weight.shape[1]), BF16),
        [VM] * (len(parts) + 1),
        (*parts, weight),
        20 * MIB,
        "down_proj",
    )


def finish_kernel(residual_ref, *refs):
    part_refs, out_ref = refs[:-1], refs[-1]
    total = part_refs[0][...].astype(F32)
    for ref in part_refs[1:]:
        total = total + ref[...].astype(F32)
    out_ref[0] = (residual_ref[...] + total).astype(BF16)


def finish(residual, parts):
    return call(
        finish_kernel,
        shape_of((1, *residual.shape), BF16),
        [VM] * (len(parts) + 1),
        (residual, *parts),
        6 * MIB,
        "finish",
    )


def on_device(
    tokens,
    parents,
    norm_gains,
    weight_xz,
    weight_bc,
    weight_dt,
    conv_inner,
    conv_groups,
    dt_bias,
    rates,
    skip_gain,
    gate_gain,
    weight_out,
    weight_up,
    weight_down,
    ssm_state,
    queue_inner,
    queue_groups,
):
    devices = lax.axis_size("dp")
    chips = devices // 2
    ranks = lax.axis_size("tensor")
    me = lax.axis_index("dp")
    chip, core = me // 2, me % 2
    local_rows = ssm_state.shape[0]
    lags = queue_inner.shape[1]
    inner = queue_inner.shape[2]
    groups_width = queue_groups.shape[3]
    capacity = max(2, 2 * local_rows // devices)
    slots = devices * capacity
    rows = parents.shape[1]
    barrier = lax.optimization_barrier

    def to_dp(value, hop, flip):
        pairs = [(i, ((i // 2 + hop) % chips) * 2 + ((i % 2) ^ flip)) for i in range(devices)]
        return lax.ppermute(value, "dp", pairs)

    def over_tensor(value):
        return [value] + [
            lax.ppermute(value, "tensor", [(i, (i + s) % ranks) for i in range(ranks)]) for s in range(1, ranks)
        ]

    hops = [(hop, flip) for hop in range(chips) for flip in range(2)]
    sources = jnp.stack([((chip + chips - hop) % chips) * 2 + (core ^ flip) for hop, flip in hops]).astype(jnp.int32)
    targets = jnp.stack([((chip + hop) % chips) * 2 + (core ^ flip) for hop, flip in hops]).astype(jnp.int32)

    chosen = parents[0]
    owner = chosen // local_rows
    place = jnp.arange(rows, dtype=jnp.int32)
    block = place // local_rows
    earlier = (owner[:, None] == owner[None, :]) & (block[:, None] == block[None, :]) & (place[None, :] < place[:, None])
    rank = jnp.sum(earlier, axis=1).astype(jnp.int32)
    code = owner * slots + block * capacity + rank
    code_row, code_col = code.reshape(1, rows), code.reshape(rows, 1)
    local_row = (chosen % local_rows).reshape(1, rows)
    own_code = lax.dynamic_slice_in_dim(code_col, me * local_rows, local_rows, 0)
    own_parents = lax.dynamic_slice_in_dim(chosen, me * local_rows, local_rows, 0)

    sibling_state = to_dp(ssm_state, 0, 1)
    far = {}
    for hop in range(1, chips):
        far[hop, 0] = to_dp(ssm_state, hop, 0)
        far[hop, 1] = to_dp(far[hop, 0], 0, 1)

    partial = in_proj(tokens[0], norm_gains, weight_xz, weight_bc, weight_dt)
    near = to_dp(partial, 0, 1)
    same_core = targets[0::2]
    picked = pick_rows(same_core, partial, near, code_row, slots)
    parts = [picked[0]] + [to_dp(picked[hop], hop, 0) for hop in range(1, chips)]
    act, message = mixer(
        sources,
        code_row,
        local_row,
        parts,
        (conv_inner, conv_groups, dt_bias, rates, skip_gain, gate_gain),
        queue_inner.transpose(1, 0, 2),
        queue_groups.transpose(1, 2, 0, 3),
        ssm_state,
    )
    acts = [act] + [to_dp(act, hop, flip) for hop, flip in hops[1:]]
    out_part = out_proj(sources, code_col, acts, weight_out)
    residual, up_part = up_proj(tokens[0], norm_gains, over_tensor(out_part), weight_up)
    up_chip = chip_sum(up_part, to_dp(up_part, 0, 1))
    down_part = down_proj([up_chip] + [to_dp(up_chip, hop, 0) for hop in range(1, chips)], weight_down)
    beam_out = finish(residual, over_tensor(down_part))

    dealt = deal(targets, message, capacity)
    messages = [dealt[0]] + [to_dp(dealt[i], *hops[i]) for i in range(1, devices)]
    final_inner, final_groups, update, keys, decay = collect(
        sources, own_code, messages, slots, inner, groups_width, lags
    )
    states = [ssm_state, sibling_state] + [far[hop, flip] for hop, flip in hops[2:]]
    final_state = update_state(own_parents, sources, states, update, keys, decay)
    return (beam_out, final_state, final_inner.transpose(1, 0, 2), final_groups.transpose(2, 0, 1, 3))


def solution(mesh):
    in_specs = (
        P(None, "groups", "dp"),
        P(None, "groups"),
        P(None, "dp"),
        P("dp", None, "tensor"),
        P("dp", None, "tensor"),
        P("dp", "tensor"),
        P(None, "tensor"),
        P(None, None, "tensor"),
        P("tensor"),
        P("tensor"),
        P("tensor"),
        P("tensor"),
        P("tensor", "dp"),
        P("dp", "tensor"),
        P("tensor", "dp"),
        P(("groups", "dp"), "tensor", None, None),
        P(("groups", "dp"), None, "tensor"),
        P(("groups", "dp"), None, None, "tensor"),
    )
    out_specs = (
        P(None, "groups", "dp"),
        P(("groups", "dp"), "tensor", None, None),
        P(("groups", "dp"), None, "tensor"),
        P(("groups", "dp"), None, None, "tensor"),
    )
    return jax.shard_map(
        on_device, mesh=mesh, in_specs=in_specs, out_specs=out_specs, check_vma=False
    )
```

profile of v0, /device:TPU:1, one launch (start us, length us, event | category | flops | bytes accessed | tf_op | source)
XLA Modules:
  0.0 218.5 jit_solution(12579268711604729463)
XLA Ops:
  0.6 2.1 collective-permute-start.14
  3.7 89.7 %collective-permute-done.14.refs_2_ = bf16[8,32,64,128]{3,2,1,0:T(8,128)(2,1)} collective-permute-done((bf16[8,32,64,128]{3,2,1,0:T(8,128)(2,1)}, bf16[8,32,64,128]{3,2,1,0:T(8,128)(2,1)}, u32[]{:S(2)}, u32[]{:S(2)}) %collective-permute-start.14) | collective-permute-done | bytes 4194336 | tf_op jit(solution)/shard_map/ppermute | solution.py:584
  93.4 1.2 collective-permute-start.15
  94.6 5.8 %copy-done = bf16[2048,2,2048]{2,1,0:T(2,128)(2,1)S(1)} copy-done((bf16[2048,2,2048]{2,1,0:T(2,128)(2,1)S(1)}, bf16[2048,2,2048]{2,1,0:T(2,128)(2,1)}, u32[]{:S(2)}) %copy-start) | copy-done | bytes 16777240
  100.4 1.6 copy-done.6
  104.5 23.6 %in_proj.1.own_ref = bf16[32,4736]{1,0:T(8,128)(2,1)S(1)} custom-call(bf16[32,2048]{1,0:T(8,128)(2,1)S(1)} %bitcast.46, f32[2,2048]{1,0:T(2,128)S(1)} %copy-done.11, bf16[2048,16,2,128]{3,2,1,0:T(2,128)(2,1)S(1)} %bitcast.44, bf16[2048,2,2,128]{3,2,1,0:T(2,128)(2,1)S(1)} %bitcast.45, bf16[32,2048]{1,0:T(8,128)(2,1)S(1)} %bitcast.48), custom_call_target="tpu_custom_call" | custom-call | tf_op jit(solution)/shard_map/in_proj/pallas_call | solution.py:51
  130.6 1.5 collective-permute-start.1
  132.4 3.7 %collective-permute-done.1.refs_1_ = bf16[16,4736]{1,0:T(8,128)(2,1)S(1)} collective-permute-done((bf16[16,4736]{1,0:T(8,128)(2,1)S(1)}, bf16[16,4736]{1,0:T(8,128)(2,1)S(1)}, u32[]{:S(2)}, u32[]{:S(2)}) %collective-permute-start.1) | collective-permute-done | bytes 151584 | tf_op jit(solution)/shard_map/ppermute | solution.py:584
  136.1 2.2 copy-done.3
  138.3 2.7 %mixer.1 = (bf16[16,2048]{1,0:T(8,128)(2,1)S(1)}, bf16[16,10240]{1,0:T(8,128)(2,1)S(1)}) custom-call(s32[4]{0:T(128)S(1)} %add_add_fusion.ids_ref, s32[1,32]{1,0:T(1,128)S(1)} %fusion.12.code_ref, s32[1,32]{1,0:T(1,128)S(1)} %get-tuple-element.46.local_ref, bf16[16,4736]{1,0:T(8,128)(2,1)S(1)} %get-tuple-element.19.refs_0_, ...), custom_call_target="tpu_custom_call" | custom-call | tf_op jit(solution)/shard_map/mixer/pallas_call | solution.py:51
  142.0 1.5 collective-permute-start.3
  143.7 1.9 collective-permute-done.3.refs_2_
  145.7 1.8 collective-permute-done.4.refs_3_
  147.5 3.4 %copy-done.5 = bf16[2048,2048]{1,0:T(8,128)(2,1)S(1)} copy-done((bf16[2048,2048]{1,0:T(8,128)(2,1)S(1)}, bf16[2048,2048]{1,0:T(8,128)(2,1)}, u32[]{:S(2)}) %copy-start.5) | copy-done | bytes 8388632
  150.9 2.3 %out_proj.1.refs_0_ = bf16[32,2048]{1,0:T(8,128)(2,1)S(1)} custom-call(s32[4]{0:T(128)S(1)} %add_add_fusion.ids_ref, s32[32,1]{1,0:T(8,128)S(1)} %fusion.3.code_ref, bf16[16,2048]{1,0:T(8,128)(2,1)S(1)} %get-tuple-element.21.refs_0_, bf16[16,2048]{1,0:T(8,128)(2,1)S(1)} %collective-permute-done.2.refs_1_, ...), custom_call_target="tpu_custom_call" | custom-call | tf_op jit(solution)/shard_map/out_proj/pallas_call | solution.py:51
  153.1 1.3 collective-permute-start.5
  154.5 2.3 %collective-permute-start.6 = (bf16[32,2048]{1,0:T(8,128)(2,1)S(1)}, bf16[32,2048]{1,0:T(8,128)(2,1)S(1)}, u32[]{:S(2)}, u32[]{:S(2)}) collective-permute-start(bf16[32,2048]{1,0:T(8,128)(2,1)S(1)} %out_proj.1.refs_0_), channel_id=1, source_target_pairs={{0,2},{1,3},{2,0},{3,1},{4,6},{5,7},{6,4},{7,5},{8,10},{9,11},{10,... | collective-permute-start | bytes 393224 | tf_op jit(solution)/shard_map/ppermute | solution.py:588
  157.8 2.0 collective-permute-done.5.refs_1_
  159.9 6.2 %collective-permute-done.6.refs_2_ = bf16[32,2048]{1,0:T(8,128)(2,1)S(1)} collective-permute-done((bf16[32,2048]{1,0:T(8,128)(2,1)S(1)}, bf16[32,2048]{1,0:T(8,128)(2,1)S(1)}, u32[]{:S(2)}, u32[]{:S(2)}) %collective-permute-start.6) | collective-permute-done | bytes 131104 | tf_op jit(solution)/shard_map/ppermute | solution.py:588
  166.1 5.8 %copy-done.1 = bf16[2048,4096]{1,0:T(8,128)(2,1)S(1)} copy-done((bf16[2048,4096]{1,0:T(8,128)(2,1)S(1)}, bf16[2048,4096]{1,0:T(8,128)(2,1)}, u32[]{:S(2)}) %copy-start.1) | copy-done | bytes 16777240
  171.9 3.0 %up_proj.1 = (f32[32,2048]{1,0:T(8,128)S(1)}, bf16[32,4224]{1,0:T(8,128)(2,1)S(1)}) custom-call(bf16[32,2048]{1,0:T(8,128)(2,1)S(1)} %bitcast.47, f32[2,2048]{1,0:T(2,128)S(1)} %copy-done.12, bf16[32,2048]{1,0:T(8,128)(2,1)S(1)} %out_proj.1.refs_0_, bf16[32,2048]{1,0:T(8,128)(2,1)S(1)} %collective-permute-done.5.refs_1_, ...), custom_call_target="tpu_custom_call" | custom-call | tf_op jit(solution)/shard_map/up_proj/pallas_call | solution.py:51
  176.7 1.2 collective-permute-start.9
  179.7 4.7 %collective-permute-done.9.refs_1_ = bf16[32,4224]{1,0:T(8,128)(2,1)S(1)} collective-permute-done((bf16[32,4224]{1,0:T(8,128)(2,1)S(1)}, bf16[32,4224]{1,0:T(8,128)(2,1)S(1)}, u32[]{:S(2)}, u32[]{:S(2)}) %collective-permute-start.9) | collective-permute-done | bytes 270368 | tf_op jit(solution)/shard_map/ppermute | solution.py:584
  184.5 3.1 %collective-permute-start.18 = (bf16[4,10240]{1,0:T(4,128)(2,1)S(1)}, bf16[4,10240]{1,0:T(4,128)(2,1)S(1)}, u32[]{:S(2)}, u32[]{:S(2)}) collective-permute-start(bf16[4,10240]{1,0:T(4,128)(2,1)S(1)} %get-tuple-element.28), channel_id=1, source_target_pairs={{0,12},{4,8},{8,4},{12,0},{1,13},{5,9},{9,5},{13,1},{2,14},{6,10},... | collective-permute-start | bytes 245768 | tf_op jit(solution)/shard_map/ppermute | solution.py:584
  187.5 5.8 %copy-done.2 = bf16[4096,2048]{1,0:T(8,128)(2,1)S(1)} copy-done((bf16[4096,2048]{1,0:T(8,128)(2,1)S(1)}, bf16[4096,2048]{1,0:T(8,128)(2,1)}, u32[]{:S(2)}) %copy-start.2) | copy-done | bytes 16777240
  193.3 3.1 %down_proj.1.refs_0_ = bf16[32,2048]{1,0:T(8,128)(2,1)S(1)} custom-call(bf16[32,4224]{1,0:T(8,128)(2,1)S(1)} %chip_sum.1.refs_0_, bf16[32,4224]{1,0:T(8,128)(2,1)S(1)} %collective-permute-done.9.refs_1_, bf16[4096,2048]{1,0:T(8,128)(2,1)S(1)} %copy-done.2), custom_call_target="tpu_custom_call" | custom-call | tf_op jit(solution)/shard_map/down_proj/pallas_call | solution.py:51
  196.4 3.0 %collective-permute-start.10 = (bf16[32,2048]{1,0:T(8,128)(2,1)S(1)}, bf16[32,2048]{1,0:T(8,128)(2,1)S(1)}, u32[]{:S(2)}, u32[]{:S(2)}) collective-permute-start(bf16[32,2048]{1,0:T(8,128)(2,1)S(1)} %down_proj.1.refs_0_), channel_id=1, source_target_pairs={{0,1},{1,2},{2,3},{3,0},{4,5},{5,6},{6,7},{7,4},{8,9},{9,10},{10,1... | collective-permute-start | bytes 393224 | tf_op jit(solution)/shard_map/ppermute | solution.py:588
  199.4 1.4 collective-permute-start.11
  201.8 1.4 collect.1
  204.3 5.0 %collective-permute-done.11.refs_2_ = bf16[32,2048]{1,0:T(8,128)(2,1)S(1)} collective-permute-done((bf16[32,2048]{1,0:T(8,128)(2,1)S(1)}, bf16[32,2048]{1,0:T(8,128)(2,1)S(1)}, u32[]{:S(2)}, u32[]{:S(2)}) %collective-permute-start.11) | collective-permute-done | bytes 131104 | tf_op jit(solution)/shard_map/ppermute | solution.py:588
  210.3 2.2 %copy-done.4 = bf16[8,32,64,128]{3,2,1,0:T(8,128)(2,1)S(1)} copy-done((bf16[8,32,64,128]{3,2,1,0:T(8,128)(2,1)S(1)}, bf16[8,32,64,128]{3,2,1,0:T(8,128)(2,1)}, u32[]{:S(2)}) %copy-start.4) | copy-done | bytes 4194328
  212.5 5.8 %update_state.1 = bf16[8,32,64,128]{3,2,1,0:T(8,128)(2,1)} custom-call(s32[8]{0:T(128)S(1)} %dynamic-slice_bitcast_fusion.1.own_parents_ref, s32[4]{0:T(128)S(1)} %add_add_fusion.ids_ref, bf16[8,32,64,128]{3,2,1,0:T(8,128)(2,1)S(1)} %copy-done.4, bf16[8,32,64,128]{3,2,1,0:T(8,128)(2,1)} %collective-permute-done.13.refs_1_, ...), custom_call_target="tpu_custom_call" | custom-call | tf_op jit(solution)/shard_map/update_state/pallas_call | solution.py:51
  (77 shorter events, 15.2 us)
Async XLA Ops:
  0.6 92.7 %collective-permute-start.14 = (bf16[8,32,64,128]{3,2,1,0:T(8,128)(2,1)}, bf16[8,32,64,128]{3,2,1,0:T(8,128)(2,1)}, u32[]{:S(2)}, u32[]{:S(2)}) collective-permute-start(bf16[8,32,64,128]{3,2,1,0:T(8,128)(2,1)} %refs_0_.1), channel_id=1, source_target_pairs={{0,8},{4,12},{8,0},{12,4},{1,9},{5,13},{9,1},{13,5},{2,10},{6,14},... | collective-permute-start | bytes 12582920 | tf_op jit(solution)/shard_map/ppermute | solution.py:584
  2.7 207.6 %collective-permute-start.13 = (bf16[8,32,64,128]{3,2,1,0:T(8,128)(2,1)}, bf16[8,32,64,128]{3,2,1,0:T(8,128)(2,1)}, u32[]{:S(2)}, u32[]{:S(2)}) collective-permute-start(bf16[8,32,64,128]{3,2,1,0:T(8,128)(2,1)} %refs_0_.1), channel_id=1, source_target_pairs={{0,4},{4,0},{8,12},{12,8},{1,5},{5,1},{9,13},{13,9},{2,6},{6,2},{1... | collective-permute-start | bytes 12582920 | tf_op jit(solution)/shard_map/ppermute | solution.py:584
  93.4 117.0 %collective-permute-start.15 = (bf16[8,32,64,128]{3,2,1,0:T(8,128)(2,1)}, bf16[8,32,64,128]{3,2,1,0:T(8,128)(2,1)}, u32[]{:S(2)}, u32[]{:S(2)}) collective-permute-start(bf16[8,32,64,128]{3,2,1,0:T(8,128)(2,1)} %collective-permute-done.14.refs_2_), channel_id=1, source_target_pairs={{0,4},{4,0},{8,12},{12,8},{1,5},{5,1},{9,13},{13,9},{2,6},{6,2},{1... | collective-permute-start | bytes 12582920 | tf_op jit(solution)/shard_map/ppermute | solution.py:584
  94.6 5.8 %copy-start = (bf16[2048,2,2048]{2,1,0:T(2,128)(2,1)S(1)}, bf16[2048,2,2048]{2,1,0:T(2,128)(2,1)}, u32[]{:S(2)}) copy-start(bf16[2048,2,2048]{2,1,0:T(2,128)(2,1)} %param.21) | copy-start | bytes 50331652
  104.5 24.0 %copy-start.17 = (s32[1,32]{1,0:T(1,128)S(1)}, s32[1,32]{1,0:T(1,128)}, u32[]{:S(2)}) copy-start(s32[1,32]{1,0:T(1,128)} %param.19) | copy-start | bytes 388
  104.5 24.2 %copy-start.20 = (f32[32]{0:T(128)S(1)}, f32[32]{0:T(128)}, u32[]{:S(2)}) copy-start(f32[32]{0:T(128)} %param.26) | copy-start | bytes 388
  104.5 27.7 %copy-start.16 = (bf16[8,3,2,256]{3,2,1,0:T(2,128)(2,1)S(1)}, bf16[8,3,2,256]{3,2,1,0:T(2,128)(2,1)}, u32[]{:S(2)}) copy-start(bf16[8,3,2,256]{3,2,1,0:T(2,128)(2,1)} %param.35) | copy-start | bytes 73732
  104.5 27.9 %copy-start.18 = (f32[32]{0:T(128)S(1)}, f32[32]{0:T(128)}, u32[]{:S(2)}) copy-start(f32[32]{0:T(128)} %param.28) | copy-start | bytes 388
  104.5 27.9 %copy-start.19 = (f32[32]{0:T(128)S(1)}, f32[32]{0:T(128)}, u32[]{:S(2)}) copy-start(f32[32]{0:T(128)} %param.27) | copy-start | bytes 388
  104.5 31.6 %copy-start.10 = (bf16[8,3,2048]{2,0,1:T(8,128)(2,1)S(1)}, bf16[8,3,2048]{2,0,1:T(8,128)(2,1)}, u32[]{:S(2)}) copy-start(bf16[8,3,2048]{2,0,1:T(8,128)(2,1)} %param.34) | copy-start | bytes 294916
  104.5 31.6 %copy-start.13 = (f32[4,2048]{1,0:T(4,128)S(1)}, f32[4,2048]{1,0:T(4,128)}, u32[]{:S(2)}) copy-start(f32[4,2048]{1,0:T(4,128)} %refs_2_.2) | copy-start | bytes 98308
  104.5 31.6 %copy-start.14 = (f32[4,2,256]{2,1,0:T(2,128)S(1)}, f32[4,2,256]{2,1,0:T(2,128)}, u32[]{:S(2)}) copy-start(f32[4,2,256]{2,1,0:T(2,128)} %refs_3_.1) | copy-start | bytes 24580
  104.5 31.6 %copy-start.15 = (f32[2048]{0:T(1024)S(1)}, f32[2048]{0:T(1024)}, u32[]{:S(2)}) copy-start(f32[2048]{0:T(1024)} %param.29) | copy-start | bytes 24580
  128.2 1.7 collective-permute-start
  130.6 5.5 %collective-permute-start.1 = (bf16[16,4736]{1,0:T(8,128)(2,1)S(1)}, bf16[16,4736]{1,0:T(8,128)(2,1)S(1)}, u32[]{:S(2)}, u32[]{:S(2)}) collective-permute-start(bf16[16,4736]{1,0:T(8,128)(2,1)S(1)} %get-tuple-element.20), channel_id=1, source_target_pairs={{0,8},{4,12},{8,0},{12,4},{1,9},{5,13},{9,1},{13,5},{2,10},{6,14},... | collective-permute-start | bytes 454664 | tf_op jit(solution)/shard_map/ppermute | solution.py:584
  141.0 2.8 %collective-permute-start.2 = (bf16[16,2048]{1,0:T(8,128)(2,1)S(1)}, bf16[16,2048]{1,0:T(8,128)(2,1)S(1)}, u32[]{:S(2)}, u32[]{:S(2)}) collective-permute-start(bf16[16,2048]{1,0:T(8,128)(2,1)S(1)} %get-tuple-element.21.refs_0_), channel_id=1, source_target_pairs={{0,4},{4,0},{8,12},{12,8},{1,5},{5,1},{9,13},{13,9},{2,6},{6,2},{1... | collective-permute-start | bytes 196616 | tf_op jit(solution)/shard_map/ppermute | solution.py:584
  142.0 3.7 %collective-permute-start.3 = (bf16[16,2048]{1,0:T(8,128)(2,1)S(1)}, bf16[16,2048]{1,0:T(8,128)(2,1)S(1)}, u32[]{:S(2)}, u32[]{:S(2)}) collective-permute-start(bf16[16,2048]{1,0:T(8,128)(2,1)S(1)} %get-tuple-element.21.refs_0_), channel_id=1, source_target_pairs={{0,8},{4,12},{8,0},{12,4},{1,9},{5,13},{9,1},{13,5},{2,10},{6,14},... | collective-permute-start | bytes 196616 | tf_op jit(solution)/shard_map/ppermute | solution.py:584
  143.5 4.0 %collective-permute-start.4 = (bf16[16,2048]{1,0:T(8,128)(2,1)S(1)}, bf16[16,2048]{1,0:T(8,128)(2,1)S(1)}, u32[]{:S(2)}, u32[]{:S(2)}) collective-permute-start(bf16[16,2048]{1,0:T(8,128)(2,1)S(1)} %get-tuple-element.21.refs_0_), channel_id=1, source_target_pairs={{0,12},{4,8},{8,4},{12,0},{1,13},{5,9},{9,5},{13,1},{2,14},{6,10},... | collective-permute-start | bytes 196616 | tf_op jit(solution)/shard_map/ppermute | solution.py:584
  143.7 22.4 %copy-start.12 = (f32[2,2048]{1,0:T(2,128)S(1)}, f32[2,2048]{1,0:T(2,128)}, u32[]{:S(2)}) copy-start(f32[2,2048]{1,0:T(2,128)} %gain_ref.3) | copy-start | bytes 49156
  150.9 15.2 %copy-start.8 = (bf16[1,32,2048]{2,1,0:T(8,128)(2,1)S(1)}, bf16[1,32,2048]{2,1,0:T(8,128)(2,1)}, u32[]{:S(2)}) copy-start(bf16[1,32,2048]{2,1,0:T(8,128)(2,1)} %param.18) | copy-start | bytes 393220
  153.1 6.7 %collective-permute-start.5 = (bf16[32,2048]{1,0:T(8,128)(2,1)S(1)}, bf16[32,2048]{1,0:T(8,128)(2,1)S(1)}, u32[]{:S(2)}, u32[]{:S(2)}) collective-permute-start(bf16[32,2048]{1,0:T(8,128)(2,1)S(1)} %out_proj.1.refs_0_), channel_id=1, source_target_pairs={{0,1},{1,2},{2,3},{3,0},{4,5},{5,6},{6,7},{7,4},{8,9},{9,10},{10,1... | collective-permute-start | bytes 393224 | tf_op jit(solution)/shard_map/ppermute | solution.py:588
  154.5 11.6 %collective-permute-start.6 = (bf16[32,2048]{1,0:T(8,128)(2,1)S(1)}, bf16[32,2048]{1,0:T(8,128)(2,1)S(1)}, u32[]{:S(2)}, u32[]{:S(2)}) collective-permute-start(bf16[32,2048]{1,0:T(8,128)(2,1)S(1)} %out_proj.1.refs_0_), channel_id=1, source_target_pairs={{0,2},{1,3},{2,0},{3,1},{4,6},{5,7},{6,4},{7,5},{8,10},{9,11},{10,... | collective-permute-start | bytes 393224 | tf_op jit(solution)/shard_map/ppermute | solution.py:588
  156.8 9.3 %collective-permute-start.7 = (bf16[32,2048]{1,0:T(8,128)(2,1)S(1)}, bf16[32,2048]{1,0:T(8,128)(2,1)S(1)}, u32[]{:S(2)}, u32[]{:S(2)}) collective-permute-start(bf16[32,2048]{1,0:T(8,128)(2,1)S(1)} %out_proj.1.refs_0_), channel_id=1, source_target_pairs={{0,3},{1,0},{2,1},{3,2},{4,7},{5,4},{6,5},{7,6},{8,11},{9,8},{10,9... | collective-permute-start | bytes 393224 | tf_op jit(solution)/shard_map/ppermute | solution.py:588
  166.1 5.8 %copy-start.1 = (bf16[2048,4096]{1,0:T(8,128)(2,1)S(1)}, bf16[2048,4096]{1,0:T(8,128)(2,1)}, u32[]{:S(2)}) copy-start(bf16[2048,4096]{1,0:T(8,128)(2,1)} %refs_4_.3) | copy-start | bytes 50331652
  174.8 1.8 collective-permute-start.8
  176.7 7.8 %collective-permute-start.9 = (bf16[32,4224]{1,0:T(8,128)(2,1)S(1)}, bf16[32,4224]{1,0:T(8,128)(2,1)S(1)}, u32[]{:S(2)}, u32[]{:S(2)}) collective-permute-start(bf16[32,4224]{1,0:T(8,128)(2,1)S(1)} %chip_sum.1.refs_0_), channel_id=1, source_target_pairs={{0,8},{4,12},{8,0},{12,4},{1,9},{5,13},{9,1},{13,5},{2,10},{6,14},... | collective-permute-start | bytes 811016 | tf_op jit(solution)/shard_map/ppermute | solution.py:584
  178.7 17.7 %collective-permute-start.16 = (bf16[4,10240]{1,0:T(4,128)(2,1)S(1)}, bf16[4,10240]{1,0:T(4,128)(2,1)S(1)}, u32[]{:S(2)}, u32[]{:S(2)}) collective-permute-start(bf16[4,10240]{1,0:T(4,128)(2,1)S(1)} %get-tuple-element.26), channel_id=1, source_target_pairs={{0,4},{4,0},{8,12},{12,8},{1,5},{5,1},{9,13},{13,9},{2,6},{6,2},{1... | collective-permute-start | bytes 245768 | tf_op jit(solution)/shard_map/ppermute | solution.py:584
  179.4 20.0 %collective-permute-start.17 = (bf16[4,10240]{1,0:T(4,128)(2,1)S(1)}, bf16[4,10240]{1,0:T(4,128)(2,1)S(1)}, u32[]{:S(2)}, u32[]{:S(2)}) collective-permute-start(bf16[4,10240]{1,0:T(4,128)(2,1)S(1)} %get-tuple-element.27), channel_id=1, source_target_pairs={{0,8},{4,12},{8,0},{12,4},{1,9},{5,13},{9,1},{13,5},{2,10},{6,14},... | collective-permute-start | bytes 245768 | tf_op jit(solution)/shard_map/ppermute | solution.py:584
  184.5 16.3 %collective-permute-start.18 = (bf16[4,10240]{1,0:T(4,128)(2,1)S(1)}, bf16[4,10240]{1,0:T(4,128)(2,1)S(1)}, u32[]{:S(2)}, u32[]{:S(2)}) collective-permute-start(bf16[4,10240]{1,0:T(4,128)(2,1)S(1)} %get-tuple-element.28), channel_id=1, source_target_pairs={{0,12},{4,8},{8,4},{12,0},{1,13},{5,9},{9,5},{13,1},{2,14},{6,10},... | collective-permute-start | bytes 245768 | tf_op jit(solution)/shard_map/ppermute | solution.py:584
  196.4 8.0 %collective-permute-start.10 = (bf16[32,2048]{1,0:T(8,128)(2,1)S(1)}, bf16[32,2048]{1,0:T(8,128)(2,1)S(1)}, u32[]{:S(2)}, u32[]{:S(2)}) collective-permute-start(bf16[32,2048]{1,0:T(8,128)(2,1)S(1)} %down_proj.1.refs_0_), channel_id=1, source_target_pairs={{0,1},{1,2},{2,3},{3,0},{4,5},{5,6},{6,7},{7,4},{8,9},{9,10},{10,1... | collective-permute-start | bytes 393224 | tf_op jit(solution)/shard_map/ppermute | solution.py:588
  199.4 9.9 %collective-permute-start.11 = (bf16[32,2048]{1,0:T(8,128)(2,1)S(1)}, bf16[32,2048]{1,0:T(8,128)(2,1)S(1)}, u32[]{:S(2)}, u32[]{:S(2)}) collective-permute-start(bf16[32,2048]{1,0:T(8,128)(2,1)S(1)} %down_proj.1.refs_0_), channel_id=1, source_target_pairs={{0,2},{1,3},{2,0},{3,1},{4,6},{5,7},{6,4},{7,5},{8,10},{9,11},{10,... | collective-permute-start | bytes 393224 | tf_op jit(solution)/shard_map/ppermute | solution.py:588
  200.8 8.8 %collective-permute-start.12 = (bf16[32,2048]{1,0:T(8,128)(2,1)S(1)}, bf16[32,2048]{1,0:T(8,128)(2,1)S(1)}, u32[]{:S(2)}, u32[]{:S(2)}) collective-permute-start(bf16[32,2048]{1,0:T(8,128)(2,1)S(1)} %down_proj.1.refs_0_), channel_id=1, source_target_pairs={{0,3},{1,0},{2,1},{3,2},{4,7},{5,4},{6,5},{7,6},{8,11},{9,8},{10,9... | collective-permute-start | bytes 393224 | tf_op jit(solution)/shard_map/ppermute | solution.py:588
  (8 other events, 17.6 us)
where the time goes:
time: 220 us; the launch traced here: 219 us
  waiting for transfers between devices  118 us (54%)
  Pallas kernels  44.2 us (20%)
  local copies, waits for them, and re-layouts  30.4 us (14%)
  starting transfers between devices  24.5 us (11%)
    ppermute x13, waiting for transfers between devices, to_dp(): return lax.ppermute(value, 'dp', pairs)  104 us
    pallas_call x11, Pallas kernels, call(): pl.pallas_call(kernel, out_shape=outs, in_specs=in_specs, out_specs=out_s...  44.2 us
    unnamed x44, local copies, waits for them, and re-layouts  29.8 us
    ppermute x13, starting transfers between devices, to_dp(): return lax.ppermute(value, 'dp', pairs)  14.6 us
    ppermute x6, waiting for transfers between devices, over_tensor(): lax.ppermute(value, 'tensor', [(i, (i + s) % ranks) for i in range(ranks)])  13.9 us
    ppermute x6, starting transfers between devices, over_tensor(): lax.ppermute(value, 'tensor', [(i, (i + s) % ranks) for i in range(ranks)])  9.92 us
  transfers between devices with their start and end apart: 19, of which 12 were waited for; matrix products, arithmetic and copies ran while one was open for 1% of the time, Pallas kernels for 18%

commit v1 on v0

v1 whole, which is shorter than its diff:
```python
import functools

import jax
import jax.numpy as jnp
from jax import lax
from jax.experimental import pallas as pl
from jax.experimental.pallas import tpu as pltpu
from jax.sharding import PartitionSpec as P

D = 8192
H = 128
G = 8
EPS = 1e-05
LANES = 128
MIB = 1 << 20

F32 = jnp.float32
BF16 = jnp.bfloat16

VM = pl.BlockSpec(memory_space=pltpu.VMEM)
SM = pl.BlockSpec(memory_space=pltpu.SMEM)
ANY = pl.BlockSpec(memory_space=pl.ANY)


def dot(a, b):
    return jnp.dot(a, b, preferred_element_type=F32)


def dot_t(a, b):
    return lax.dot_general(a, b, (((1,), (1,)), ((), ())), preferred_element_type=F32)


def iota(shape, dim):
    return lax.broadcasted_iota(jnp.int32, shape, dim)


def one_hot(condition):
    return jnp.where(condition, 1.0, 0.0).astype(BF16)


def codes(parents_ref, local_rows, capacity, slots):
    rows = parents_ref.shape[1]
    parents = parents_ref[...]
    one, other = iota((rows, rows), 0), iota((rows, rows), 1)
    across = jnp.broadcast_to(parents, (rows, rows))
    down = jnp.sum(jnp.where(one == other, across, 0), axis=1, keepdims=True)
    same = (across // local_rows == down // local_rows) & (one // local_rows == other // local_rows)
    rank_row = jnp.sum(jnp.where(same & (one < other), 1, 0), axis=0, keepdims=True)
    rank_col = jnp.sum(jnp.where(same & (other < one), 1, 0), axis=1, keepdims=True)
    code_row = parents // local_rows * slots + iota((1, rows), 1) // local_rows * capacity + rank_row
    code_col = down // local_rows * slots + iota((rows, 1), 0) // local_rows * capacity + rank_col
    return code_row, code_col


def in_hbm(value):
    return pltpu.with_memory_space_constraint(value, pltpu.HBM)


def in_vmem(value):
    return pltpu.with_memory_space_constraint(value, pltpu.VMEM)


def split_two(value):
    high = value.astype(BF16)
    low = (value - high.astype(F32)).astype(BF16)
    return high, low


def call(kernel, outs, in_specs, args, vmem, name, scratch=(), out_specs=None, cost=None):
    single = not isinstance(outs, (list, tuple))
    if out_specs is None:
        out_specs = VM if single else [VM] * len(outs)
    return pl.pallas_call(
        kernel,
        out_shape=outs,
        in_specs=in_specs,
        out_specs=out_specs,
        scratch_shapes=list(scratch),
        name=name,
        cost_estimate=cost,
        compiler_params=pltpu.CompilerParams(vmem_limit_bytes=vmem),
    )(*args)


def shape_of(shape, dtype):
    return jax.ShapeDtypeStruct(shape, dtype)


def first_rows_kernel(ids_ref, parents_ref, state_ref, *refs):
    out_refs, sem = refs[:-1], refs[-1]
    local_rows = state_ref.shape[0]
    both = 2 * local_rows
    me = ids_ref[0]
    copies = []
    for hop, out_ref in enumerate(out_refs, 1):
        to = ids_ref[2 * hop] // 2
        low = jnp.int32(local_rows)
        for i in range(both):
            parent = parents_ref[0, to * both + i]
            here = parent // local_rows == me
            low = jnp.where(here, jnp.minimum(low, lax.rem(parent, local_rows)), low)
        row = jnp.where(low < local_rows, low, 0)
        copies.append(pltpu.make_async_copy(state_ref.at[pl.ds(row, 1)], out_ref, sem.at[hop - 1]))
        copies[-1].start()
    for copy in copies:
        copy.wait()


def first_rows(targets, parents, state):
    count = targets.shape[0] // 2 - 1
    return call(
        first_rows_kernel,
        [pltpu.VMEM((1, *state.shape[1:]), BF16)] * count,
        [SM, SM, ANY],
        (targets, parents, in_hbm(state)),
        MIB,
        "first_rows",
        scratch=[pltpu.SemaphoreType.DMA((count,))],
    )


def in_load_kernel(
    tok_hbm, gain_hbm, dt_hbm, xz_hbm, lhs_ref, tail_ref, piece_ref, tok_ref, gain_ref, dt_ref, sem_small, sem
):
    rows, depth = tok_ref.shape
    heads = dt_hbm.shape[0]
    small = [
        pltpu.make_async_copy(tok_hbm, tok_ref, sem_small.at[0]),
        pltpu.make_async_copy(gain_hbm, gain_ref, sem_small.at[1]),
        pltpu.make_async_copy(dt_hbm, dt_ref.at[pl.ds(0, heads)], sem_small.at[2]),
    ]
    copies = [pltpu.make_async_copy(xz_hbm.at[:, t], piece_ref.at[t], sem.at[t]) for t in range(piece_ref.shape[0])]
    for one in small + copies:
        one.start()
    dt_ref[heads:, :] = jnp.zeros((LANES - heads, depth), BF16)
    small[0].wait()
    small[1].wait()
    inputs = tok_ref[...].astype(F32)
    squares = jnp.sum(inputs * inputs, axis=1, keepdims=True)
    scaled = (inputs * gain_ref[0:1, :]).astype(BF16)
    row = iota((LANES, 4 * LANES), 0)
    col = iota((LANES, 4 * LANES), 1)
    spread = one_hot((col == 2 * row) | (col == 2 * LANES + 2 * row + 1))
    blocks = depth // LANES
    stacked = jnp.concatenate([scaled[:, i * LANES : (i + 1) * LANES] for i in range(blocks)], axis=0)
    wide = dot(stacked, spread).astype(BF16)
    for i in range(blocks):
        where = slice(i * 2 * LANES, (i + 1) * 2 * LANES)
        block = wide[i * rows : (i + 1) * rows]
        lhs_ref[0:rows, where] = block[:, : 2 * LANES]
        lhs_ref[rows : 2 * rows, where] = block[:, 2 * LANES :]
    small[2].wait()
    tail = dot_t(scaled, dt_ref[...])
    high, low = split_two(squares)
    lane = iota(tail.shape, 1)
    tail = jnp.where(lane == heads, high.astype(F32), jnp.where(lane == heads + 1, low.astype(F32), tail))
    tail_ref[...] = tail.astype(BF16)
    for one in copies:
        one.wait()


def multiply_tiles(lhs, tiles_ref, store):
    count = tiles_ref.shape[0]
    step = 2 if count % 2 == 0 else 1
    for t in range(0, count, step):
        weights = tiles_ref[t] if step == 1 else jnp.concatenate([tiles_ref[t], tiles_ref[t + 1]], axis=1)
        store(t * LANES, step * LANES, dot(lhs, weights).astype(BF16))


def in_middle_kernel(lhs_ref, tiles_ref, xz_hbm, bc_hbm, out_ref, piece_ref, piece_bc_ref, sem, sem_bc):
    done = tiles_ref.shape[0]
    copies = [
        pltpu.make_async_copy(xz_hbm.at[:, done + t], piece_ref.at[t], sem.at[t]) for t in range(piece_ref.shape[0])
    ] + [pltpu.make_async_copy(bc_hbm.at[:, t], piece_bc_ref.at[t], sem_bc.at[t]) for t in range(piece_bc_ref.shape[0])]
    for one in copies:
        one.start()

    def store(start, width, product):
        out_ref[:, start : start + width] = product

    multiply_tiles(lhs_ref[...], tiles_ref, store)
    for one in copies:
        one.wait()


def in_last_kernel(lhs_ref, early_ref, tail_ref, tiles_ref, tiles_bc_ref, out_ref):
    rows = tail_ref.shape[0]
    before = early_ref.shape[1]
    inner = before + tiles_ref.shape[0] * LANES
    groups_width = tiles_bc_ref.shape[0] * LANES
    out_ref[:, 0:before] = early_ref[0:rows]
    out_ref[:, inner : inner + before] = early_ref[rows : 2 * rows]
    base = 2 * inner + 2 * groups_width
    out_ref[:, base : base + LANES] = tail_ref[...]

    def store_at(first, second):
        def store(start, width, product):
            out_ref[:, first + start : first + start + width] = product[0:rows]
            out_ref[:, second + start : second + start + width] = product[rows : 2 * rows]

        return store

    multiply_tiles(lhs_ref[...], tiles_ref, store_at(before, inner + before))
    multiply_tiles(lhs_ref[...], tiles_bc_ref, store_at(2 * inner, 2 * inner + groups_width))


def in_proj(tokens, gains, weight_xz, weight_bc, weight_dt):
    rows, depth = tokens.shape
    inner = weight_xz.shape[2]
    groups_width = weight_bc.shape[2]
    heads = weight_dt.shape[1]
    tiles, tiles_bc = inner // LANES, groups_width // LANES
    half = tiles // 2
    xz = weight_xz.reshape(depth, 2, tiles, LANES).transpose(0, 2, 1, 3)
    bc = weight_bc.reshape(depth, 2, tiles_bc, LANES).transpose(0, 2, 1, 3)
    width = 2 * inner + 2 * groups_width + LANES

    def flat(piece):
        return in_vmem(piece.reshape(piece.shape[0], 2 * depth, LANES))

    def piece_of(count):
        return pltpu.VMEM((count, depth, 2, LANES), BF16)

    lhs, tail, piece = call(
        in_load_kernel,
        [shape_of((2 * rows, 2 * depth), BF16), shape_of((rows, LANES), BF16), piece_of(half)],
        [ANY] * 4,
        [in_hbm(one) for one in (tokens, gains, weight_dt.T, xz)],
        6 * MIB,
        "in_load",
        scratch=[
            pltpu.VMEM((rows, depth), BF16),
            pltpu.VMEM(gains.shape, F32),
            pltpu.VMEM((LANES, depth), BF16),
            pltpu.SemaphoreType.DMA((3,)),
            pltpu.SemaphoreType.DMA((half,)),
        ],
        cost=moved(weight_xz.size),
    )
    early, piece, piece_bc = call(
        in_middle_kernel,
        [shape_of((2 * rows, half * LANES), BF16), piece_of(tiles - half), piece_of(tiles_bc)],
        [VM, VM, ANY, ANY],
        (lhs, flat(piece), in_hbm(xz), in_hbm(bc)),
        8 * MIB,
        "in_middle",
        scratch=[pltpu.SemaphoreType.DMA((tiles - half,)), pltpu.SemaphoreType.DMA((tiles_bc,))],
    )
    return call(
        in_last_kernel,
        shape_of((rows, width), BF16),
        [VM] * 5,
        (lhs, early, tail, flat(piece), flat(piece_bc)),
        8 * MIB,
        "in_last",
    )


def moved(size):
    return pl.CostEstimate(flops=0, bytes_accessed=2 * size, transcendentals=0)


def prefetch_kernel(from_ref, to_ref, sem):
    copy = pltpu.make_async_copy(from_ref, to_ref, sem)
    copy.start()
    copy.wait()


def prefetch(weight, after):
    weight, _ = lax.optimization_barrier((weight, after))
    return call(
        prefetch_kernel,
        pltpu.VMEM(weight.shape, BF16),
        [ANY],
        (in_hbm(weight),),
        MIB,
        "prefetch",
        scratch=[pltpu.SemaphoreType.DMA],
        cost=moved(2 * weight.size),
    )


def pick_rows_kernel(local_rows, capacity, slots, ids_ref, own_ref, other_ref, parents_ref, *out_refs):
    code_row, _ = codes(parents_ref, local_rows, capacity, slots)
    total = (own_ref[...].astype(F32) + other_ref[...].astype(F32)).astype(BF16)
    rows = total.shape[0]
    slot = iota((slots, rows), 0)
    for i, out_ref in enumerate(out_refs):
        pick = one_hot(code_row == ids_ref[i] * slots + slot)
        out_ref[...] = dot(pick, total).astype(BF16)


def pick_rows(targets, own, other, parents, local_rows, capacity, slots):
    width = own.shape[1]
    count = targets.shape[0]
    return call(
        functools.partial(pick_rows_kernel, local_rows, capacity, slots),
        [shape_of((slots, width), BF16)] * count,
        [SM, VM, VM, VM],
        (targets, own, other, parents),
        8 * MIB,
        "pick_rows",
    )


def chip_sum_kernel(own_ref, other_ref, out_ref):
    out_ref[...] = (own_ref[...].astype(F32) + other_ref[...].astype(F32)).astype(BF16)


def chip_sum(own, other):
    return call(chip_sum_kernel, shape_of(own.shape, BF16), [VM, VM], (own, other), 4 * MIB, "chip_sum")


def mixer_kernel(parts, heads, capacity, ids_ref, parents_ref, *refs):
    part_refs = refs[:parts]
    (
        conv_ref,
        conv_bc_ref,
        bias_ref,
        rates_ref,
        skip_ref,
        gain_ref,
        queue_ref,
        queue_bc_ref,
        state_hbm,
        act_ref,
        message_ref,
        state_ref,
        sem,
    ) = refs[parts:]
    fetched = [pltpu.make_async_copy(state_hbm.at[r], state_ref.at[r], sem.at[r]) for r in range(state_ref.shape[0])]
    for one in fetched:
        one.start()
    slots = part_refs[0].shape[0]
    inner = gain_ref.shape[1]
    lags, local_rows, _ = queue_ref.shape
    groups_width = queue_bc_ref.shape[3]
    state_size = state_ref.shape[3]
    head_size = state_ref.shape[2]
    groups_here = groups_width // state_size
    per_group = inner // groups_here
    proj = part_refs[0][...].astype(F32)
    for ref in part_refs[1:]:
        proj = proj + ref[...].astype(F32)
    base_bc = 2 * inner
    base = base_bc + 2 * groups_width
    tail = proj[:, base : base + LANES]
    lane = iota(tail.shape, 1)
    squares = jnp.sum(jnp.where((lane == heads) | (lane == heads + 1), tail, 0.0), axis=1, keepdims=True)
    scale = lax.rsqrt(squares / D + EPS)
    code_row, _ = codes(parents_ref, local_rows, capacity, slots)
    slot = iota((slots, code_row.shape[1]), 0)
    mine = code_row == ids_ref[0] * slots + slot
    valid = jnp.sum(jnp.where(mine, 1.0, 0.0), axis=1, keepdims=True)
    parent = jnp.sum(jnp.where(mine, lax.rem(parents_ref[...], local_rows), 0), axis=1, keepdims=True)
    pick = jnp.where((iota((slots, local_rows), 1) == parent) & (valid > 0.0), 1.0, 0.0).astype(BF16)

    now = proj[:, 0:inner] * scale
    gate = proj[:, inner : 2 * inner] * scale
    conv = now * conv_ref[lags : lags + 1, :]
    for k in range(lags):
        held = dot(pick, queue_ref[k])
        conv = conv + held * conv_ref[k : k + 1, :]
        if k > 0:
            message_ref[:, (k - 1) * inner : k * inner] = held.astype(BF16)
    message_ref[:, (lags - 1) * inner : lags * inner] = now.astype(BF16)
    inner_vals = conv * jax.nn.sigmoid(conv)
    at = lags * inner
    keys = []
    for j in range(2):
        start = base_bc + j * groups_width
        now_bc = proj[:, start : start + groups_width] * scale
        conv_bc = now_bc * conv_bc_ref[lags, j : j + 1, :]
        for k in range(lags):
            held = dot(pick, queue_bc_ref[k, j])
            conv_bc = conv_bc + held * conv_bc_ref[k, j : j + 1, :]
            if k > 0:
                to = at + ((k - 1) * 2 + j) * groups_width
                message_ref[:, to : to + groups_width] = held.astype(BF16)
        to = at + ((lags - 1) * 2 + j) * groups_width
        message_ref[:, to : to + groups_width] = now_bc.astype(BF16)
        keys.append(conv_bc * jax.nn.sigmoid(conv_bc))
    at = at + lags * 2 * groups_width

    raw = tail * scale + bias_ref[...]
    steps = jnp.maximum(raw, 0.0) + jnp.log1p(jnp.exp(-jnp.abs(raw)))
    decays = jnp.exp(-steps * rates_ref[...])
    spread = one_hot(iota((LANES, inner), 0) == iota((LANES, inner), 1) // head_size)

    def expand(value):
        high, low = split_two(value)
        return dot(high, spread) + dot(low, spread)

    steps_wide = expand(steps)
    decays_wide = expand(decays)
    skip_wide = expand(jnp.broadcast_to(skip_ref[...], (8, LANES)))[0:1]
    update = steps_wide * inner_vals
    message_ref[:, at : at + inner] = update.astype(BF16)
    at = at + inner
    message_ref[:, at : at + groups_width] = keys[0].astype(BF16)
    at = at + groups_width
    decay_high, decay_low = split_two(decays)
    message_ref[:, at : at + LANES] = decay_high
    message_ref[:, at + LANES : at + 2 * LANES] = decay_low

    for g in range(groups_here):
        lanes = slice(g * state_size, (g + 1) * state_size)
        wide = slice(g * per_group, (g + 1) * per_group)
        b_vals, c_vals = keys[0][:, lanes], keys[1][:, lanes]
        high, low = split_two(c_vals)
        c_both = jnp.concatenate([high, low], axis=0)
        mixed = jnp.zeros((slots, per_group), F32)
        first_head = g * (per_group // head_size)
        for r in range(local_rows):
            if g == 0:
                fetched[r].wait()
            block = state_ref[r, first_head : first_head + per_group // head_size]
            both = dot_t(c_both, block.reshape(per_group, state_size))
            mixed = mixed + jnp.where(parent == r, both[0:slots] + both[slots : 2 * slots], 0.0)
        inside = jnp.sum(b_vals * c_vals, axis=1, keepdims=True)
        mixed = decays_wide[:, wide] * mixed + update[:, wide] * inside + skip_wide[:, wide] * inner_vals[:, wide]
        gated = mixed * (gate[:, wide] * jax.nn.sigmoid(gate[:, wide]))
        mean = jnp.sum(gated * gated, axis=1, keepdims=True) / per_group
        out = gated * lax.rsqrt(mean + EPS) * gain_ref[:, wide]
        act_ref[:, wide] = jnp.where(valid > 0.0, out, 0.0).astype(BF16)


def mixer(ids, parents, capacity, parts, params, queue, queue_bc, state):
    conv, conv_bc, bias, rates, skip, gain = params
    slots = parts[0].shape[0]
    inner = gain.shape[0]
    lags = queue.shape[0]
    groups_width = queue_bc.shape[3]
    heads = bias.shape[0]
    message = lags * (inner + 2 * groups_width) + inner + groups_width + 2 * LANES

    def lane_row(vector):
        return jnp.pad(vector, (0, LANES - heads)).reshape(1, LANES)

    return call(
        functools.partial(mixer_kernel, len(parts), heads, capacity),
        [shape_of((slots, inner), BF16), shape_of((slots, message), BF16)],
        [SM, VM] + [VM] * len(parts) + [VM] * 8 + [ANY],
        (ids, parents, *parts, conv, conv_bc, lane_row(bias), lane_row(rates), lane_row(skip), gain.reshape(1, inner), queue, queue_bc, in_hbm(state)),
        10 * MIB,
        "mixer",
        scratch=[pltpu.VMEM(state.shape, BF16), pltpu.SemaphoreType.DMA((state.shape[0],))],
    )


def deal_kernel(capacity, ids_ref, message_ref, *out_refs):
    slots = message_ref.shape[0]
    count = len(out_refs)
    row = iota((slots, slots), 0)
    want = row
    for i in range(slots // capacity):
        want = jnp.where(row // capacity == i, ids_ref[i] * capacity + row % capacity, want)
    order = one_hot(iota((slots, slots), 1) == want)
    dealt = dot(order, message_ref[...])
    at = 0
    for out_ref in out_refs:
        size = out_ref.shape[0]
        out_ref[...] = dealt[at : at + size].astype(BF16)
        at += size


def deal(targets, message, capacity):
    sizes = [capacity, capacity] + [2 * capacity] * (targets.shape[0] // 2 - 1)
    return call(
        functools.partial(deal_kernel, capacity),
        [shape_of((size, message.shape[1]), BF16) for size in sizes],
        [SM, VM],
        (targets, message),
        8 * MIB,
        "deal",
    )


def collect_kernel(rows, capacity, slots, lags, groups_width, ids_ref, parents_ref, *refs):
    in_refs, (inner_ref, groups_ref, update_ref, keys_ref, decay_ref) = refs[:-5], refs[-5:]
    count = len(in_refs)
    code_row, code_col = codes(parents_ref, rows, capacity, slots)
    everyone = code_col.shape[0]
    inner = update_ref.shape[1]
    me = ids_ref[0]
    parts = []
    for i, ref in enumerate(in_refs):
        value = ref[...].astype(F32)
        start = capacity if i > 1 and i % 2 else 0
        parts.append(value[start : start + capacity])
    held = jnp.concatenate(parts, axis=0).astype(BF16)
    col = iota((everyone, count * capacity), 1)
    want = jnp.full(col.shape, -1, jnp.int32)
    for i in range(count):
        want = jnp.where(col // capacity == i, ids_ref[i] * slots + me * capacity + col % capacity, want)
    chosen = one_hot(code_col == want)
    here = one_hot(iota((rows, everyone), 1) == me * rows + iota((rows, everyone), 0))
    mine = dot(dot(here, chosen).astype(BF16), held)
    for k in range(lags):
        inner_ref[k] = mine[:, k * inner : (k + 1) * inner].astype(BF16)
    at = lags * inner
    for k in range(lags):
        for j in range(2):
            start = at + (2 * k + j) * groups_width
            groups_ref[:, k, j, :] = mine[:, start : start + groups_width].astype(BF16)
    at = at + 2 * lags * groups_width
    update_ref[...] = mine[:, at : at + inner]
    at = at + inner
    keys_ref[...] = mine[:, at : at + groups_width]
    at = at + groups_width
    decay_ref[...] = mine[:, at : at + LANES] + mine[:, at + LANES : at + 2 * LANES]


def collect(sources, parents, rows, messages, slots, inner, groups_width, lags):
    capacity = messages[0].shape[0]
    return call(
        functools.partial(collect_kernel, rows, capacity, slots, lags, groups_width),
        [
            shape_of((lags, rows, inner), BF16),
            shape_of((rows, lags, 2, groups_width), BF16),
            shape_of((rows, inner), F32),
            shape_of((rows, groups_width), F32),
            shape_of((rows, LANES), F32),
        ],
        [SM, VM] + [VM] * len(messages),
        (sources, parents, *messages),
        8 * MIB,
        "collect",
    )


def fetch_row(entry, local_rows, kinds, refs, to, sem):
    kind = entry // local_rows
    row = lax.rem(entry, local_rows)
    for known, ref in zip(kinds, refs):

        @pl.when(kind == known)
        def _(ref=ref):
            pltpu.make_async_copy(ref.at[pl.ds(row, 1)], to, sem).start()


def gather_kernel(local_rows, kinds, table_ref, *refs):
    count = len(kinds)
    in_refs, out_refs, sem = refs[:count], refs[count:-1], refs[-1]
    places = [(ref, i) for ref in out_refs for i in range(ref.shape[0])]
    for j, (ref, i) in enumerate(places):
        fetch_row(table_ref[j], local_rows, kinds, in_refs, ref.at[pl.ds(i, 1)], sem.at[j])
    for j, (ref, i) in enumerate(places):
        pltpu.make_async_copy(in_refs[0].at[pl.ds(0, 1)], ref.at[pl.ds(i, 1)], sem.at[j]).wait()


def gather_rows(table, states, sizes):
    shape = states[0].shape
    return call(
        functools.partial(gather_kernel, shape[0], tuple(range(len(states)))),
        [pltpu.VMEM((size, *shape[1:]), BF16) for size in sizes],
        [SM] + [ANY] * len(states),
        (table, in_hbm(states[0]), *states[1:]),
        MIB,
        "gather_rows",
        scratch=[pltpu.SemaphoreType.DMA((sum(sizes),))],
    )


def update_kernel(kinds, is_mine, table_ref, *refs):
    sources = len(kinds)
    state_refs = refs[:sources]
    update_ref, keys_ref, decay_ref = refs[sources : sources + 3]
    out_ref, held, made, sem_in, sem_out = refs[-5:]
    rows, heads, head_size, state_size = held.shape
    inner = update_ref.shape[1]
    groups_here = keys_ref.shape[1] // state_size
    per_group = inner // groups_here
    heads_group = heads // groups_here

    mine = [is_mine(table_ref[j] // rows) for j in range(rows)]
    for j in range(rows):

        @pl.when(mine[j])
        def _(j=j):
            fetch_row(table_ref[j], rows, kinds, state_refs, held.at[pl.ds(j, 1)], sem_in.at[j])

    spread = one_hot(iota((LANES, inner), 0) == iota((LANES, inner), 1) // head_size)
    high, low = split_two(decay_ref[...])
    decay_high, decay_low = dot(high, spread), dot(low, spread)
    columns = []
    for g in range(groups_here):
        wide = slice(g * per_group, (g + 1) * per_group)
        stacked = jnp.concatenate([update_ref[:, wide], decay_high[:, wide], decay_low[:, wide]], axis=0)
        columns.append(jnp.transpose(stacked).astype(BF16))
    row_id = iota((3 * rows, state_size), 0)
    def renew(j):
        pltpu.make_async_copy(state_refs[0].at[pl.ds(0, 1)], held.at[pl.ds(j, 1)], sem_in.at[j]).wait()
        for g in range(groups_here):
            keys = keys_ref[j : j + 1, g * state_size : (g + 1) * state_size]
            right_keys = jnp.where(row_id == j, keys, 0.0)
            right_ones = jnp.where((row_id == rows + j) | (row_id == 2 * rows + j), 1.0, 0.0)
            right = jnp.concatenate([right_keys, right_ones], axis=1).astype(BF16)
            both = dot(columns[g], right)
            which = slice(g * heads_group, (g + 1) * heads_group)
            before = held[j, which].reshape(per_group, state_size).astype(F32)
            after = both[:, state_size:] * before + both[:, :state_size]
            made[j, which] = after.astype(BF16).reshape(heads_group, head_size, state_size)
        pltpu.make_async_copy(made.at[j], out_ref.at[j], sem_out.at[j]).start()

    for j in range(rows):
        pl.when(mine[j])(functools.partial(renew, j))
    for j in range(rows):

        @pl.when(mine[j])
        def _(j=j):
            pltpu.make_async_copy(made.at[j], out_ref.at[j], sem_out.at[j]).wait()


def update_state(table, states, update, keys, decay, is_mine, before=None):
    kinds = tuple(sorted(states))
    shape = states[0].shape
    args = [table, in_hbm(states[0]), *[states[kind] for kind in kinds[1:]], update, keys, decay]
    specs = [SM] + [ANY] * len(kinds) + [VM] * 3
    aliases = {}
    if before is not None:
        aliases = {len(args): 0}
        args.append(in_hbm(before))
        specs.append(pl.BlockSpec(memory_space=pltpu.HBM))
    return pl.pallas_call(
        functools.partial(update_kernel, kinds, is_mine),
        out_shape=pltpu.HBM(shape, BF16),
        in_specs=specs,
        out_specs=pl.BlockSpec(memory_space=pltpu.HBM),
        scratch_shapes=[
            pltpu.VMEM(shape, BF16),
            pltpu.VMEM(shape, BF16),
            pltpu.SemaphoreType.DMA((shape[0],)),
            pltpu.SemaphoreType.DMA((shape[0],)),
        ],
        input_output_aliases=aliases,
        name="update_state",
        compiler_params=pltpu.CompilerParams(vmem_limit_bytes=16 * MIB),
    )(*args)


def no_rows_kernel(*refs):
    pass


def no_rows(shape, count):
    return pl.pallas_call(
        no_rows_kernel,
        out_shape=[pltpu.HBM(shape, BF16)] * count,
        out_specs=[pl.BlockSpec(memory_space=pltpu.HBM)] * count,
        name="no_rows",
    )()


def fetch_pieces(from_ref, to_ref, sem):
    count = sem.shape[0]
    depth = to_ref.shape[0] // count
    pieces = []
    for i in range(count):
        piece = pl.ds(i * depth, depth)
        copy = pltpu.make_async_copy(from_ref.at[piece], to_ref.at[piece], sem.at[i])
        copy.start()
        pieces.append((slice(i * depth, (i + 1) * depth), copy))
    return pieces


def multiply_pieces(left, weight_ref, pieces):
    total = None
    for piece, copy in pieces:
        copy.wait()
        product = dot(left[:, piece], weight_ref[piece, :])
        total = product if total is None else total + product
    return total


def out_proj_kernel(local_rows, capacity, slots, ids_ref, parents_ref, *refs):
    act_refs, (weight_hbm, out_ref, weight_ref, sem) = refs[:-4], refs[-4:]
    pieces = fetch_pieces(weight_hbm, weight_ref, sem)
    _, code_col = codes(parents_ref, local_rows, capacity, slots)
    rows = code_col.shape[0]
    devices = len(act_refs)
    col = iota((rows, devices * slots), 1)
    want = jnp.full(col.shape, -1, jnp.int32)
    for i in range(devices):
        want = jnp.where(col // slots == i, ids_ref[i] * slots + col % slots, want)
    held = jnp.concatenate([ref[...] for ref in act_refs], axis=0)
    activity = dot(one_hot(code_col == want), held).astype(BF16)
    out_ref[...] = multiply_pieces(activity, weight_ref, pieces).astype(BF16)


def out_proj(sources, parents, local_rows, capacity, acts, weight):
    rows = parents.shape[1]
    return call(
        functools.partial(out_proj_kernel, local_rows, capacity, acts[0].shape[0]),
        shape_of((rows, weight.shape[1]), BF16),
        [SM, VM] + [VM] * len(acts) + [ANY],
        (sources, parents, *acts, in_hbm(weight)),
        12 * MIB,
        "out_proj",
        scratch=[pltpu.VMEM(weight.shape, BF16), pltpu.SemaphoreType.DMA((4,))],
    )


def up_kernel(parts, tok_ref, gain_ref, *refs):
    part_refs = refs[:parts]
    weight_ref, residual_ref, out_ref = refs[parts:]
    residual = tok_ref[...].astype(F32)
    total = part_refs[0][...].astype(F32)
    for ref in part_refs[1:]:
        total = total + ref[...].astype(F32)
    residual = residual + total
    residual_ref[...] = residual
    squares = jnp.sum(residual * residual, axis=1, keepdims=True)
    scaled = (residual * gain_ref[1:2, :]).astype(BF16)
    width = weight_ref.shape[1]
    high, low = split_two(squares)
    lane = iota((scaled.shape[0], LANES), 1)
    out_ref[:, width : width + LANES] = jnp.where(
        lane == 0, high.astype(F32), jnp.where(lane == 1, low.astype(F32), 0.0)
    ).astype(BF16)
    out_ref[:, 0:width] = dot(scaled, weight_ref[...]).astype(BF16)


def up_proj(tokens, gains, parts, weight):
    rows, width = tokens.shape
    return call(
        functools.partial(up_kernel, len(parts)),
        [shape_of((rows, width), F32), shape_of((rows, weight.shape[1] + LANES), BF16)],
        [VM] * (len(parts) + 3),
        (tokens, gains, *parts, in_vmem(weight)),
        8 * MIB,
        "up_proj",
    )


def down_kernel(*refs):
    part_refs, (weight_hbm, out_ref, weight_ref, sem) = refs[:-4], refs[-4:]
    pieces = fetch_pieces(weight_hbm, weight_ref, sem)
    total = part_refs[0][...].astype(F32)
    for ref in part_refs[1:]:
        total = total + ref[...].astype(F32)
    width = weight_ref.shape[0]
    squares = jnp.sum(total[:, width : width + LANES], axis=1, keepdims=True)
    hidden = jnp.maximum(total[:, 0:width] * lax.rsqrt(squares / D + EPS), 0.0)
    out_ref[...] = multiply_pieces((hidden * hidden).astype(BF16), weight_ref, pieces).astype(BF16)


def down_proj(parts, weight):
    rows = parts[0].shape[0]
    return call(
        down_kernel,
        shape_of((rows, weight.shape[1]), BF16),
        [VM] * len(parts) + [ANY],
        (*parts, in_hbm(weight)),
        20 * MIB,
        "down_proj",
        scratch=[pltpu.VMEM(weight.shape, BF16), pltpu.SemaphoreType.DMA((8,))],
    )


def finish_kernel(residual_ref, *refs):
    part_refs, out_ref = refs[:-1], refs[-1]
    total = part_refs[0][...].astype(F32)
    for ref in part_refs[1:]:
        total = total + ref[...].astype(F32)
    out_ref[0] = (residual_ref[...] + total).astype(BF16)


def finish(residual, parts):
    return call(
        finish_kernel,
        shape_of((1, *residual.shape), BF16),
        [VM] * (len(parts) + 1),
        (residual, *parts),
        6 * MIB,
        "finish",
    )


def plan_rows(chosen, chips, local_rows):
    rows = chosen.shape[0]
    both = 2 * local_rows
    same = chosen[:, None] == jnp.arange(rows, dtype=jnp.int32)[None, :]
    needed = jnp.any(same.reshape(chips, both, rows), axis=1).reshape(chips, chips, 2, local_rows)
    small = jnp.arange(local_rows, dtype=jnp.int32)
    before = jnp.sum(jnp.where(small[None, :] < small[:, None], needed[:, :, :, None, :], False), axis=4)
    first = (needed & (before == 0)).reshape(chips, chips, both)
    needed = needed.reshape(chips, chips, both)
    rest = needed & ~first
    wide = jnp.arange(both, dtype=jnp.int32)
    rank = jnp.sum(jnp.where(wide[None, :] < wide[:, None], rest[:, :, None, :], False), axis=3)
    lane = jnp.where(first, wide // local_rows, rank % 2)
    turn = jnp.where(first, 0, 1 + rank // 2)
    return needed, lane.astype(jnp.int32), turn.astype(jnp.int32)


def rounds_of(chosen, chips, local_rows):
    rows = chosen.shape[0]
    same = chosen[:, None] == jnp.arange(rows, dtype=jnp.int32)[None, :]
    needed = jnp.any(same.reshape(chips, 2 * local_rows, rows), axis=1).reshape(chips, chips, 2, local_rows)
    counts = jnp.sum(needed, axis=3).astype(jnp.int32)
    rest = jnp.sum(counts - jnp.minimum(counts, 1), axis=2)
    apart = jnp.arange(chips)[:, None] != jnp.arange(chips)[None, :]
    return jnp.max(jnp.where(apart, 1 + (rest + 1) // 2, 0))


def on_device(
    tokens,
    parents,
    norm_gains,
    weight_xz,
    weight_bc,
    weight_dt,
    conv_inner,
    conv_groups,
    dt_bias,
    rates,
    skip_gain,
    gate_gain,
    weight_out,
    weight_up,
    weight_down,
    ssm_state,
    queue_inner,
    queue_groups,
):
    devices = lax.axis_size("dp")
    chips = devices // 2
    ranks = lax.axis_size("tensor")
    me = lax.axis_index("dp")
    chip, core = me // 2, me % 2
    local_rows = ssm_state.shape[0]
    lags = queue_inner.shape[1]
    inner = queue_inner.shape[2]
    groups_width = queue_groups.shape[3]
    capacity = max(2, 2 * local_rows // devices)
    slots = devices * capacity
    rows = parents.shape[1]
    barrier = lax.optimization_barrier

    def to_dp(value, hop, flip):
        pairs = [(i, ((i // 2 + hop) % chips) * 2 + ((i % 2) ^ flip)) for i in range(devices)]
        return lax.ppermute(value, "dp", pairs)

    def over_tensor(value):
        return [value] + [
            lax.ppermute(value, "tensor", [(i, (i + s) % ranks) for i in range(ranks)]) for s in range(1, ranks)
        ]

    hops = [(hop, flip) for hop in range(chips) for flip in range(2)]
    sources = jnp.stack([((chip + chips - hop) % chips) * 2 + (core ^ flip) for hop, flip in hops]).astype(jnp.int32)
    targets = jnp.stack([((chip + hop) % chips) * 2 + (core ^ flip) for hop, flip in hops]).astype(jnp.int32)

    chosen = parents[0]
    place = jnp.arange(rows, dtype=jnp.int32)

    def after(value, *earlier):
        return barrier((value, *earlier))[0]

    sibling_state = to_dp(ssm_state, 0, 1)
    states = {0: ssm_state, 1: sibling_state}
    first_sent = first_rows(targets, parents, ssm_state)
    first = [to_dp(buffer, hop, 0) for hop, buffer in enumerate(first_sent, 1)]
    partial = in_proj(after(tokens[0], *first_sent), norm_gains, weight_xz, weight_bc, weight_dt)

    near = to_dp(partial, 0, 1)
    most = min(2 * local_rows, 4 * capacity)
    turns = 1 + (max(min(most, local_rows) - 1, most - 2) + 1) // 2
    early = (turns + 1) // 2
    near, *first = barrier((near, *first))
    picked = pick_rows(targets[0::2], partial, near, parents, local_rows, capacity, slots)
    needed, lane, turn = plan_rows(after(chosen, picked[0]), chips, local_rows)
    chip_rows = jnp.arange(2 * local_rows, dtype=jnp.int32)
    entries = ((chip_rows // local_rows) ^ core) * local_rows + chip_rows % local_rows
    send_tables = []
    for hop in range(1, chips):
        to = (chip + hop) % chips
        mine = needed[to, chip] & (lane[to, chip] == core)
        at_turn = mine[None, :] & (turn[to, chip][None, :] == jnp.arange(turns, dtype=jnp.int32)[:, None])
        send_tables.append(jnp.sum(jnp.where(at_turn, entries[None, :], 0), axis=1).astype(jnp.int32))

    def where_from():
        own_chosen = lax.dynamic_slice_in_dim(chosen, me * local_rows, local_rows, 0)
        parent_chip = own_chosen // (2 * local_rows)
        lookup = own_chosen[:, None] == place[None, :]
        lane_of = jnp.sum(jnp.where(lookup, lane[chip].reshape(1, rows), 0), axis=1)
        turn_of = jnp.sum(jnp.where(lookup, turn[chip].reshape(1, rows), 0), axis=1)
        hop_of = (chip + chips - parent_chip) % chips
        here = ((own_chosen // local_rows) % 2) ^ core
        start_of = jnp.minimum(turn_of, early)
        there = 2 + ((hop_of - 1) * 2 + (lane_of ^ core)) * turns + start_of
        inside = jnp.where(parent_chip == chip, own_chosen % local_rows, turn_of - start_of)
        return (jnp.where(parent_chip == chip, here, there) * local_rows + inside).astype(jnp.int32)

    def kind_of(hop, at):
        return 2 + (hop - 1) * 2 * turns + at

    parts = [picked[0]] + [to_dp(picked[hop], hop, 0) for hop in range(1, chips)]

    waiting = []
    for hop in range(1, chips):
        wanted = after(send_tables[hop - 1][1:early], picked[0])
        waiting.append(gather_rows(wanted, [ssm_state, sibling_state], [1] * (early - 1)))
    table = where_from()
    parts[0] = after(parts[0], table, *[some[0] for some in waiting])
    act, message = mixer(
        sources,
        parents,
        capacity,
        parts,
        (conv_inner, conv_groups, dt_bias, rates, skip_gain, gate_gain),
        queue_inner.transpose(1, 0, 2),
        queue_groups.transpose(1, 2, 0, 3),
        ssm_state,
    )
    acts = [act] + [to_dp(act, hop, flip) for hop, flip in hops[1:]]
    arrived, relayed = {0: first}, {}

    def relay(at, *earlier):
        relayed[at] = [to_dp(after(some, *earlier), 0, 1) for some in arrived[at]]

    relay(0, act)
    acts[0], relayed[0] = barrier((acts[0], relayed[0]))


    def send_turn(at, *earlier):
        return [to_dp(after(some[at - 1], *earlier), hop, 0) for hop, some in enumerate(waiting, 1)]

    out_part = out_proj(sources, parents, local_rows, capacity, acts, weight_out)
    arrived[1] = send_turn(1, *acts)
    out_parts = over_tensor(out_part)
    for at in range(2, early - 1):
        arrived[at] = send_turn(at, out_part)
    weight_up = prefetch(weight_up, out_part)
    dealt = deal(targets, after(message, weight_up), capacity)
    out_parts[0], arrived[1], *dealt = barrier((out_parts[0], arrived[1], *dealt))
    residual, up_part = up_proj(tokens[0], norm_gains, out_parts, weight_up)
    last = early - 1
    between = {at: arrived[at] for at in range(2, last)}
    near_up, between = barrier((to_dp(up_part, 0, 1), between))
    arrived.update(between)
    up_chip = chip_sum(up_part, near_up)
    up_parts = [up_chip] + [to_dp(up_chip, hop, 0) for hop in range(1, chips)]

    for at in range(1, last):
        relay(at, up_chip)
    messages = [dealt[0], to_dp(after(dealt[1], up_chip), 0, 1)]
    up_parts[0], relayed = barrier((up_parts[0], relayed))
    sent = [to_dp(after(dealt[1 + hop], *up_parts), hop, 0) for hop in range(1, chips)]
    down_part = down_proj(up_parts, weight_down)
    down_parts = over_tensor(down_part)
    if last > 1:
        arrived[last] = send_turn(last, down_part)

    for some in sent:
        messages += [some, to_dp(after(some, down_part), 0, 1)]
    final_inner, final_groups, update, keys, decay = collect(
        sources, parents, local_rows, messages, slots, inner, groups_width, lags
    )

    def is_early(kind):
        return (kind < 2) | (lax.rem(kind - 2, turns) < last)

    def is_late(kind):
        return jnp.logical_not(is_early(kind))

    chosen = after(chosen, update)
    groups = lax.axis_size("groups")
    longest = rounds_of(chosen, chips, local_rows)
    for shift in range(1, groups):
        other = lax.ppermute(chosen, "groups", [(i, (i + shift) % groups) for i in range(groups)])
        longest = jnp.maximum(longest, rounds_of(other, chips, local_rows))

    def add_states(turn_range):
        for at in turn_range:
            for hop in range(1, chips):
                states[kind_of(hop, at)] = arrived[at][hop - 1]
                states[kind_of(hop, at) + turns] = relayed[at][hop - 1]

    add_states(range(last))
    final_state = update_state(table, states, update, keys, decay, is_early)
    residual, final_state = barrier((residual, final_state))
    beam_out = finish(residual, down_parts)
    relay(last, beam_out)
    add_states([last])

    more = (turns - early, *ssm_state.shape[1:])

    def fetch_more():
        fetched = []
        for hop in range(1, chips):
            wanted = send_tables[hop - 1][early:]
            (buffer,) = gather_rows(wanted, [ssm_state, sibling_state], [turns - early])
            fetched.append(to_dp(buffer, hop, 0))
            fetched.append(to_dp(fetched[-1], 0, 1))
        return tuple(fetched)

    fetched = lax.cond(longest > early, fetch_more, lambda: tuple(no_rows(more, 2 * (chips - 1))))
    late_states = {0: ssm_state}
    for hop in range(1, chips):
        for lane_kind, buffer in ((kind_of(hop, early), fetched[2 * hop - 2]), (kind_of(hop, early) + turns, fetched[2 * hop - 1])):
            late_states[lane_kind] = buffer
        for lane_kind in (kind_of(hop, last), kind_of(hop, last) + turns):
            late_states[lane_kind] = states[lane_kind]
    final_state = update_state(table, late_states, update, keys, decay, is_late, final_state)
    return (beam_out, final_state, final_inner.transpose(1, 0, 2), final_groups)


def solution(mesh):
    in_specs = (
        P(None, "groups", "dp"),
        P(None, "groups"),
        P(None, "dp"),
        P("dp", None, "tensor"),
        P("dp", None, "tensor"),
        P("dp", "tensor"),
        P(None, "tensor"),
        P(None, None, "tensor"),
        P("tensor"),
        P("tensor"),
        P("tensor"),
        P("tensor"),
        P("tensor", "dp"),
        P("dp", "tensor"),
        P("tensor", "dp"),
        P(("groups", "dp"), "tensor", None, None),
        P(("groups", "dp"), None, "tensor"),
        P(("groups", "dp"), None, None, "tensor"),
    )
    out_specs = (
        P(None, "groups", "dp"),
        P(("groups", "dp"), "tensor", None, None),
        P(("groups", "dp"), None, "tensor"),
        P(("groups", "dp"), None, None, "tensor"),
    )
    return jax.shard_map(
        on_device, mesh=mesh, in_specs=in_specs, out_specs=out_specs, check_vma=False
    )
```

time: 220 us -> 118 us (0.54)
  waiting for transfers between devices: 118 us -> 29.7 us
  local copies, waits for them, and re-layouts: 30.4 us -> 2.91 us
  Pallas kernels: 44.2 us -> 50.6 us
  starting transfers between devices: 24.5 us -> 27.8 us
  other arithmetic: 0.39 us -> 2.62 us
    ppermute x13 -> x19, waiting for transfers between devices: 104 us -> 24.5 us  [to_dp(): return lax.ppermute(value, 'dp', pairs)]
    unnamed x44 -> x33, local copies, waits for them, and re-layouts: 29.8 us -> 1.79 us
    ppermute x6, waiting for transfers between devices: 13.9 us -> 5.18 us  [over_tensor(): lax.ppermute(value, 'tensor', [(i, (i + s) % ranks) for i in range(ranks)])]
    pallas_call x0 -> x3, Pallas kernels: none -> 7.03 us  [the longest x2 7.03 us: update_state(): pl.pallas_call(functools.partial(update_kernel, kinds, is_mine), out_shap...]
    ppermute x13 -> x19, starting transfers between devices: 14.6 us -> 19.5 us  [to_dp(): return lax.ppermute(value, 'dp', pairs)]
    ppermute x6, starting transfers between devices: 9.92 us -> 7.02 us  [over_tensor(): lax.ppermute(value, 'tensor', [(i, (i + s) % ranks) for i in range(ranks)])]
    pallas_call x11 -> x15, Pallas kernels: 44.2 us -> 43.6 us  [call(): pl.pallas_call(kernel, out_shape=outs, in_specs=in_specs, out_specs=out_s...]
  transfers between devices with their start and end apart: 19 -> 26, of which waited for: 12 -> 12; matrix products, arithmetic and copies ran while one was open for 1% -> 3% of each run, Pallas kernels for 18% -> 33%
where the time goes in v1:
time: 118 us; the launch traced here: 116 us
  Pallas kernels  50.6 us (43%)
  waiting for transfers between devices  29.7 us (25%)
  starting transfers between devices  27.8 us (24%)
  local copies, waits for them, and re-layouts  2.91 us (2%)
  other arithmetic  2.62 us (2%)
  between operations  2.52 us (2%)
    pallas_call x15, Pallas kernels, call(): pl.pallas_call(kernel, out_shape=outs, in_specs=in_specs, out_specs=out_s...  43.6 us
    ppermute x19, waiting for transfers between devices, to_dp(): return lax.ppermute(value, 'dp', pairs)  24.5 us
    ppermute x19, starting transfers between devices, to_dp(): return lax.ppermute(value, 'dp', pairs)  19.5 us
    pallas_call x2, Pallas kernels, update_state(): pl.pallas_call(functools.partial(update_kernel, kinds, is_mine), out_shap...  7.03 us
    ppermute x6, starting transfers between devices, over_tensor(): lax.ppermute(value, 'tensor', [(i, (i + s) % ranks) for i in range(ranks)])  7.02 us
    ppermute x6, waiting for transfers between devices, over_tensor(): lax.ppermute(value, 'tensor', [(i, (i + s) % ranks) for i in range(ranks)])  5.18 us
  transfers between devices with their start and end apart: 26, of which 12 were waited for; matrix products, arithmetic and copies ran while one was open for 3% of the time, Pallas kernels for 33%

profile of v1, /device:TPU:1, one launch (start us, length us, event | category | flops | bytes accessed | tf_op | source)
XLA Modules:
  0.0 116.1 jit_solution(17575112835056576581)
XLA Ops:
  1.5 1.7 %first_rows.1 = bf16[1,32,64,128]{3,2,1,0:T(8,128)(2,1)S(1)} custom-call(s32[4]{0:T(128)S(1)} %add_add_fusion.1.ids_ref, s32[1,32]{1,0:T(1,128)S(1)} %copy-done.8, bf16[8,32,64,128]{3,2,1,0:T(8,128)(2,1)} %refs_0_.5), custom_call_target="tpu_custom_call" | custom-call | tf_op jit(solution)/shard_map/first_rows/pallas_call | solution.py:73
  3.2 2.7 %collective-permute-start.3 = (bf16[1,32,64,128]{3,2,1,0:T(8,128)(2,1)S(1)}, bf16[1,32,64,128]{3,2,1,0:T(8,128)(2,1)S(1)}, u32[]{:S(2)}, u32[]{:S(2)}) collective-permute-start(bf16[1,32,64,128]{3,2,1,0:T(8,128)(2,1)S(1)} %first_rows.1), channel_id=1, source_target_pairs={{0,8},{4,12},{8,0},{12,4},{1,9},{5,13},{9,1},{13,5},{2,10},{6,14},... | collective-permute-start | bytes 1572872 | tf_op jit(solution)/shard_map/ppermute | solution.py:843
  5.9 3.7 %in_load.1 = (bf16[64,4096]{1,0:T(8,128)(2,1)S(1)}, bf16[32,128]{1,0:T(8,128)(2,1)S(1)}, bf16[8,2048,2,128]{3,2,1,0:T(2,128)(2,1)S(1)}) custom-call(bf16[32,2048]{1,0:T(8,128)(2,1)} %bitcast.41, f32[2,2048]{1,0:T(2,128)} %gain_ref.1, bf16[32,2048]{1,0:T(8,128)(2,1)} %bitcast.52, bf16[2048,16,2,128]{3,2,1,0:T(2,128)(2,1)} %bitcast.49), custom_call_target="tpu_custom_call" | custom-call | bytes 16777216 | tf_op jit(solution)/shard_map/in_load/pallas_call | solution.py:73
  9.6 4.4 %in_middle.1 = (bf16[64,1024]{1,0:T(8,128)(2,1)S(1)}, bf16[8,2048,2,128]{3,2,1,0:T(2,128)(2,1)S(1)}, bf16[2,2048,2,128]{3,2,1,0:T(2,128)(2,1)S(1)}) custom-call(bf16[64,4096]{1,0:T(8,128)(2,1)S(1)} %get-tuple-element.73.lhs_ref, bf16[8,4096,128]{2,1,0:T(8,128)(2,1)S(1)} %bitcast.39, bf16[2048,16,2,128]{3,2,1,0:T(2,128)(2,1)} %bitcast.50, ...), custom_call_target="tpu_custom_call" | custom-call | tf_op jit(solution)/shard_map/in_middle/pallas_call | solution.py:73
  14.2 1.9 %in_last.1.own_ref = bf16[32,4736]{1,0:T(8,128)(2,1)S(1)} custom-call(bf16[64,4096]{1,0:T(8,128)(2,1)S(1)} %get-tuple-element.73.lhs_ref, bf16[64,1024]{1,0:T(8,128)(2,1)S(1)} %get-tuple-element.75.early_ref, bf16[32,128]{1,0:T(8,128)(2,1)S(1)} %get-tuple-element.76.tail_ref, bf16[8,4096,128]{2,1,0:T(8,128)(2,1)S(1)} %bitcast.38, ...), custom_call_target="tpu_custom_call" | custom-call | tf_op jit(solution)/shard_map/in_last/pallas_call | solution.py:73
  20.3 1.3 %collective-permute-start.5 = (bf16[16,4736]{1,0:T(8,128)(2,1)S(1)}, bf16[16,4736]{1,0:T(8,128)(2,1)S(1)}, u32[]{:S(2)}, u32[]{:S(2)}) collective-permute-start(bf16[16,4736]{1,0:T(8,128)(2,1)S(1)} %get-tuple-element.85), channel_id=1, source_target_pairs={{0,8},{4,12},{8,0},{12,4},{1,9},{5,13},{9,1},{13,5},{2,10},{6,14},... | collective-permute-start | bytes 454664 | tf_op jit(solution)/shard_map/ppermute | solution.py:843
  21.9 2.7 %gather_rows.3 = (bf16[1,32,64,128]{3,2,1,0:T(8,128)(2,1)S(1)}, bf16[1,32,64,128]{3,2,1,0:T(8,128)(2,1)S(1)}, bf16[1,32,64,128]{3,2,1,0:T(8,128)(2,1)}) custom-call(s32[3]{0:T(128)S(1)} %slice.10.table_ref, bf16[8,32,64,128]{3,2,1,0:T(8,128)(2,1)} %refs_0_.5, bf16[8,32,64,128]{3,2,1,0:T(8,128)(2,1)} %collective-permute-done.4.refs_1_), custom_call_target="tpu_custom_call" | custom-call | tf_op jit(solution)/shard_map/gather_rows/pallas_call | solution.py:73
  25.2 4.1 %mixer.1 = (bf16[16,2048]{1,0:T(8,128)(2,1)S(1)}, bf16[16,10240]{1,0:T(8,128)(2,1)S(1)}) custom-call(s32[4]{0:T(128)S(1)} %add_add_fusion.ids_ref, s32[1,32]{1,0:T(1,128)S(1)} %copy-done.9, bf16[16,4736]{1,0:T(8,128)(2,1)S(1)} %get-tuple-element.84.refs_0_, bf16[16,4736]{1,0:T(8,128)(2,1)S(1)} %collective-permute-done.5.refs_1_, f32[4,2048]{1,0:T(4,128)S(1)} %copy-done.7, ...), custom_call_target="tpu_custom_call" | custom-call | tf_op jit(solution)/shard_map/mixer/pallas_call | solution.py:73
  29.3 1.6 %collective-permute-start.6 = (bf16[1,32,64,128]{3,2,1,0:T(8,128)(2,1)S(1)}, bf16[1,32,64,128]{3,2,1,0:T(8,128)(2,1)S(1)}, u32[]{:S(2)}, u32[]{:S(2)}) collective-permute-start(bf16[1,32,64,128]{3,2,1,0:T(8,128)(2,1)S(1)} %collective-permute-done.3.refs_2_), channel_id=1, source_target_pairs={{0,4},{4,0},{8,12},{12,8},{1,5},{5,1},{9,13},{13,9},{2,6},{6,2},{1... | collective-permute-start | bytes 1572872 | tf_op jit(solution)/shard_map/ppermute | solution.py:843
  30.9 1.2 %collective-permute-start.9 = (bf16[16,2048]{1,0:T(8,128)(2,1)S(1)}, bf16[16,2048]{1,0:T(8,128)(2,1)S(1)}, u32[]{:S(2)}, u32[]{:S(2)}) collective-permute-start(bf16[16,2048]{1,0:T(8,128)(2,1)S(1)} %get-tuple-element.89.refs_0_), channel_id=1, source_target_pairs={{0,12},{4,8},{8,4},{12,0},{1,13},{5,9},{9,5},{13,1},{2,14},{6,10},... | collective-permute-start | bytes 196616 | tf_op jit(solution)/shard_map/ppermute | solution.py:843
  33.1 1.8 %collective-permute-done.9.refs_3_ = bf16[16,2048]{1,0:T(8,128)(2,1)S(1)} collective-permute-done((bf16[16,2048]{1,0:T(8,128)(2,1)S(1)}, bf16[16,2048]{1,0:T(8,128)(2,1)S(1)}, u32[]{:S(2)}, u32[]{:S(2)}) %collective-permute-start.9) | collective-permute-done | bytes 65568 | tf_op jit(solution)/shard_map/ppermute | solution.py:843
  35.4 1.7 %collective-permute-start.10 = (bf16[1,32,64,128]{3,2,1,0:T(8,128)(2,1)S(1)}, bf16[1,32,64,128]{3,2,1,0:T(8,128)(2,1)S(1)}, u32[]{:S(2)}, u32[]{:S(2)}) collective-permute-start(bf16[1,32,64,128]{3,2,1,0:T(8,128)(2,1)S(1)} %get-tuple-element.90), channel_id=1, source_target_pairs={{0,8},{4,12},{8,0},{12,4},{1,9},{5,13},{9,1},{13,5},{2,10},{6,14},... | collective-permute-start | bytes 1572872 | tf_op jit(solution)/shard_map/ppermute | solution.py:843
  37.1 4.7 %out_proj.1.refs_0_ = bf16[32,2048]{1,0:T(8,128)(2,1)S(1)} custom-call(s32[4]{0:T(128)S(1)} %add_add_fusion.ids_ref, s32[1,32]{1,0:T(1,128)S(1)} %copy-done.9, bf16[16,2048]{1,0:T(8,128)(2,1)S(1)} %get-tuple-element.89.refs_0_, bf16[16,2048]{1,0:T(8,128)(2,1)S(1)} %collective-permute-done.7.refs_1_, bf16[16,2048]{1,0:T(8,128)(2,1)S(1)} %collective-permute-done.8.refs_2_, ...), custom_call_target="tpu_custom_call" | custom-call | tf_op jit(solution)/shard_map/out_proj/pallas_call | solution.py:73
  41.9 3.4 %collective-permute-start.13 = (bf16[32,2048]{1,0:T(8,128)(2,1)S(1)}, bf16[32,2048]{1,0:T(8,128)(2,1)S(1)}, u32[]{:S(2)}, u32[]{:S(2)}) collective-permute-start(bf16[32,2048]{1,0:T(8,128)(2,1)S(1)} %out_proj.1.refs_0_), channel_id=1, source_target_pairs={{0,3},{1,0},{2,1},{3,2},{4,7},{5,4},{6,5},{7,6},{8,11},{9,8},{10,9... | collective-permute-start | bytes 393224 | tf_op jit(solution)/shard_map/ppermute | solution.py:847
  45.7 5.8 %prefetch.1.refs_4_ = bf16[2048,4096]{1,0:T(8,128)(2,1)S(1)} custom-call(bf16[2048,4096]{1,0:T(8,128)(2,1)} %from_ref), custom_call_target="tpu_custom_call" | custom-call | bytes 33554432 | tf_op jit(solution)/shard_map/prefetch/pallas_call | solution.py:73
  52.3 4.3 %collective-permute-done.12.refs_2_ = bf16[32,2048]{1,0:T(8,128)(2,1)S(1)} collective-permute-done((bf16[32,2048]{1,0:T(8,128)(2,1)S(1)}, bf16[32,2048]{1,0:T(8,128)(2,1)S(1)}, u32[]{:S(2)}, u32[]{:S(2)}) %collective-permute-start.12) | collective-permute-done | bytes 131104 | tf_op jit(solution)/shard_map/ppermute | solution.py:847
  56.6 3.0 %up_proj.1 = (f32[32,2048]{1,0:T(8,128)S(1)}, bf16[32,4224]{1,0:T(8,128)(2,1)S(1)}) custom-call(bf16[32,2048]{1,0:T(8,128)(2,1)S(1)} %bitcast.42, f32[2,2048]{1,0:T(2,128)S(1)} %copy-done.6, bf16[32,2048]{1,0:T(8,128)(2,1)S(1)} %out_proj.1.refs_0_, bf16[32,2048]{1,0:T(8,128)(2,1)S(1)} %collective-permute-done.11.refs_1_, ...), custom_call_target="tpu_custom_call" | custom-call | tf_op jit(solution)/shard_map/up_proj/pallas_call | solution.py:73
  59.6 1.5 %collective-permute-start.14 = (bf16[32,4224]{1,0:T(8,128)(2,1)S(1)}, bf16[32,4224]{1,0:T(8,128)(2,1)S(1)}, u32[]{:S(2)}, u32[]{:S(2)}) collective-permute-start(bf16[32,4224]{1,0:T(8,128)(2,1)S(1)} %get-tuple-element.100.own_ref), channel_id=1, source_target_pairs={{0,4},{4,0},{8,12},{12,8},{1,5},{5,1},{9,13},{13,9},{2,6},{6,2},{1... | collective-permute-start | bytes 811016 | tf_op jit(solution)/shard_map/ppermute | solution.py:843
  63.0 1.2 %collective-permute-start.19 = (bf16[32,4224]{1,0:T(8,128)(2,1)S(1)}, bf16[32,4224]{1,0:T(8,128)(2,1)S(1)}, u32[]{:S(2)}, u32[]{:S(2)}) collective-permute-start(bf16[32,4224]{1,0:T(8,128)(2,1)S(1)} %chip_sum.1.refs_0_), channel_id=1, source_target_pairs={{0,8},{4,12},{8,0},{12,4},{1,9},{5,13},{9,1},{13,5},{2,10},{6,14},... | collective-permute-start | bytes 811016 | tf_op jit(solution)/shard_map/ppermute | solution.py:843
  65.1 5.5 %collective-permute-done.19.refs_1_ = bf16[32,4224]{1,0:T(8,128)(2,1)S(1)} collective-permute-done((bf16[32,4224]{1,0:T(8,128)(2,1)S(1)}, bf16[32,4224]{1,0:T(8,128)(2,1)S(1)}, u32[]{:S(2)}, u32[]{:S(2)}) %collective-permute-start.19) | collective-permute-done | bytes 270368 | tf_op jit(solution)/shard_map/ppermute | solution.py:843
  70.7 6.4 %down_proj.1.refs_0_ = bf16[32,2048]{1,0:T(8,128)(2,1)S(1)} custom-call(bf16[32,4224]{1,0:T(8,128)(2,1)S(1)} %chip_sum.1.refs_0_, bf16[32,4224]{1,0:T(8,128)(2,1)S(1)} %collective-permute-done.19.refs_1_, bf16[4096,2048]{1,0:T(8,128)(2,1)} %refs_2_.3), custom_call_target="tpu_custom_call" | custom-call | tf_op jit(solution)/shard_map/down_proj/pallas_call | solution.py:73
  77.1 1.3 %collective-permute-start.25 = (bf16[1,32,64,128]{3,2,1,0:T(8,128)(2,1)}, bf16[1,32,64,128]{3,2,1,0:T(8,128)(2,1)S(1)}, u32[]{:S(2)}, u32[]{:S(2)}) collective-permute-start(bf16[1,32,64,128]{3,2,1,0:T(8,128)(2,1)} %get-tuple-element.123), channel_id=1, source_target_pairs={{0,8},{4,12},{8,0},{12,4},{1,9},{5,13},{9,1},{13,5},{2,10},{6,14},... | collective-permute-start | bytes 1572872 | tf_op jit(solution)/shard_map/ppermute | solution.py:843
  78.6 1.8 %collective-permute-start.18 = (bf16[4,10240]{1,0:T(4,128)(2,1)S(1)}, bf16[4,10240]{1,0:T(4,128)(2,1)S(1)}, u32[]{:S(2)}, u32[]{:S(2)}) collective-permute-start(bf16[4,10240]{1,0:T(4,128)(2,1)S(1)} %get-tuple-element.113), channel_id=1, source_target_pairs={{0,4},{4,0},{8,12},{12,8},{1,5},{5,1},{9,13},{13,9},{2,6},{6,2},{1... | collective-permute-start | bytes 245768 | tf_op jit(solution)/shard_map/ppermute | solution.py:843
  80.4 12.7 %collective-permute-done.20.refs_2_ = bf16[8,10240]{1,0:T(8,128)(2,1)S(1)} collective-permute-done((bf16[8,10240]{1,0:T(8,128)(2,1)S(1)}, bf16[8,10240]{1,0:T(8,128)(2,1)S(1)}, u32[]{:S(2)}, u32[]{:S(2)}) %collective-permute-start.20) | collective-permute-done | bytes 163872 | tf_op jit(solution)/shard_map/ppermute | solution.py:843
  93.1 2.1 %collective-permute-start.21 = (bf16[8,10240]{1,0:T(8,128)(2,1)S(1)}, bf16[8,10240]{1,0:T(8,128)(2,1)S(1)}, u32[]{:S(2)}, u32[]{:S(2)}) collective-permute-start(bf16[8,10240]{1,0:T(8,128)(2,1)S(1)} %collective-permute-done.20.refs_2_), channel_id=1, source_target_pairs={{0,4},{4,0},{8,12},{12,8},{1,5},{5,1},{9,13},{13,9},{2,6},{6,2},{1... | collective-permute-start | bytes 491528 | tf_op jit(solution)/shard_map/ppermute | solution.py:843
  95.2 1.7 %collective-permute-start.24 = (bf16[32,2048]{1,0:T(8,128)(2,1)S(1)}, bf16[32,2048]{1,0:T(8,128)(2,1)}, u32[]{:S(2)}, u32[]{:S(2)}) collective-permute-start(bf16[32,2048]{1,0:T(8,128)(2,1)S(1)} %down_proj.1.refs_0_), channel_id=1, source_target_pairs={{0,3},{1,0},{2,1},{3,2},{4,7},{5,4},{6,5},{7,6},{8,11},{9,8},{10,9... | collective-permute-start | bytes 393224 | tf_op jit(solution)/shard_map/ppermute | solution.py:847
  97.0 1.5 %collective-permute-start.22 = (bf16[32,2048]{1,0:T(8,128)(2,1)S(1)}, bf16[32,2048]{1,0:T(8,128)(2,1)}, u32[]{:S(2)}, u32[]{:S(2)}) collective-permute-start(bf16[32,2048]{1,0:T(8,128)(2,1)S(1)} %down_proj.1.refs_0_), channel_id=1, source_target_pairs={{0,1},{1,2},{2,3},{3,0},{4,5},{5,6},{6,7},{7,4},{8,9},{9,10},{10,1... | collective-permute-start | bytes 393224 | tf_op jit(solution)/shard_map/ppermute | solution.py:847
  98.4 1.7 %collect.1 = (bf16[3,8,2048]{2,1,0:T(8,128)(2,1)}, bf16[8,3,2,256]{3,2,1,0:T(2,128)(2,1)}, f32[8,2048]{1,0:T(8,128)S(1)}, f32[8,256]{1,0:T(8,128)S(1)}, f32[8,128]{1,0:T(8,128)S(1)}) custom-call(s32[4]{0:T(128)S(1)} %add_add_fusion.ids_ref, s32[1,32]{1,0:T(1,128)S(1)} %copy-done.9, bf16[4,10240]{1,0:T(4,128)(2,1)S(1)} %get-tuple-element.111.refs_0_, ...), custom_call_target="tpu_custom_call" | custom-call | tf_op jit(solution)/shard_map/collect/pallas_call | solution.py:73
  100.2 1.2 %collective-permute-start.26 = (s32[32]{0:T(128)S(1)}, s32[32]{0:T(128)S(1)}, u32[]{:S(2)}, u32[]{:S(2)}) collective-permute-start(s32[32]{0:T(128)S(1)} %bitcast.47), channel_id=1, source_target_pairs={{0,16},{16,0},{1,17},{17,1},{2,18},{18,2},{3,19},{19,3},{4,20},{20... | collective-permute-start | bytes 392 | tf_op jit(solution)/shard_map/ppermute | solution.py:971
  102.5 5.9 %update_state.2.refs_8_ = bf16[8,32,64,128]{3,2,1,0:T(8,128)(2,1)} custom-call(s32[8]{0:T(128)S(1)} %multiply_add_fusion.table_ref, bf16[8,32,64,128]{3,2,1,0:T(8,128)(2,1)} %refs_0_.5, bf16[8,32,64,128]{3,2,1,0:T(8,128)(2,1)} %collective-permute-done.4.refs_1_, bf16[1,32,64,128]{3,2,1,0:T(8,128)(2,1)S(1)} %collective-permute-done.3.refs_2_, ...), custom_call_target="tpu_custom_call" | custom-call | tf_op jit(solution)/shard_map/update_state/pallas_call | solution.py:625
  109.2 1.8 %finish.1 = bf16[1,32,2048]{2,1,0:T(8,128)(2,1)} custom-call(f32[32,2048]{1,0:T(8,128)S(1)} %copy-done.4, bf16[32,2048]{1,0:T(8,128)(2,1)S(1)} %down_proj.1.refs_0_, bf16[32,2048]{1,0:T(8,128)(2,1)} %collective-permute-done.22.refs_1_, bf16[32,2048]{1,0:T(8,128)(2,1)} %collective-permute-done.23.refs_2_, bf16[32,2048]{1,0:T(8,128)(2,1)} %collective-permute-done.24.refs_3_), custom_call_target="tpu_custom_call" | custom-call | tf_op jit(solution)/shard_map/finish/pallas_call | solution.py:73
  114.8 1.2 %update_state.3 = bf16[8,32,64,128]{3,2,1,0:T(8,128)(2,1)} custom-call(s32[8]{0:T(128)S(1)} %multiply_add_fusion.table_ref, bf16[8,32,64,128]{3,2,1,0:T(8,128)(2,1)} %refs_0_.5, bf16[1,32,64,128]{3,2,1,0:T(8,128)(2,1)S(1)} %collective-permute-done.25.refs_1_, bf16[4,32,64,128]{3,2,1,0:T(8,128)(2,1)} %get-tuple-element.125.refs_2_, ...), custom_call_target="tpu_custom_call", output_to_operand_aliasing={{}: (9, {})} | custom-call | tf_op jit(solution)/shard_map/update_state/pallas_call | solution.py:625
  (116 shorter events, 16.2 us)
Async XLA Ops:
  0.6 21.3 %collective-permute-start.4 = (bf16[8,32,64,128]{3,2,1,0:T(8,128)(2,1)}, bf16[8,32,64,128]{3,2,1,0:T(8,128)(2,1)}, u32[]{:S(2)}, u32[]{:S(2)}) collective-permute-start(bf16[8,32,64,128]{3,2,1,0:T(8,128)(2,1)} %refs_0_.5), channel_id=1, source_target_pairs={{0,4},{4,0},{8,12},{12,8},{1,5},{5,1},{9,13},{13,9},{2,6},{6,2},{1... | collective-permute-start | bytes 12582920 | tf_op jit(solution)/shard_map/ppermute | solution.py:843
  3.2 14.9 %collective-permute-start.3 = (bf16[1,32,64,128]{3,2,1,0:T(8,128)(2,1)S(1)}, bf16[1,32,64,128]{3,2,1,0:T(8,128)(2,1)S(1)}, u32[]{:S(2)}, u32[]{:S(2)}) collective-permute-start(bf16[1,32,64,128]{3,2,1,0:T(8,128)(2,1)S(1)} %first_rows.1), channel_id=1, source_target_pairs={{0,8},{4,12},{8,0},{12,4},{1,9},{5,13},{9,1},{13,5},{2,10},{6,14},... | collective-permute-start | bytes 1572872 | tf_op jit(solution)/shard_map/ppermute | solution.py:843
  16.0 1.7 %collective-permute-start.2 = (bf16[32,4736]{1,0:T(8,128)(2,1)S(1)}, bf16[32,4736]{1,0:T(8,128)(2,1)S(1)}, u32[]{:S(2)}, u32[]{:S(2)}) collective-permute-start(bf16[32,4736]{1,0:T(8,128)(2,1)S(1)} %in_last.1.own_ref), channel_id=1, source_target_pairs={{0,4},{4,0},{8,12},{12,8},{1,5},{5,1},{9,13},{13,9},{2,6},{6,2},{1... | collective-permute-start | bytes 909320 | tf_op jit(solution)/shard_map/ppermute | solution.py:843
  20.3 4.8 %collective-permute-start.5 = (bf16[16,4736]{1,0:T(8,128)(2,1)S(1)}, bf16[16,4736]{1,0:T(8,128)(2,1)S(1)}, u32[]{:S(2)}, u32[]{:S(2)}) collective-permute-start(bf16[16,4736]{1,0:T(8,128)(2,1)S(1)} %get-tuple-element.85), channel_id=1, source_target_pairs={{0,8},{4,12},{8,0},{12,4},{1,9},{5,13},{9,1},{13,5},{2,10},{6,14},... | collective-permute-start | bytes 454664 | tf_op jit(solution)/shard_map/ppermute | solution.py:843
  21.9 3.3 %copy-start.5 = (bf16[8,3,2048]{2,0,1:T(8,128)(2,1)S(1)}, bf16[8,3,2048]{2,0,1:T(8,128)(2,1)}, u32[]{:S(2)}) copy-start(bf16[8,3,2048]{2,0,1:T(8,128)(2,1)} %param.36) | copy-start | bytes 294916
  29.3 3.7 %collective-permute-start.6 = (bf16[1,32,64,128]{3,2,1,0:T(8,128)(2,1)S(1)}, bf16[1,32,64,128]{3,2,1,0:T(8,128)(2,1)S(1)}, u32[]{:S(2)}, u32[]{:S(2)}) collective-permute-start(bf16[1,32,64,128]{3,2,1,0:T(8,128)(2,1)S(1)} %collective-permute-done.3.refs_2_), channel_id=1, source_target_pairs={{0,4},{4,0},{8,12},{12,8},{1,5},{5,1},{9,13},{13,9},{2,6},{6,2},{1... | collective-permute-start | bytes 1572872 | tf_op jit(solution)/shard_map/ppermute | solution.py:843
  30.9 4.0 %collective-permute-start.9 = (bf16[16,2048]{1,0:T(8,128)(2,1)S(1)}, bf16[16,2048]{1,0:T(8,128)(2,1)S(1)}, u32[]{:S(2)}, u32[]{:S(2)}) collective-permute-start(bf16[16,2048]{1,0:T(8,128)(2,1)S(1)} %get-tuple-element.89.refs_0_), channel_id=1, source_target_pairs={{0,12},{4,8},{8,4},{12,0},{1,13},{5,9},{9,5},{13,1},{2,14},{6,10},... | collective-permute-start | bytes 196616 | tf_op jit(solution)/shard_map/ppermute | solution.py:843
  32.1 3.2 %collective-permute-start.8 = (bf16[16,2048]{1,0:T(8,128)(2,1)S(1)}, bf16[16,2048]{1,0:T(8,128)(2,1)S(1)}, u32[]{:S(2)}, u32[]{:S(2)}) collective-permute-start(bf16[16,2048]{1,0:T(8,128)(2,1)S(1)} %get-tuple-element.89.refs_0_), channel_id=1, source_target_pairs={{0,8},{4,12},{8,0},{12,4},{1,9},{5,13},{9,1},{13,5},{2,10},{6,14},... | collective-permute-start | bytes 196616 | tf_op jit(solution)/shard_map/ppermute | solution.py:843
  32.3 3.1 %collective-permute-start.7 = (bf16[16,2048]{1,0:T(8,128)(2,1)S(1)}, bf16[16,2048]{1,0:T(8,128)(2,1)S(1)}, u32[]{:S(2)}, u32[]{:S(2)}) collective-permute-start(bf16[16,2048]{1,0:T(8,128)(2,1)S(1)} %get-tuple-element.89.refs_0_), channel_id=1, source_target_pairs={{0,4},{4,0},{8,12},{12,8},{1,5},{5,1},{9,13},{13,9},{2,6},{6,2},{1... | collective-permute-start | bytes 196616 | tf_op jit(solution)/shard_map/ppermute | solution.py:843
  35.4 16.9 %collective-permute-start.10 = (bf16[1,32,64,128]{3,2,1,0:T(8,128)(2,1)S(1)}, bf16[1,32,64,128]{3,2,1,0:T(8,128)(2,1)S(1)}, u32[]{:S(2)}, u32[]{:S(2)}) collective-permute-start(bf16[1,32,64,128]{3,2,1,0:T(8,128)(2,1)S(1)} %get-tuple-element.90), channel_id=1, source_target_pairs={{0,8},{4,12},{8,0},{12,4},{1,9},{5,13},{9,1},{13,5},{2,10},{6,14},... | collective-permute-start | bytes 1572872 | tf_op jit(solution)/shard_map/ppermute | solution.py:843
  41.8 14.8 %copy-start = (bf16[1,32,2048]{2,1,0:T(8,128)(2,1)S(1)}, bf16[1,32,2048]{2,1,0:T(8,128)(2,1)}, u32[]{:S(2)}) copy-start(bf16[1,32,2048]{2,1,0:T(8,128)(2,1)} %param.20) | copy-start | bytes 393220
  41.8 14.8 %copy-start.6 = (f32[2,2048]{1,0:T(2,128)S(1)}, f32[2,2048]{1,0:T(2,128)}, u32[]{:S(2)}) copy-start(f32[2,2048]{1,0:T(2,128)} %gain_ref.1) | copy-start | bytes 49156
  41.8 19.3 %collective-permute-start.15 = (bf16[1,32,64,128]{3,2,1,0:T(8,128)(2,1)S(1)}, bf16[1,32,64,128]{3,2,1,0:T(8,128)(2,1)S(1)}, u32[]{:S(2)}, u32[]{:S(2)}) collective-permute-start(bf16[1,32,64,128]{3,2,1,0:T(8,128)(2,1)S(1)} %get-tuple-element.102), channel_id=1, source_target_pairs={{0,8},{4,12},{8,0},{12,4},{1,9},{5,13},{9,1},{13,5},{2,10},{6,14},... | collective-permute-start | bytes 1572872 | tf_op jit(solution)/shard_map/ppermute | solution.py:843
  41.9 10.4 %collective-permute-start.13 = (bf16[32,2048]{1,0:T(8,128)(2,1)S(1)}, bf16[32,2048]{1,0:T(8,128)(2,1)S(1)}, u32[]{:S(2)}, u32[]{:S(2)}) collective-permute-start(bf16[32,2048]{1,0:T(8,128)(2,1)S(1)} %out_proj.1.refs_0_), channel_id=1, source_target_pairs={{0,3},{1,0},{2,1},{3,2},{4,7},{5,4},{6,5},{7,6},{8,11},{9,8},{10,9... | collective-permute-start | bytes 393224 | tf_op jit(solution)/shard_map/ppermute | solution.py:847
  45.3 11.3 %collective-permute-start.12 = (bf16[32,2048]{1,0:T(8,128)(2,1)S(1)}, bf16[32,2048]{1,0:T(8,128)(2,1)S(1)}, u32[]{:S(2)}, u32[]{:S(2)}) collective-permute-start(bf16[32,2048]{1,0:T(8,128)(2,1)S(1)} %out_proj.1.refs_0_), channel_id=1, source_target_pairs={{0,2},{1,3},{2,0},{3,1},{4,6},{5,7},{6,4},{7,5},{8,10},{9,11},{10,... | collective-permute-start | bytes 393224 | tf_op jit(solution)/shard_map/ppermute | solution.py:847
  45.3 11.3 %collective-permute-start.11 = (bf16[32,2048]{1,0:T(8,128)(2,1)S(1)}, bf16[32,2048]{1,0:T(8,128)(2,1)S(1)}, u32[]{:S(2)}, u32[]{:S(2)}) collective-permute-start(bf16[32,2048]{1,0:T(8,128)(2,1)S(1)} %out_proj.1.refs_0_), channel_id=1, source_target_pairs={{0,1},{1,2},{2,3},{3,0},{4,5},{5,6},{6,7},{7,4},{8,9},{9,10},{10,1... | collective-permute-start | bytes 393224 | tf_op jit(solution)/shard_map/ppermute | solution.py:847
  59.6 17.5 %copy-start.3 = (f32[32,2048]{1,0:T(8,128)}, f32[32,2048]{1,0:T(8,128)S(1)}, u32[]{:S(2)}) copy-start(f32[32,2048]{1,0:T(8,128)S(1)} %get-tuple-element.121.residual_ref) | copy-start | bytes 786436
  59.6 2.7 %collective-permute-start.14 = (bf16[32,4224]{1,0:T(8,128)(2,1)S(1)}, bf16[32,4224]{1,0:T(8,128)(2,1)S(1)}, u32[]{:S(2)}, u32[]{:S(2)}) collective-permute-start(bf16[32,4224]{1,0:T(8,128)(2,1)S(1)} %get-tuple-element.100.own_ref), channel_id=1, source_target_pairs={{0,4},{4,0},{8,12},{12,8},{1,5},{5,1},{9,13},{13,9},{2,6},{6,2},{1... | collective-permute-start | bytes 811016 | tf_op jit(solution)/shard_map/ppermute | solution.py:843
  62.4 2.0 %collective-permute-start.16 = (bf16[1,32,64,128]{3,2,1,0:T(8,128)(2,1)S(1)}, bf16[1,32,64,128]{3,2,1,0:T(8,128)(2,1)S(1)}, u32[]{:S(2)}, u32[]{:S(2)}) collective-permute-start(bf16[1,32,64,128]{3,2,1,0:T(8,128)(2,1)S(1)} %collective-permute-done.10.refs_3_), channel_id=1, source_target_pairs={{0,4},{4,0},{8,12},{12,8},{1,5},{5,1},{9,13},{13,9},{2,6},{6,2},{1... | collective-permute-start | bytes 1572872 | tf_op jit(solution)/shard_map/ppermute | solution.py:843
  62.8 2.3 %collective-permute-start.17 = (bf16[1,32,64,128]{3,2,1,0:T(8,128)(2,1)S(1)}, bf16[1,32,64,128]{3,2,1,0:T(8,128)(2,1)S(1)}, u32[]{:S(2)}, u32[]{:S(2)}) collective-permute-start(bf16[1,32,64,128]{3,2,1,0:T(8,128)(2,1)S(1)} %collective-permute-done.15.refs_4_), channel_id=1, source_target_pairs={{0,4},{4,0},{8,12},{12,8},{1,5},{5,1},{9,13},{13,9},{2,6},{6,2},{1... | collective-permute-start | bytes 1572872 | tf_op jit(solution)/shard_map/ppermute | solution.py:843
  63.0 7.7 %collective-permute-start.19 = (bf16[32,4224]{1,0:T(8,128)(2,1)S(1)}, bf16[32,4224]{1,0:T(8,128)(2,1)S(1)}, u32[]{:S(2)}, u32[]{:S(2)}) collective-permute-start(bf16[32,4224]{1,0:T(8,128)(2,1)S(1)} %chip_sum.1.refs_0_), channel_id=1, source_target_pairs={{0,8},{4,12},{8,0},{12,4},{1,9},{5,13},{9,1},{13,5},{2,10},{6,14},... | collective-permute-start | bytes 811016 | tf_op jit(solution)/shard_map/ppermute | solution.py:843
  65.1 12.0 %copy-start.1 = (bf16[1,32,64,128]{3,2,1,0:T(8,128)(2,1)}, bf16[1,32,64,128]{3,2,1,0:T(8,128)(2,1)S(1)}, u32[]{:S(2)}) copy-start(bf16[1,32,64,128]{3,2,1,0:T(8,128)(2,1)S(1)} %collective-permute-done.17.refs_7_) | copy-start | bytes 1572868
  77.1 33.9 %collective-permute-start.25 = (bf16[1,32,64,128]{3,2,1,0:T(8,128)(2,1)}, bf16[1,32,64,128]{3,2,1,0:T(8,128)(2,1)S(1)}, u32[]{:S(2)}, u32[]{:S(2)}) collective-permute-start(bf16[1,32,64,128]{3,2,1,0:T(8,128)(2,1)} %get-tuple-element.123), channel_id=1, source_target_pairs={{0,8},{4,12},{8,0},{12,4},{1,9},{5,13},{9,1},{13,5},{2,10},{6,14},... | collective-permute-start | bytes 1572872 | tf_op jit(solution)/shard_map/ppermute | solution.py:843
  78.4 14.7 %collective-permute-start.20 = (bf16[8,10240]{1,0:T(8,128)(2,1)S(1)}, bf16[8,10240]{1,0:T(8,128)(2,1)S(1)}, u32[]{:S(2)}, u32[]{:S(2)}) collective-permute-start(bf16[8,10240]{1,0:T(8,128)(2,1)S(1)} %get-tuple-element.116), channel_id=1, source_target_pairs={{0,8},{4,12},{8,0},{12,4},{1,9},{5,13},{9,1},{13,5},{2,10},{6,14},... | collective-permute-start | bytes 491528 | tf_op jit(solution)/shard_map/ppermute | solution.py:843
  78.6 18.3 %collective-permute-start.18 = (bf16[4,10240]{1,0:T(4,128)(2,1)S(1)}, bf16[4,10240]{1,0:T(4,128)(2,1)S(1)}, u32[]{:S(2)}, u32[]{:S(2)}) collective-permute-start(bf16[4,10240]{1,0:T(4,128)(2,1)S(1)} %get-tuple-element.113), channel_id=1, source_target_pairs={{0,4},{4,0},{8,12},{12,8},{1,5},{5,1},{9,13},{13,9},{2,6},{6,2},{1... | collective-permute-start | bytes 245768 | tf_op jit(solution)/shard_map/ppermute | solution.py:843
  93.1 5.3 %collective-permute-start.21 = (bf16[8,10240]{1,0:T(8,128)(2,1)S(1)}, bf16[8,10240]{1,0:T(8,128)(2,1)S(1)}, u32[]{:S(2)}, u32[]{:S(2)}) collective-permute-start(bf16[8,10240]{1,0:T(8,128)(2,1)S(1)} %collective-permute-done.20.refs_2_), channel_id=1, source_target_pairs={{0,4},{4,0},{8,12},{12,8},{1,5},{5,1},{9,13},{13,9},{2,6},{6,2},{1... | collective-permute-start | bytes 491528 | tf_op jit(solution)/shard_map/ppermute | solution.py:843
  95.2 13.1 %collective-permute-start.24 = (bf16[32,2048]{1,0:T(8,128)(2,1)S(1)}, bf16[32,2048]{1,0:T(8,128)(2,1)}, u32[]{:S(2)}, u32[]{:S(2)}) collective-permute-start(bf16[32,2048]{1,0:T(8,128)(2,1)S(1)} %down_proj.1.refs_0_), channel_id=1, source_target_pairs={{0,3},{1,0},{2,1},{3,2},{4,7},{5,4},{6,5},{7,6},{8,11},{9,8},{10,9... | collective-permute-start | bytes 393224 | tf_op jit(solution)/shard_map/ppermute | solution.py:847
  96.9 12.3 %collective-permute-start.23 = (bf16[32,2048]{1,0:T(8,128)(2,1)S(1)}, bf16[32,2048]{1,0:T(8,128)(2,1)}, u32[]{:S(2)}, u32[]{:S(2)}) collective-permute-start(bf16[32,2048]{1,0:T(8,128)(2,1)S(1)} %down_proj.1.refs_0_), channel_id=1, source_target_pairs={{0,2},{1,3},{2,0},{3,1},{4,6},{5,7},{6,4},{7,5},{8,10},{9,11},{10,... | collective-permute-start | bytes 393224 | tf_op jit(solution)/shard_map/ppermute | solution.py:847
  97.0 12.2 %collective-permute-start.22 = (bf16[32,2048]{1,0:T(8,128)(2,1)S(1)}, bf16[32,2048]{1,0:T(8,128)(2,1)}, u32[]{:S(2)}, u32[]{:S(2)}) collective-permute-start(bf16[32,2048]{1,0:T(8,128)(2,1)S(1)} %down_proj.1.refs_0_), channel_id=1, source_target_pairs={{0,1},{1,2},{2,3},{3,0},{4,5},{5,6},{6,7},{7,4},{8,9},{9,10},{10,1... | collective-permute-start | bytes 393224 | tf_op jit(solution)/shard_map/ppermute | solution.py:847
  100.2 12.0 %collective-permute-start.26 = (s32[32]{0:T(128)S(1)}, s32[32]{0:T(128)S(1)}, u32[]{:S(2)}, u32[]{:S(2)}) collective-permute-start(s32[32]{0:T(128)S(1)} %bitcast.47), channel_id=1, source_target_pairs={{0,16},{16,0},{1,17},{17,1},{2,18},{18,2},{3,19},{19,3},{4,20},{20... | collective-permute-start | bytes 392 | tf_op jit(solution)/shard_map/ppermute | solution.py:971
  102.5 6.7 %copy-start.4 = (f32[32,2048]{1,0:T(8,128)S(1)}, f32[32,2048]{1,0:T(8,128)}, u32[]{:S(2)}) copy-start(f32[32,2048]{1,0:T(8,128)} %copy-done.3) | copy-start | bytes 786436
  111.0 3.8 %collective-permute-start.27 = (bf16[1,32,64,128]{3,2,1,0:T(8,128)(2,1)S(1)}, bf16[1,32,64,128]{3,2,1,0:T(8,128)(2,1)S(1)}, u32[]{:S(2)}, u32[]{:S(2)}) collective-permute-start(bf16[1,32,64,128]{3,2,1,0:T(8,128)(2,1)S(1)} %collective-permute-done.25.refs_1_), channel_id=1, source_target_pairs={{0,4},{4,0},{8,12},{12,8},{1,5},{5,1},{9,13},{13,9},{2,6},{6,2},{1... | collective-permute-start | bytes 1572872 | tf_op jit(solution)/shard_map/ppermute | solution.py:843
  (10 other events, 23.8 us)

commit v2 on v1

--- a/solution.py
+++ b/solution.py
@@ -866,7 +866,8 @@
     near = to_dp(partial, 0, 1)
     most = min(2 * local_rows, 4 * capacity)
     turns = 1 + (max(min(most, local_rows) - 1, most - 2) + 1) // 2
-    early = (turns + 1) // 2
+    early = min(turns, max(3, (turns + 2) // 2))
+    single = min(3, early)
     near, *first = barrier((near, *first))
     picked = pick_rows(targets[0::2], partial, near, parents, local_rows, capacity, slots)
     needed, lane, turn = plan_rows(after(chosen, picked[0]), chips, local_rows)
@@ -887,7 +888,7 @@
         turn_of = jnp.sum(jnp.where(lookup, turn[chip].reshape(1, rows), 0), axis=1)
         hop_of = (chip + chips - parent_chip) % chips
         here = ((own_chosen // local_rows) % 2) ^ core
-        start_of = jnp.minimum(turn_of, early)
+        start_of = jnp.where(turn_of >= early, early, jnp.minimum(turn_of, single))
         there = 2 + ((hop_of - 1) * 2 + (lane_of ^ core)) * turns + start_of
         inside = jnp.where(parent_chip == chip, own_chosen % local_rows, turn_of - start_of)
         return (jnp.where(parent_chip == chip, here, there) * local_rows + inside).astype(jnp.int32)
@@ -898,9 +899,10 @@
     parts = [picked[0]] + [to_dp(picked[hop], hop, 0) for hop in range(1, chips)]
 
     waiting = []
+    sizes = [1] * (single - 1) + [early - single] * (early > single)
     for hop in range(1, chips):
         wanted = after(send_tables[hop - 1][1:early], picked[0])
-        waiting.append(gather_rows(wanted, [ssm_state, sibling_state], [1] * (early - 1)))
+        waiting.append(gather_rows(wanted, [ssm_state, sibling_state], sizes))
     table = where_from()
     parts[0] = after(parts[0], table, *[some[0] for some in waiting])
     act, message = mixer(
@@ -929,60 +931,58 @@
     out_part = out_proj(sources, parents, local_rows, capacity, acts, weight_out)
     arrived[1] = send_turn(1, *acts)
     out_parts = over_tensor(out_part)
-    for at in range(2, early - 1):
+    for at in range(2, single):
         arrived[at] = send_turn(at, out_part)
     weight_up = prefetch(weight_up, out_part)
     dealt = deal(targets, after(message, weight_up), capacity)
     out_parts[0], arrived[1], *dealt = barrier((out_parts[0], arrived[1], *dealt))
     residual, up_part = up_proj(tokens[0], norm_gains, out_parts, weight_up)
-    last = early - 1
-    between = {at: arrived[at] for at in range(2, last)}
-    near_up, between = barrier((to_dp(up_part, 0, 1), between))
+    sent = [to_dp(dealt[1 + hop], hop, 0) for hop in range(1, chips)]
+    between = {at: arrived[at] for at in range(2, single)}
+    near_up, between, sent = barrier((to_dp(up_part, 0, 1), between, sent))
     arrived.update(between)
     up_chip = chip_sum(up_part, near_up)
     up_parts = [up_chip] + [to_dp(up_chip, hop, 0) for hop in range(1, chips)]
 
-    for at in range(1, last):
+    for at in range(1, single):
         relay(at, up_chip)
     messages = [dealt[0], to_dp(after(dealt[1], up_chip), 0, 1)]
-    up_parts[0], relayed = barrier((up_parts[0], relayed))
-    sent = [to_dp(after(dealt[1 + hop], *up_parts), hop, 0) for hop in range(1, chips)]
+    for some in sent:
+        messages += [some, to_dp(after(some, up_chip), 0, 1)]
+    final_inner, final_groups, update, keys, decay = collect(
+        sources, parents, local_rows, messages, slots, inner, groups_width, lags
+    )
+    up_parts[0], relayed, update = barrier((up_parts[0], relayed, update))
+    if early > single:
+        arrived[single] = send_turn(single, *up_parts)
     down_part = down_proj(up_parts, weight_down)
     down_parts = over_tensor(down_part)
-    if last > 1:
-        arrived[last] = send_turn(last, down_part)
-
-    for some in sent:
-        messages += [some, to_dp(after(some, down_part), 0, 1)]
-    final_inner, final_groups, update, keys, decay = collect(
-        sources, parents, local_rows, messages, slots, inner, groups_width, lags
-    )
 
     def is_early(kind):
-        return (kind < 2) | (lax.rem(kind - 2, turns) < last)
+        return (kind < 2) | (lax.rem(kind - 2, turns) < single)
 
     def is_late(kind):
         return jnp.logical_not(is_early(kind))
 
-    chosen = after(chosen, update)
+    def add_states(turn_range):
+        for at in turn_range:
+            for hop in range(1, chips):
+                states[kind_of(hop, at)] = arrived[at][hop - 1]
+                states[kind_of(hop, at) + turns] = relayed[at][hop - 1]
+
+    add_states(range(single))
+    final_state = update_state(table, states, update, keys, decay, is_early)
+    chosen = after(chosen, final_state)
     groups = lax.axis_size("groups")
     longest = rounds_of(chosen, chips, local_rows)
     for shift in range(1, groups):
         other = lax.ppermute(chosen, "groups", [(i, (i + shift) % groups) for i in range(groups)])
         longest = jnp.maximum(longest, rounds_of(other, chips, local_rows))
-
-    def add_states(turn_range):
-        for at in turn_range:
-            for hop in range(1, chips):
-                states[kind_of(hop, at)] = arrived[at][hop - 1]
-                states[kind_of(hop, at) + turns] = relayed[at][hop - 1]
-
-    add_states(range(last))
-    final_state = update_state(table, states, update, keys, decay, is_early)
-    residual, final_state = barrier((residual, final_state))
+    residual, final_state, longest = barrier((residual, final_state, longest))
     beam_out = finish(residual, down_parts)
-    relay(last, beam_out)
-    add_states([last])
+    if early > single:
+        relay(single, beam_out)
+        add_states([single])
 
     more = (turns - early, *ssm_state.shape[1:])
 
@@ -995,13 +995,17 @@
             fetched.append(to_dp(fetched[-1], 0, 1))
         return tuple(fetched)
 
-    fetched = lax.cond(longest > early, fetch_more, lambda: tuple(no_rows(more, 2 * (chips - 1))))
+    fetched = []
+    if turns > early:
+        fetched = lax.cond(longest > early, fetch_more, lambda: tuple(no_rows(more, 2 * (chips - 1))))
     late_states = {0: ssm_state}
     for hop in range(1, chips):
-        for lane_kind, buffer in ((kind_of(hop, early), fetched[2 * hop - 2]), (kind_of(hop, early) + turns, fetched[2 * hop - 1])):
-            late_states[lane_kind] = buffer
-        for lane_kind in (kind_of(hop, last), kind_of(hop, last) + turns):
-            late_states[lane_kind] = states[lane_kind]
+        if turns > early:
+            late_states[kind_of(hop, early)] = fetched[2 * hop - 2]
+            late_states[kind_of(hop, early) + turns] = fetched[2 * hop - 1]
+        if early > single:
+            for kind in (kind_of(hop, single), kind_of(hop, single) + turns):
+                late_states[kind] = states[kind]
     final_state = update_state(table, late_states, update, keys, decay, is_late, final_state)
     return (beam_out, final_state, final_inner.transpose(1, 0, 2), final_groups)
 

time: 118 us -> 107 us (0.907); the launches traced: 116 us -> 107 us
  waiting for transfers between devices: 29.7 us -> 21.5 us
    ppermute x19, waiting for transfers between devices: 24.5 us -> 16.5 us  [to_dp(): return lax.ppermute(value, 'dp', pairs)]
    pallas_call x15, Pallas kernels: 43.6 us -> 41.9 us  [call(): pl.pallas_call(kernel, out_shape=outs, in_specs=in_specs, out_specs=out_s...]
  transfers between devices with their start and end apart: 26 -> 26, of which waited for: 12 -> 12; matrix products, arithmetic and copies ran while one was open for 3% -> 3% of each run, Pallas kernels for 33% -> 40%
where the time goes in v2:
time: 107 us
  Pallas kernels  49.5 us (46%)
  starting transfers between devices  28.7 us (27%)
  waiting for transfers between devices  21.5 us (20%)
  other arithmetic  2.56 us (2%)
  between operations  2.44 us (2%)
  local copies, waits for them, and re-layouts  1.85 us (2%)
    pallas_call x15, Pallas kernels, call(): pl.pallas_call(kernel, out_shape=outs, in_specs=in_specs, out_specs=out_s...  41.9 us
    ppermute x19, starting transfers between devices, to_dp(): return lax.ppermute(value, 'dp', pairs)  19.7 us
    ppermute x19, waiting for transfers between devices, to_dp(): return lax.ppermute(value, 'dp', pairs)  16.5 us
    pallas_call x2, Pallas kernels, update_state(): pl.pallas_call(functools.partial(update_kernel, kinds, is_mine), out_shap...  7.6 us
    ppermute x6, starting transfers between devices, over_tensor(): lax.ppermute(value, 'tensor', [(i, (i + s) % ranks) for i in range(ranks)])  7.29 us
    ppermute x6, waiting for transfers between devices, over_tensor(): lax.ppermute(value, 'tensor', [(i, (i + s) % ranks) for i in range(ranks)])  4.32 us
  transfers between devices with their start and end apart: 26, of which 12 were waited for; matrix products, arithmetic and copies ran while one was open for 3% of the time, Pallas kernels for 40%

profile of v2, /device:TPU:1, one launch (start us, length us, event | category | flops | bytes accessed | tf_op | source)
XLA Modules:
  0.0 106.6 jit_solution(4178069237410283526)
XLA Ops:
  1.5 1.7 %first_rows.1 = bf16[1,32,64,128]{3,2,1,0:T(8,128)(2,1)S(1)} custom-call(s32[4]{0:T(128)S(1)} %add_add_fusion.1.ids_ref, s32[1,32]{1,0:T(1,128)S(1)} %copy-done.4, bf16[8,32,64,128]{3,2,1,0:T(8,128)(2,1)} %refs_0_.5), custom_call_target="tpu_custom_call" | custom-call | tf_op jit(solution)/shard_map/first_rows/pallas_call | solution.py:73
  3.2 2.7 %collective-permute-start.3 = (bf16[1,32,64,128]{3,2,1,0:T(8,128)(2,1)S(1)}, bf16[1,32,64,128]{3,2,1,0:T(8,128)(2,1)S(1)}, u32[]{:S(2)}, u32[]{:S(2)}) collective-permute-start(bf16[1,32,64,128]{3,2,1,0:T(8,128)(2,1)S(1)} %first_rows.1), channel_id=1, source_target_pairs={{0,8},{4,12},{8,0},{12,4},{1,9},{5,13},{9,1},{13,5},{2,10},{6,14},... | collective-permute-start | bytes 1572872 | tf_op jit(solution)/shard_map/ppermute | solution.py:843
  5.9 3.7 %in_load.1 = (bf16[64,4096]{1,0:T(8,128)(2,1)S(1)}, bf16[32,128]{1,0:T(8,128)(2,1)S(1)}, bf16[8,2048,2,128]{3,2,1,0:T(2,128)(2,1)S(1)}) custom-call(bf16[32,2048]{1,0:T(8,128)(2,1)} %bitcast.41, f32[2,2048]{1,0:T(2,128)} %gain_ref.1, bf16[32,2048]{1,0:T(8,128)(2,1)} %bitcast.52, bf16[2048,16,2,128]{3,2,1,0:T(2,128)(2,1)} %bitcast.49), custom_call_target="tpu_custom_call" | custom-call | bytes 16777216 | tf_op jit(solution)/shard_map/in_load/pallas_call | solution.py:73
  9.6 4.4 %in_middle.1 = (bf16[64,1024]{1,0:T(8,128)(2,1)S(1)}, bf16[8,2048,2,128]{3,2,1,0:T(2,128)(2,1)S(1)}, bf16[2,2048,2,128]{3,2,1,0:T(2,128)(2,1)S(1)}) custom-call(bf16[64,4096]{1,0:T(8,128)(2,1)S(1)} %get-tuple-element.75.lhs_ref, bf16[8,4096,128]{2,1,0:T(8,128)(2,1)S(1)} %bitcast.39, bf16[2048,16,2,128]{3,2,1,0:T(2,128)(2,1)} %bitcast.50, ...), custom_call_target="tpu_custom_call" | custom-call | tf_op jit(solution)/shard_map/in_middle/pallas_call | solution.py:73
  14.2 1.9 %in_last.1.own_ref = bf16[32,4736]{1,0:T(8,128)(2,1)S(1)} custom-call(bf16[64,4096]{1,0:T(8,128)(2,1)S(1)} %get-tuple-element.75.lhs_ref, bf16[64,1024]{1,0:T(8,128)(2,1)S(1)} %get-tuple-element.77.early_ref, bf16[32,128]{1,0:T(8,128)(2,1)S(1)} %get-tuple-element.78.tail_ref, bf16[8,4096,128]{2,1,0:T(8,128)(2,1)S(1)} %bitcast.38, ...), custom_call_target="tpu_custom_call" | custom-call | tf_op jit(solution)/shard_map/in_last/pallas_call | solution.py:73
  20.3 1.3 %collective-permute-start.5 = (bf16[16,4736]{1,0:T(8,128)(2,1)S(1)}, bf16[16,4736]{1,0:T(8,128)(2,1)S(1)}, u32[]{:S(2)}, u32[]{:S(2)}) collective-permute-start(bf16[16,4736]{1,0:T(8,128)(2,1)S(1)} %get-tuple-element.87), channel_id=1, source_target_pairs={{0,8},{4,12},{8,0},{12,4},{1,9},{5,13},{9,1},{13,5},{2,10},{6,14},... | collective-permute-start | bytes 454664 | tf_op jit(solution)/shard_map/ppermute | solution.py:843
  21.9 2.1 %gather_rows.3 = (bf16[1,32,64,128]{3,2,1,0:T(8,128)(2,1)S(1)}, bf16[1,32,64,128]{3,2,1,0:T(8,128)(2,1)S(1)}, bf16[2,32,64,128]{3,2,1,0:T(8,128)(2,1)S(1)}) custom-call(s32[4]{0:T(128)S(1)} %slice.10.table_ref, bf16[8,32,64,128]{3,2,1,0:T(8,128)(2,1)} %refs_0_.5, bf16[8,32,64,128]{3,2,1,0:T(8,128)(2,1)} %collective-permute-done.4.refs_1_), custom_call_target="tpu_custom_call" | custom-call | tf_op jit(solution)/shard_map/gather_rows/pallas_call | solution.py:73
  25.1 4.1 %mixer.1 = (bf16[16,2048]{1,0:T(8,128)(2,1)S(1)}, bf16[16,10240]{1,0:T(8,128)(2,1)S(1)}) custom-call(s32[4]{0:T(128)S(1)} %add_add_fusion.ids_ref, s32[1,32]{1,0:T(1,128)S(1)} %copy-done.5, bf16[16,4736]{1,0:T(8,128)(2,1)S(1)} %get-tuple-element.86.refs_0_, bf16[16,4736]{1,0:T(8,128)(2,1)S(1)} %collective-permute-done.5.refs_1_, f32[4,2048]{1,0:T(4,128)S(1)} %copy-done.3, ...), custom_call_target="tpu_custom_call" | custom-call | tf_op jit(solution)/shard_map/mixer/pallas_call | solution.py:73
  29.3 1.6 %collective-permute-start.6 = (bf16[1,32,64,128]{3,2,1,0:T(8,128)(2,1)S(1)}, bf16[1,32,64,128]{3,2,1,0:T(8,128)(2,1)S(1)}, u32[]{:S(2)}, u32[]{:S(2)}) collective-permute-start(bf16[1,32,64,128]{3,2,1,0:T(8,128)(2,1)S(1)} %collective-permute-done.3.refs_2_), channel_id=1, source_target_pairs={{0,4},{4,0},{8,12},{12,8},{1,5},{5,1},{9,13},{13,9},{2,6},{6,2},{1... | collective-permute-start | bytes 1572872 | tf_op jit(solution)/shard_map/ppermute | solution.py:843
  30.9 1.2 %collective-permute-start.9 = (bf16[16,2048]{1,0:T(8,128)(2,1)S(1)}, bf16[16,2048]{1,0:T(8,128)(2,1)S(1)}, u32[]{:S(2)}, u32[]{:S(2)}) collective-permute-start(bf16[16,2048]{1,0:T(8,128)(2,1)S(1)} %get-tuple-element.91.refs_0_), channel_id=1, source_target_pairs={{0,12},{4,8},{8,4},{12,0},{1,13},{5,9},{9,5},{13,1},{2,14},{6,10},... | collective-permute-start | bytes 196616 | tf_op jit(solution)/shard_map/ppermute | solution.py:843
  33.1 1.8 %collective-permute-done.9.refs_3_ = bf16[16,2048]{1,0:T(8,128)(2,1)S(1)} collective-permute-done((bf16[16,2048]{1,0:T(8,128)(2,1)S(1)}, bf16[16,2048]{1,0:T(8,128)(2,1)S(1)}, u32[]{:S(2)}, u32[]{:S(2)}) %collective-permute-start.9) | collective-permute-done | bytes 65568 | tf_op jit(solution)/shard_map/ppermute | solution.py:843
  35.4 1.7 %collective-permute-start.10 = (bf16[1,32,64,128]{3,2,1,0:T(8,128)(2,1)S(1)}, bf16[1,32,64,128]{3,2,1,0:T(8,128)(2,1)S(1)}, u32[]{:S(2)}, u32[]{:S(2)}) collective-permute-start(bf16[1,32,64,128]{3,2,1,0:T(8,128)(2,1)S(1)} %get-tuple-element.92), channel_id=1, source_target_pairs={{0,8},{4,12},{8,0},{12,4},{1,9},{5,13},{9,1},{13,5},{2,10},{6,14},... | collective-permute-start | bytes 1572872 | tf_op jit(solution)/shard_map/ppermute | solution.py:843
  37.1 4.7 %out_proj.1.refs_0_ = bf16[32,2048]{1,0:T(8,128)(2,1)S(1)} custom-call(s32[4]{0:T(128)S(1)} %add_add_fusion.ids_ref, s32[1,32]{1,0:T(1,128)S(1)} %copy-done.5, bf16[16,2048]{1,0:T(8,128)(2,1)S(1)} %get-tuple-element.91.refs_0_, bf16[16,2048]{1,0:T(8,128)(2,1)S(1)} %collective-permute-done.7.refs_1_, bf16[16,2048]{1,0:T(8,128)(2,1)S(1)} %collective-permute-done.8.refs_2_, ...), custom_call_target="tpu_custom_call" | custom-call | tf_op jit(solution)/shard_map/out_proj/pallas_call | solution.py:73
  41.9 3.4 %collective-permute-start.13 = (bf16[32,2048]{1,0:T(8,128)(2,1)S(1)}, bf16[32,2048]{1,0:T(8,128)(2,1)S(1)}, u32[]{:S(2)}, u32[]{:S(2)}) collective-permute-start(bf16[32,2048]{1,0:T(8,128)(2,1)S(1)} %out_proj.1.refs_0_), channel_id=1, source_target_pairs={{0,3},{1,0},{2,1},{3,2},{4,7},{5,4},{6,5},{7,6},{8,11},{9,8},{10,9... | collective-permute-start | bytes 393224 | tf_op jit(solution)/shard_map/ppermute | solution.py:847
  45.7 5.8 %prefetch.1.refs_4_ = bf16[2048,4096]{1,0:T(8,128)(2,1)S(1)} custom-call(bf16[2048,4096]{1,0:T(8,128)(2,1)} %from_ref), custom_call_target="tpu_custom_call" | custom-call | bytes 33554432 | tf_op jit(solution)/shard_map/prefetch/pallas_call | solution.py:73
  52.3 4.3 %collective-permute-done.12.refs_2_ = bf16[32,2048]{1,0:T(8,128)(2,1)S(1)} collective-permute-done((bf16[32,2048]{1,0:T(8,128)(2,1)S(1)}, bf16[32,2048]{1,0:T(8,128)(2,1)S(1)}, u32[]{:S(2)}, u32[]{:S(2)}) %collective-permute-start.12) | collective-permute-done | bytes 131104 | tf_op jit(solution)/shard_map/ppermute | solution.py:847
  56.6 3.0 %up_proj.1 = (f32[32,2048]{1,0:T(8,128)S(1)}, bf16[32,4224]{1,0:T(8,128)(2,1)S(1)}) custom-call(bf16[32,2048]{1,0:T(8,128)(2,1)S(1)} %bitcast.42, f32[2,2048]{1,0:T(2,128)S(1)} %copy-done.2, bf16[32,2048]{1,0:T(8,128)(2,1)S(1)} %out_proj.1.refs_0_, bf16[32,2048]{1,0:T(8,128)(2,1)S(1)} %collective-permute-done.11.refs_1_, ...), custom_call_target="tpu_custom_call" | custom-call | tf_op jit(solution)/shard_map/up_proj/pallas_call | solution.py:73
  59.6 1.5 %collective-permute-start.14 = (bf16[32,4224]{1,0:T(8,128)(2,1)S(1)}, bf16[32,4224]{1,0:T(8,128)(2,1)S(1)}, u32[]{:S(2)}, u32[]{:S(2)}) collective-permute-start(bf16[32,4224]{1,0:T(8,128)(2,1)S(1)} %get-tuple-element.102.own_ref), channel_id=1, source_target_pairs={{0,4},{4,0},{8,12},{12,8},{1,5},{5,1},{9,13},{13,9},{2,6},{6,2},{1... | collective-permute-start | bytes 811016 | tf_op jit(solution)/shard_map/ppermute | solution.py:843
  61.1 1.2 %collective-permute-start.16 = (bf16[8,10240]{1,0:T(8,128)(2,1)S(1)}, bf16[8,10240]{1,0:T(8,128)(2,1)S(1)}, u32[]{:S(2)}, u32[]{:S(2)}) collective-permute-start(bf16[8,10240]{1,0:T(8,128)(2,1)S(1)} %get-tuple-element.105), channel_id=1, source_target_pairs={{0,8},{4,12},{8,0},{12,4},{1,9},{5,13},{9,1},{13,5},{2,10},{6,14},... | collective-permute-start | bytes 491528 | tf_op jit(solution)/shard_map/ppermute | solution.py:843
  62.3 4.6 %collective-permute-done.16.refs_2_ = bf16[8,10240]{1,0:T(8,128)(2,1)S(1)} collective-permute-done((bf16[8,10240]{1,0:T(8,128)(2,1)S(1)}, bf16[8,10240]{1,0:T(8,128)(2,1)S(1)}, u32[]{:S(2)}, u32[]{:S(2)}) %collective-permute-start.16) | collective-permute-done | bytes 163872 | tf_op jit(solution)/shard_map/ppermute | solution.py:843
  68.0 1.2 %collective-permute-start.22 = (bf16[32,4224]{1,0:T(8,128)(2,1)S(1)}, bf16[32,4224]{1,0:T(8,128)(2,1)S(1)}, u32[]{:S(2)}, u32[]{:S(2)}) collective-permute-start(bf16[32,4224]{1,0:T(8,128)(2,1)S(1)} %chip_sum.1.refs_0_), channel_id=1, source_target_pairs={{0,8},{4,12},{8,0},{12,4},{1,9},{5,13},{9,1},{13,5},{2,10},{6,14},... | collective-permute-start | bytes 811016 | tf_op jit(solution)/shard_map/ppermute | solution.py:843
  69.9 1.3 %collective-permute-done.19.refs_1_ = bf16[4,10240]{1,0:T(4,128)(2,1)S(1)} collective-permute-done((bf16[4,10240]{1,0:T(4,128)(2,1)S(1)}, bf16[4,10240]{1,0:T(4,128)(2,1)S(1)}, u32[]{:S(2)}, u32[]{:S(2)}) %collective-permute-start.19) | collective-permute-done | bytes 81952 | tf_op jit(solution)/shard_map/ppermute | solution.py:843
  71.2 1.7 %collect.1 = (bf16[3,8,2048]{2,1,0:T(8,128)(2,1)}, bf16[8,3,2,256]{3,2,1,0:T(2,128)(2,1)}, f32[8,2048]{1,0:T(8,128)S(1)}, f32[8,256]{1,0:T(8,128)S(1)}, f32[8,128]{1,0:T(8,128)S(1)}) custom-call(s32[4]{0:T(128)S(1)} %add_add_fusion.ids_ref, s32[1,32]{1,0:T(1,128)S(1)} %copy-done.5, bf16[4,10240]{1,0:T(4,128)(2,1)S(1)} %get-tuple-element.111.refs_0_, ...), custom_call_target="tpu_custom_call" | custom-call | tf_op jit(solution)/shard_map/collect/pallas_call | solution.py:73
  72.8 2.8 %collective-permute-done.22.refs_1_ = bf16[32,4224]{1,0:T(8,128)(2,1)S(1)} collective-permute-done((bf16[32,4224]{1,0:T(8,128)(2,1)S(1)}, bf16[32,4224]{1,0:T(8,128)(2,1)S(1)}, u32[]{:S(2)}, u32[]{:S(2)}) %collective-permute-start.22) | collective-permute-done | bytes 270368 | tf_op jit(solution)/shard_map/ppermute | solution.py:843
  75.6 1.2 %collective-permute-start.26 = (bf16[2,32,64,128]{3,2,1,0:T(8,128)(2,1)S(1)}, bf16[2,32,64,128]{3,2,1,0:T(8,128)(2,1)S(1)}, u32[]{:S(2)}, u32[]{:S(2)}) collective-permute-start(bf16[2,32,64,128]{3,2,1,0:T(8,128)(2,1)S(1)} %get-tuple-element.127), channel_id=1, source_target_pairs={{0,8},{4,12},{8,0},{12,4},{1,9},{5,13},{9,1},{13,5},{2,10},{6,14},... | collective-permute-start | bytes 3145736 | tf_op jit(solution)/shard_map/ppermute | solution.py:843
  76.8 6.4 %down_proj.1.refs_0_ = bf16[32,2048]{1,0:T(8,128)(2,1)S(1)} custom-call(bf16[32,4224]{1,0:T(8,128)(2,1)S(1)} %chip_sum.1.refs_0_, bf16[32,4224]{1,0:T(8,128)(2,1)S(1)} %collective-permute-done.22.refs_1_, bf16[4096,2048]{1,0:T(8,128)(2,1)} %refs_2_.3), custom_call_target="tpu_custom_call" | custom-call | tf_op jit(solution)/shard_map/down_proj/pallas_call | solution.py:73
  85.3 1.4 %collective-permute-start.23 = (bf16[32,2048]{1,0:T(8,128)(2,1)S(1)}, bf16[32,2048]{1,0:T(8,128)(2,1)S(1)}, u32[]{:S(2)}, u32[]{:S(2)}) collective-permute-start(bf16[32,2048]{1,0:T(8,128)(2,1)S(1)} %down_proj.1.refs_0_), channel_id=1, source_target_pairs={{0,1},{1,2},{2,3},{3,0},{4,5},{5,6},{6,7},{7,4},{8,9},{9,10},{10,1... | collective-permute-start | bytes 393224 | tf_op jit(solution)/shard_map/ppermute | solution.py:847
  86.6 5.2 %update_state.2.refs_8_ = bf16[8,32,64,128]{3,2,1,0:T(8,128)(2,1)} custom-call(s32[8]{0:T(128)S(1)} %fusion.9.table_ref, bf16[8,32,64,128]{3,2,1,0:T(8,128)(2,1)} %refs_0_.5, bf16[8,32,64,128]{3,2,1,0:T(8,128)(2,1)} %collective-permute-done.4.refs_1_, bf16[1,32,64,128]{3,2,1,0:T(8,128)(2,1)S(1)} %collective-permute-done.3.refs_2_, ...), custom_call_target="tpu_custom_call" | custom-call | tf_op jit(solution)/shard_map/update_state/pallas_call | solution.py:625
  91.9 1.7 %collective-permute-start.21 = (s32[32]{0:T(128)S(1)}, s32[32]{0:T(128)S(1)}, u32[]{:S(2)}, u32[]{:S(2)}) collective-permute-start(s32[32]{0:T(128)S(1)} %bitcast.47), channel_id=1, source_target_pairs={{0,16},{16,0},{1,17},{17,1},{2,18},{18,2},{3,19},{19,3},{4,20},{20... | collective-permute-start | bytes 392 | tf_op jit(solution)/shard_map/ppermute | solution.py:979
  99.0 2.8 %collective-permute-start.27 = (bf16[2,32,64,128]{3,2,1,0:T(8,128)(2,1)S(1)}, bf16[2,32,64,128]{3,2,1,0:T(8,128)(2,1)S(1)}, u32[]{:S(2)}, u32[]{:S(2)}) collective-permute-start(bf16[2,32,64,128]{3,2,1,0:T(8,128)(2,1)S(1)} %collective-permute-done.26.refs_1_), channel_id=1, source_target_pairs={{0,4},{4,0},{8,12},{12,8},{1,5},{5,1},{9,13},{13,9},{2,6},{6,2},{1... | collective-permute-start | bytes 3145736 | tf_op jit(solution)/shard_map/ppermute | solution.py:843
  101.8 2.3 %collective-permute-done.27.refs_3_ = bf16[2,32,64,128]{3,2,1,0:T(8,128)(2,1)S(1)} collective-permute-done((bf16[2,32,64,128]{3,2,1,0:T(8,128)(2,1)S(1)}, bf16[2,32,64,128]{3,2,1,0:T(8,128)(2,1)S(1)}, u32[]{:S(2)}, u32[]{:S(2)}) %collective-permute-start.27) | collective-permute-done | bytes 1048608 | tf_op jit(solution)/shard_map/ppermute | solution.py:843
  104.0 2.4 %update_state.3 = bf16[8,32,64,128]{3,2,1,0:T(8,128)(2,1)} custom-call(s32[8]{0:T(128)S(1)} %fusion.9.table_ref, bf16[8,32,64,128]{3,2,1,0:T(8,128)(2,1)} %refs_0_.5, bf16[2,32,64,128]{3,2,1,0:T(8,128)(2,1)S(1)} %collective-permute-done.26.refs_1_, bf16[3,32,64,128]{3,2,1,0:T(8,128)(2,1)} %get-tuple-element.129.refs_2_, ...), custom_call_target="tpu_custom_call", output_to_operand_aliasing={{}: (9, {})} | custom-call | tf_op jit(solution)/shard_map/update_state/pallas_call | solution.py:625
  (108 shorter events, 17.1 us)
Async XLA Ops:
  0.6 21.3 %collective-permute-start.4 = (bf16[8,32,64,128]{3,2,1,0:T(8,128)(2,1)}, bf16[8,32,64,128]{3,2,1,0:T(8,128)(2,1)}, u32[]{:S(2)}, u32[]{:S(2)}) collective-permute-start(bf16[8,32,64,128]{3,2,1,0:T(8,128)(2,1)} %refs_0_.5), channel_id=1, source_target_pairs={{0,4},{4,0},{8,12},{12,8},{1,5},{5,1},{9,13},{13,9},{2,6},{6,2},{1... | collective-permute-start | bytes 12582920 | tf_op jit(solution)/shard_map/ppermute | solution.py:843
  3.2 14.9 %collective-permute-start.3 = (bf16[1,32,64,128]{3,2,1,0:T(8,128)(2,1)S(1)}, bf16[1,32,64,128]{3,2,1,0:T(8,128)(2,1)S(1)}, u32[]{:S(2)}, u32[]{:S(2)}) collective-permute-start(bf16[1,32,64,128]{3,2,1,0:T(8,128)(2,1)S(1)} %first_rows.1), channel_id=1, source_target_pairs={{0,8},{4,12},{8,0},{12,4},{1,9},{5,13},{9,1},{13,5},{2,10},{6,14},... | collective-permute-start | bytes 1572872 | tf_op jit(solution)/shard_map/ppermute | solution.py:843
  16.1 1.7 %collective-permute-start.2 = (bf16[32,4736]{1,0:T(8,128)(2,1)S(1)}, bf16[32,4736]{1,0:T(8,128)(2,1)S(1)}, u32[]{:S(2)}, u32[]{:S(2)}) collective-permute-start(bf16[32,4736]{1,0:T(8,128)(2,1)S(1)} %in_last.1.own_ref), channel_id=1, source_target_pairs={{0,4},{4,0},{8,12},{12,8},{1,5},{5,1},{9,13},{13,9},{2,6},{6,2},{1... | collective-permute-start | bytes 909320 | tf_op jit(solution)/shard_map/ppermute | solution.py:843
  20.3 4.8 %collective-permute-start.5 = (bf16[16,4736]{1,0:T(8,128)(2,1)S(1)}, bf16[16,4736]{1,0:T(8,128)(2,1)S(1)}, u32[]{:S(2)}, u32[]{:S(2)}) collective-permute-start(bf16[16,4736]{1,0:T(8,128)(2,1)S(1)} %get-tuple-element.87), channel_id=1, source_target_pairs={{0,8},{4,12},{8,0},{12,4},{1,9},{5,13},{9,1},{13,5},{2,10},{6,14},... | collective-permute-start | bytes 454664 | tf_op jit(solution)/shard_map/ppermute | solution.py:843
  21.9 3.3 %copy-start.1 = (bf16[8,3,2048]{2,0,1:T(8,128)(2,1)S(1)}, bf16[8,3,2048]{2,0,1:T(8,128)(2,1)}, u32[]{:S(2)}) copy-start(bf16[8,3,2048]{2,0,1:T(8,128)(2,1)} %param.36) | copy-start | bytes 294916
  21.9 3.2 %copy-start.3 = (f32[4,2048]{1,0:T(4,128)S(1)}, f32[4,2048]{1,0:T(4,128)}, u32[]{:S(2)}) copy-start(f32[4,2048]{1,0:T(4,128)} %refs_2_.2) | copy-start | bytes 98308
  21.9 3.2 %copy-start.6 = (f32[4,2,256]{2,1,0:T(2,128)S(1)}, f32[4,2,256]{2,1,0:T(2,128)}, u32[]{:S(2)}) copy-start(f32[4,2,256]{2,1,0:T(2,128)} %refs_3_.1) | copy-start | bytes 24580
  21.9 3.2 %copy-start.7 = (f32[2048]{0:T(1024)S(1)}, f32[2048]{0:T(1024)}, u32[]{:S(2)}) copy-start(f32[2048]{0:T(1024)} %param.31) | copy-start | bytes 24580
  29.3 3.8 %collective-permute-start.6 = (bf16[1,32,64,128]{3,2,1,0:T(8,128)(2,1)S(1)}, bf16[1,32,64,128]{3,2,1,0:T(8,128)(2,1)S(1)}, u32[]{:S(2)}, u32[]{:S(2)}) collective-permute-start(bf16[1,32,64,128]{3,2,1,0:T(8,128)(2,1)S(1)} %collective-permute-done.3.refs_2_), channel_id=1, source_target_pairs={{0,4},{4,0},{8,12},{12,8},{1,5},{5,1},{9,13},{13,9},{2,6},{6,2},{1... | collective-permute-start | bytes 1572872 | tf_op jit(solution)/shard_map/ppermute | solution.py:843
  30.9 4.0 %collective-permute-start.9 = (bf16[16,2048]{1,0:T(8,128)(2,1)S(1)}, bf16[16,2048]{1,0:T(8,128)(2,1)S(1)}, u32[]{:S(2)}, u32[]{:S(2)}) collective-permute-start(bf16[16,2048]{1,0:T(8,128)(2,1)S(1)} %get-tuple-element.91.refs_0_), channel_id=1, source_target_pairs={{0,12},{4,8},{8,4},{12,0},{1,13},{5,9},{9,5},{13,1},{2,14},{6,10},... | collective-permute-start | bytes 196616 | tf_op jit(solution)/shard_map/ppermute | solution.py:843
  32.1 3.2 %collective-permute-start.8 = (bf16[16,2048]{1,0:T(8,128)(2,1)S(1)}, bf16[16,2048]{1,0:T(8,128)(2,1)S(1)}, u32[]{:S(2)}, u32[]{:S(2)}) collective-permute-start(bf16[16,2048]{1,0:T(8,128)(2,1)S(1)} %get-tuple-element.91.refs_0_), channel_id=1, source_target_pairs={{0,8},{4,12},{8,0},{12,4},{1,9},{5,13},{9,1},{13,5},{2,10},{6,14},... | collective-permute-start | bytes 196616 | tf_op jit(solution)/shard_map/ppermute | solution.py:843
  32.3 3.1 %collective-permute-start.7 = (bf16[16,2048]{1,0:T(8,128)(2,1)S(1)}, bf16[16,2048]{1,0:T(8,128)(2,1)S(1)}, u32[]{:S(2)}, u32[]{:S(2)}) collective-permute-start(bf16[16,2048]{1,0:T(8,128)(2,1)S(1)} %get-tuple-element.91.refs_0_), channel_id=1, source_target_pairs={{0,4},{4,0},{8,12},{12,8},{1,5},{5,1},{9,13},{13,9},{2,6},{6,2},{1... | collective-permute-start | bytes 196616 | tf_op jit(solution)/shard_map/ppermute | solution.py:843
  35.4 16.9 %collective-permute-start.10 = (bf16[1,32,64,128]{3,2,1,0:T(8,128)(2,1)S(1)}, bf16[1,32,64,128]{3,2,1,0:T(8,128)(2,1)S(1)}, u32[]{:S(2)}, u32[]{:S(2)}) collective-permute-start(bf16[1,32,64,128]{3,2,1,0:T(8,128)(2,1)S(1)} %get-tuple-element.92), channel_id=1, source_target_pairs={{0,8},{4,12},{8,0},{12,4},{1,9},{5,13},{9,1},{13,5},{2,10},{6,14},... | collective-permute-start | bytes 1572872 | tf_op jit(solution)/shard_map/ppermute | solution.py:843
  41.8 14.8 %copy-start = (bf16[1,32,2048]{2,1,0:T(8,128)(2,1)S(1)}, bf16[1,32,2048]{2,1,0:T(8,128)(2,1)}, u32[]{:S(2)}) copy-start(bf16[1,32,2048]{2,1,0:T(8,128)(2,1)} %param.20) | copy-start | bytes 393220
  41.8 14.8 %copy-start.2 = (f32[2,2048]{1,0:T(2,128)S(1)}, f32[2,2048]{1,0:T(2,128)}, u32[]{:S(2)}) copy-start(f32[2,2048]{1,0:T(2,128)} %gain_ref.1) | copy-start | bytes 49156
  41.8 20.5 %collective-permute-start.15 = (bf16[1,32,64,128]{3,2,1,0:T(8,128)(2,1)S(1)}, bf16[1,32,64,128]{3,2,1,0:T(8,128)(2,1)S(1)}, u32[]{:S(2)}, u32[]{:S(2)}) collective-permute-start(bf16[1,32,64,128]{3,2,1,0:T(8,128)(2,1)S(1)} %get-tuple-element.104), channel_id=1, source_target_pairs={{0,8},{4,12},{8,0},{12,4},{1,9},{5,13},{9,1},{13,5},{2,10},{6,14},... | collective-permute-start | bytes 1572872 | tf_op jit(solution)/shard_map/ppermute | solution.py:843
  41.9 10.4 %collective-permute-start.13 = (bf16[32,2048]{1,0:T(8,128)(2,1)S(1)}, bf16[32,2048]{1,0:T(8,128)(2,1)S(1)}, u32[]{:S(2)}, u32[]{:S(2)}) collective-permute-start(bf16[32,2048]{1,0:T(8,128)(2,1)S(1)} %out_proj.1.refs_0_), channel_id=1, source_target_pairs={{0,3},{1,0},{2,1},{3,2},{4,7},{5,4},{6,5},{7,6},{8,11},{9,8},{10,9... | collective-permute-start | bytes 393224 | tf_op jit(solution)/shard_map/ppermute | solution.py:847
  45.3 11.3 %collective-permute-start.12 = (bf16[32,2048]{1,0:T(8,128)(2,1)S(1)}, bf16[32,2048]{1,0:T(8,128)(2,1)S(1)}, u32[]{:S(2)}, u32[]{:S(2)}) collective-permute-start(bf16[32,2048]{1,0:T(8,128)(2,1)S(1)} %out_proj.1.refs_0_), channel_id=1, source_target_pairs={{0,2},{1,3},{2,0},{3,1},{4,6},{5,7},{6,4},{7,5},{8,10},{9,11},{10,... | collective-permute-start | bytes 393224 | tf_op jit(solution)/shard_map/ppermute | solution.py:847
  45.3 11.3 %collective-permute-start.11 = (bf16[32,2048]{1,0:T(8,128)(2,1)S(1)}, bf16[32,2048]{1,0:T(8,128)(2,1)S(1)}, u32[]{:S(2)}, u32[]{:S(2)}) collective-permute-start(bf16[32,2048]{1,0:T(8,128)(2,1)S(1)} %out_proj.1.refs_0_), channel_id=1, source_target_pairs={{0,1},{1,2},{2,3},{3,0},{4,5},{5,6},{6,7},{7,4},{8,9},{9,10},{10,1... | collective-permute-start | bytes 393224 | tf_op jit(solution)/shard_map/ppermute | solution.py:847
  59.6 7.3 %collective-permute-start.14 = (bf16[32,4224]{1,0:T(8,128)(2,1)S(1)}, bf16[32,4224]{1,0:T(8,128)(2,1)S(1)}, u32[]{:S(2)}, u32[]{:S(2)}) collective-permute-start(bf16[32,4224]{1,0:T(8,128)(2,1)S(1)} %get-tuple-element.102.own_ref), channel_id=1, source_target_pairs={{0,4},{4,0},{8,12},{12,8},{1,5},{5,1},{9,13},{13,9},{2,6},{6,2},{1... | collective-permute-start | bytes 811016 | tf_op jit(solution)/shard_map/ppermute | solution.py:843
  61.1 5.8 %collective-permute-start.16 = (bf16[8,10240]{1,0:T(8,128)(2,1)S(1)}, bf16[8,10240]{1,0:T(8,128)(2,1)S(1)}, u32[]{:S(2)}, u32[]{:S(2)}) collective-permute-start(bf16[8,10240]{1,0:T(8,128)(2,1)S(1)} %get-tuple-element.105), channel_id=1, source_target_pairs={{0,8},{4,12},{8,0},{12,4},{1,9},{5,13},{9,1},{13,5},{2,10},{6,14},... | collective-permute-start | bytes 491528 | tf_op jit(solution)/shard_map/ppermute | solution.py:843
  67.0 5.9 %collective-permute-start.17 = (bf16[1,32,64,128]{3,2,1,0:T(8,128)(2,1)S(1)}, bf16[1,32,64,128]{3,2,1,0:T(8,128)(2,1)S(1)}, u32[]{:S(2)}, u32[]{:S(2)}) collective-permute-start(bf16[1,32,64,128]{3,2,1,0:T(8,128)(2,1)S(1)} %collective-permute-done.10.refs_3_), channel_id=1, source_target_pairs={{0,4},{4,0},{8,12},{12,8},{1,5},{5,1},{9,13},{13,9},{2,6},{6,2},{1... | collective-permute-start | bytes 1572872 | tf_op jit(solution)/shard_map/ppermute | solution.py:843
  67.9 4.9 %collective-permute-start.18 = (bf16[1,32,64,128]{3,2,1,0:T(8,128)(2,1)S(1)}, bf16[1,32,64,128]{3,2,1,0:T(8,128)(2,1)S(1)}, u32[]{:S(2)}, u32[]{:S(2)}) collective-permute-start(bf16[1,32,64,128]{3,2,1,0:T(8,128)(2,1)S(1)} %collective-permute-done.15.refs_4_), channel_id=1, source_target_pairs={{0,4},{4,0},{8,12},{12,8},{1,5},{5,1},{9,13},{13,9},{2,6},{6,2},{1... | collective-permute-start | bytes 1572872 | tf_op jit(solution)/shard_map/ppermute | solution.py:843
  68.0 7.6 %collective-permute-start.22 = (bf16[32,4224]{1,0:T(8,128)(2,1)S(1)}, bf16[32,4224]{1,0:T(8,128)(2,1)S(1)}, u32[]{:S(2)}, u32[]{:S(2)}) collective-permute-start(bf16[32,4224]{1,0:T(8,128)(2,1)S(1)} %chip_sum.1.refs_0_), channel_id=1, source_target_pairs={{0,8},{4,12},{8,0},{12,4},{1,9},{5,13},{9,1},{13,5},{2,10},{6,14},... | collective-permute-start | bytes 811016 | tf_op jit(solution)/shard_map/ppermute | solution.py:843
  69.2 2.0 %collective-permute-start.20 = (bf16[8,10240]{1,0:T(8,128)(2,1)S(1)}, bf16[8,10240]{1,0:T(8,128)(2,1)S(1)}, u32[]{:S(2)}, u32[]{:S(2)}) collective-permute-start(bf16[8,10240]{1,0:T(8,128)(2,1)S(1)} %collective-permute-done.16.refs_2_), channel_id=1, source_target_pairs={{0,4},{4,0},{8,12},{12,8},{1,5},{5,1},{9,13},{13,9},{2,6},{6,2},{1... | collective-permute-start | bytes 491528 | tf_op jit(solution)/shard_map/ppermute | solution.py:843
  69.9 1.3 %collective-permute-start.19 = (bf16[4,10240]{1,0:T(4,128)(2,1)S(1)}, bf16[4,10240]{1,0:T(4,128)(2,1)S(1)}, u32[]{:S(2)}, u32[]{:S(2)}) collective-permute-start(bf16[4,10240]{1,0:T(4,128)(2,1)S(1)} %get-tuple-element.113), channel_id=1, source_target_pairs={{0,4},{4,0},{8,12},{12,8},{1,5},{5,1},{9,13},{13,9},{2,6},{6,2},{1... | collective-permute-start | bytes 245768 | tf_op jit(solution)/shard_map/ppermute | solution.py:843
  75.6 23.4 %collective-permute-start.26 = (bf16[2,32,64,128]{3,2,1,0:T(8,128)(2,1)S(1)}, bf16[2,32,64,128]{3,2,1,0:T(8,128)(2,1)S(1)}, u32[]{:S(2)}, u32[]{:S(2)}) collective-permute-start(bf16[2,32,64,128]{3,2,1,0:T(8,128)(2,1)S(1)} %get-tuple-element.127), channel_id=1, source_target_pairs={{0,8},{4,12},{8,0},{12,4},{1,9},{5,13},{9,1},{13,5},{2,10},{6,14},... | collective-permute-start | bytes 3145736 | tf_op jit(solution)/shard_map/ppermute | solution.py:843
  83.2 14.1 %collective-permute-start.25 = (bf16[32,2048]{1,0:T(8,128)(2,1)S(1)}, bf16[32,2048]{1,0:T(8,128)(2,1)S(1)}, u32[]{:S(2)}, u32[]{:S(2)}) collective-permute-start(bf16[32,2048]{1,0:T(8,128)(2,1)S(1)} %down_proj.1.refs_0_), channel_id=1, source_target_pairs={{0,3},{1,0},{2,1},{3,2},{4,7},{5,4},{6,5},{7,6},{8,11},{9,8},{10,9... | collective-permute-start | bytes 393224 | tf_op jit(solution)/shard_map/ppermute | solution.py:847
  84.2 13.2 %collective-permute-start.24 = (bf16[32,2048]{1,0:T(8,128)(2,1)S(1)}, bf16[32,2048]{1,0:T(8,128)(2,1)S(1)}, u32[]{:S(2)}, u32[]{:S(2)}) collective-permute-start(bf16[32,2048]{1,0:T(8,128)(2,1)S(1)} %down_proj.1.refs_0_), channel_id=1, source_target_pairs={{0,2},{1,3},{2,0},{3,1},{4,6},{5,7},{6,4},{7,5},{8,10},{9,11},{10,... | collective-permute-start | bytes 393224 | tf_op jit(solution)/shard_map/ppermute | solution.py:847
  85.3 12.1 %collective-permute-start.23 = (bf16[32,2048]{1,0:T(8,128)(2,1)S(1)}, bf16[32,2048]{1,0:T(8,128)(2,1)S(1)}, u32[]{:S(2)}, u32[]{:S(2)}) collective-permute-start(bf16[32,2048]{1,0:T(8,128)(2,1)S(1)} %down_proj.1.refs_0_), channel_id=1, source_target_pairs={{0,1},{1,2},{2,3},{3,0},{4,5},{5,6},{6,7},{7,4},{8,9},{9,10},{10,1... | collective-permute-start | bytes 393224 | tf_op jit(solution)/shard_map/ppermute | solution.py:847
  91.9 2.9 %collective-permute-start.21 = (s32[32]{0:T(128)S(1)}, s32[32]{0:T(128)S(1)}, u32[]{:S(2)}, u32[]{:S(2)}) collective-permute-start(s32[32]{0:T(128)S(1)} %bitcast.47), channel_id=1, source_target_pairs={{0,16},{16,0},{1,17},{17,1},{2,18},{18,2},{3,19},{19,3},{4,20},{20... | collective-permute-start | bytes 392 | tf_op jit(solution)/shard_map/ppermute | solution.py:979
  99.0 5.1 %collective-permute-start.27 = (bf16[2,32,64,128]{3,2,1,0:T(8,128)(2,1)S(1)}, bf16[2,32,64,128]{3,2,1,0:T(8,128)(2,1)S(1)}, u32[]{:S(2)}, u32[]{:S(2)}) collective-permute-start(bf16[2,32,64,128]{3,2,1,0:T(8,128)(2,1)S(1)} %collective-permute-done.26.refs_1_), channel_id=1, source_target_pairs={{0,4},{4,0},{8,12},{12,8},{1,5},{5,1},{9,13},{13,9},{2,6},{6,2},{1... | collective-permute-start | bytes 3145736 | tf_op jit(solution)/shard_map/ppermute | solution.py:843
  (6 other events, 13.2 us)

commit v3 on v2

--- a/solution.py
+++ b/solution.py
@@ -937,9 +937,9 @@
     dealt = deal(targets, after(message, weight_up), capacity)
     out_parts[0], arrived[1], *dealt = barrier((out_parts[0], arrived[1], *dealt))
     residual, up_part = up_proj(tokens[0], norm_gains, out_parts, weight_up)
-    sent = [to_dp(dealt[1 + hop], hop, 0) for hop in range(1, chips)]
+    sent = [to_dp(after(dealt[1 + hop], up_part), hop, 0) for hop in range(1, chips)]
     between = {at: arrived[at] for at in range(2, single)}
-    near_up, between, sent = barrier((to_dp(up_part, 0, 1), between, sent))
+    near_up, between = barrier((to_dp(up_part, 0, 1), between))
     arrived.update(between)
     up_chip = chip_sum(up_part, near_up)
     up_parts = [up_chip] + [to_dp(up_chip, hop, 0) for hop in range(1, chips)]
@@ -952,6 +952,12 @@
     final_inner, final_groups, update, keys, decay = collect(
         sources, parents, local_rows, messages, slots, inner, groups_width, lags
     )
+    chosen = after(chosen, update)
+    groups = lax.axis_size("groups")
+    longest = rounds_of(chosen, chips, local_rows)
+    for shift in range(1, groups):
+        other = lax.ppermute(chosen, "groups", [(i, (i + shift) % groups) for i in range(groups)])
+        longest = jnp.maximum(longest, rounds_of(other, chips, local_rows))
     up_parts[0], relayed, update = barrier((up_parts[0], relayed, update))
     if early > single:
         arrived[single] = send_turn(single, *up_parts)
@@ -972,16 +978,10 @@
 
     add_states(range(single))
     final_state = update_state(table, states, update, keys, decay, is_early)
-    chosen = after(chosen, final_state)
-    groups = lax.axis_size("groups")
-    longest = rounds_of(chosen, chips, local_rows)
-    for shift in range(1, groups):
-        other = lax.ppermute(chosen, "groups", [(i, (i + shift) % groups) for i in range(groups)])
-        longest = jnp.maximum(longest, rounds_of(other, chips, local_rows))
     residual, final_state, longest = barrier((residual, final_state, longest))
     beam_out = finish(residual, down_parts)
     if early > single:
-        relay(single, beam_out)
+        relay(single, final_state)
         add_states([single])
 
     more = (turns - early, *ssm_state.shape[1:])

time: 107 us -> 125 us (1.17)
  waiting for transfers between devices: 21.5 us -> 36 us
  local copies, waits for them, and re-layouts: 1.85 us -> 6.24 us
  starting transfers between devices: 28.7 us -> 26.4 us
    ppermute x6, waiting for transfers between devices: 4.32 us -> 14.9 us  [over_tensor(): lax.ppermute(value, 'tensor', [(i, (i + s) % ranks) for i in range(ranks)])]
    unnamed x25 -> x41, local copies, waits for them, and re-layouts: 0.73 us -> 5.12 us
    ppermute x19, waiting for transfers between devices: 16.5 us -> 20.2 us  [to_dp(): return lax.ppermute(value, 'dp', pairs)]
    ppermute x19, starting transfers between devices: 19.7 us -> 18.1 us  [to_dp(): return lax.ppermute(value, 'dp', pairs)]
  transfers between devices with their start and end apart: 26 -> 26, of which waited for: 12 -> 13; matrix products, arithmetic and copies ran while one was open for 3% -> 3% of each run, Pallas kernels for 40% -> 36%
where the time goes in v3:
time: 125 us; the launch traced here: 124 us
  Pallas kernels  50 us (40%)
  waiting for transfers between devices  36 us (29%)
  starting transfers between devices  26.4 us (21%)
  local copies, waits for them, and re-layouts  6.24 us (5%)
  other arithmetic  2.58 us (2%)
  between operations  2.49 us (2%)
    pallas_call x15, Pallas kernels, call(): pl.pallas_call(kernel, out_shape=outs, in_specs=in_specs, out_specs=out_s...  43 us
    ppermute x19, waiting for transfers between devices, to_dp(): return lax.ppermute(value, 'dp', pairs)  20.2 us
    ppermute x19, starting transfers between devices, to_dp(): return lax.ppermute(value, 'dp', pairs)  18.1 us
    ppermute x6, waiting for transfers between devices, over_tensor(): lax.ppermute(value, 'tensor', [(i, (i + s) % ranks) for i in range(ranks)])  14.9 us
    ppermute x6, starting transfers between devices, over_tensor(): lax.ppermute(value, 'tensor', [(i, (i + s) % ranks) for i in range(ranks)])  7.07 us
    pallas_call x2, Pallas kernels, update_state(): pl.pallas_call(functools.partial(update_kernel, kinds, is_mine), out_shap...  7.03 us
    unnamed x41, local copies, waits for them, and re-layouts  5.12 us
  transfers between devices with their start and end apart: 26, of which 13 were waited for; matrix products, arithmetic and copies ran while one was open for 3% of the time, Pallas kernels for 36%

profile of v3, /device:TPU:1, one launch (start us, length us, event | category | flops | bytes accessed | tf_op | source)
XLA Modules:
  0.0 123.8 jit_solution(10685356859229278326)
XLA Ops:
  1.5 1.7 %first_rows.1 = bf16[1,32,64,128]{3,2,1,0:T(8,128)(2,1)S(1)} custom-call(s32[4]{0:T(128)S(1)} %add_add_fusion.1.ids_ref, s32[1,32]{1,0:T(1,128)S(1)} %copy-done.12, bf16[8,32,64,128]{3,2,1,0:T(8,128)(2,1)} %refs_0_.5), custom_call_target="tpu_custom_call" | custom-call | tf_op jit(solution)/shard_map/first_rows/pallas_call | solution.py:73
  3.2 2.7 %collective-permute-start.3 = (bf16[1,32,64,128]{3,2,1,0:T(8,128)(2,1)S(1)}, bf16[1,32,64,128]{3,2,1,0:T(8,128)(2,1)S(1)}, u32[]{:S(2)}, u32[]{:S(2)}) collective-permute-start(bf16[1,32,64,128]{3,2,1,0:T(8,128)(2,1)S(1)} %first_rows.1), channel_id=1, source_target_pairs={{0,8},{4,12},{8,0},{12,4},{1,9},{5,13},{9,1},{13,5},{2,10},{6,14},... | collective-permute-start | bytes 1572872 | tf_op jit(solution)/shard_map/ppermute | solution.py:843
  5.9 3.7 %in_load.1 = (bf16[64,4096]{1,0:T(8,128)(2,1)S(1)}, bf16[32,128]{1,0:T(8,128)(2,1)S(1)}, bf16[8,2048,2,128]{3,2,1,0:T(2,128)(2,1)S(1)}) custom-call(bf16[32,2048]{1,0:T(8,128)(2,1)} %bitcast.41, f32[2,2048]{1,0:T(2,128)} %gain_ref.1, bf16[32,2048]{1,0:T(8,128)(2,1)} %bitcast.52, bf16[2048,16,2,128]{3,2,1,0:T(2,128)(2,1)} %bitcast.49), custom_call_target="tpu_custom_call" | custom-call | bytes 16777216 | tf_op jit(solution)/shard_map/in_load/pallas_call | solution.py:73
  9.6 4.4 %in_middle.1 = (bf16[64,1024]{1,0:T(8,128)(2,1)S(1)}, bf16[8,2048,2,128]{3,2,1,0:T(2,128)(2,1)S(1)}, bf16[2,2048,2,128]{3,2,1,0:T(2,128)(2,1)S(1)}) custom-call(bf16[64,4096]{1,0:T(8,128)(2,1)S(1)} %get-tuple-element.75.lhs_ref, bf16[8,4096,128]{2,1,0:T(8,128)(2,1)S(1)} %bitcast.39, bf16[2048,16,2,128]{3,2,1,0:T(2,128)(2,1)} %bitcast.50, ...), custom_call_target="tpu_custom_call" | custom-call | tf_op jit(solution)/shard_map/in_middle/pallas_call | solution.py:73
  14.2 1.9 %in_last.1.own_ref = bf16[32,4736]{1,0:T(8,128)(2,1)S(1)} custom-call(bf16[64,4096]{1,0:T(8,128)(2,1)S(1)} %get-tuple-element.75.lhs_ref, bf16[64,1024]{1,0:T(8,128)(2,1)S(1)} %get-tuple-element.77.early_ref, bf16[32,128]{1,0:T(8,128)(2,1)S(1)} %get-tuple-element.78.tail_ref, bf16[8,4096,128]{2,1,0:T(8,128)(2,1)S(1)} %bitcast.38, ...), custom_call_target="tpu_custom_call" | custom-call | tf_op jit(solution)/shard_map/in_last/pallas_call | solution.py:73
  20.3 1.3 %collective-permute-start.5 = (bf16[16,4736]{1,0:T(8,128)(2,1)S(1)}, bf16[16,4736]{1,0:T(8,128)(2,1)S(1)}, u32[]{:S(2)}, u32[]{:S(2)}) collective-permute-start(bf16[16,4736]{1,0:T(8,128)(2,1)S(1)} %get-tuple-element.87), channel_id=1, source_target_pairs={{0,8},{4,12},{8,0},{12,4},{1,9},{5,13},{9,1},{13,5},{2,10},{6,14},... | collective-permute-start | bytes 454664 | tf_op jit(solution)/shard_map/ppermute | solution.py:843
  21.9 3.1 %gather_rows.3 = (bf16[1,32,64,128]{3,2,1,0:T(8,128)(2,1)S(1)}, bf16[1,32,64,128]{3,2,1,0:T(8,128)(2,1)S(1)}, bf16[2,32,64,128]{3,2,1,0:T(8,128)(2,1)}) custom-call(s32[4]{0:T(128)S(1)} %slice.10.table_ref, bf16[8,32,64,128]{3,2,1,0:T(8,128)(2,1)} %refs_0_.5, bf16[8,32,64,128]{3,2,1,0:T(8,128)(2,1)} %collective-permute-done.4.refs_1_), custom_call_target="tpu_custom_call" | custom-call | tf_op jit(solution)/shard_map/gather_rows/pallas_call | solution.py:73
  25.2 4.2 %mixer.1 = (bf16[16,2048]{1,0:T(8,128)(2,1)S(1)}, bf16[16,10240]{1,0:T(8,128)(2,1)S(1)}) custom-call(s32[4]{0:T(128)S(1)} %add_add_fusion.ids_ref, s32[1,32]{1,0:T(1,128)S(1)} %copy-done.13, bf16[16,4736]{1,0:T(8,128)(2,1)S(1)} %get-tuple-element.86.refs_0_, bf16[16,4736]{1,0:T(8,128)(2,1)S(1)} %collective-permute-done.5.refs_1_, f32[4,2048]{1,0:T(4,128)S(1)} %copy-done.11, ...), custom_call_target="tpu_custom_call" | custom-call | tf_op jit(solution)/shard_map/mixer/pallas_call | solution.py:73
  29.3 1.6 %collective-permute-start.6 = (bf16[1,32,64,128]{3,2,1,0:T(8,128)(2,1)S(1)}, bf16[1,32,64,128]{3,2,1,0:T(8,128)(2,1)S(1)}, u32[]{:S(2)}, u32[]{:S(2)}) collective-permute-start(bf16[1,32,64,128]{3,2,1,0:T(8,128)(2,1)S(1)} %collective-permute-done.3.refs_2_), channel_id=1, source_target_pairs={{0,4},{4,0},{8,12},{12,8},{1,5},{5,1},{9,13},{13,9},{2,6},{6,2},{1... | collective-permute-start | bytes 1572872 | tf_op jit(solution)/shard_map/ppermute | solution.py:843
  30.9 1.2 collective-permute-start.9
  33.1 1.8 %collective-permute-done.9.refs_3_ = bf16[16,2048]{1,0:T(8,128)(2,1)S(1)} collective-permute-done((bf16[16,2048]{1,0:T(8,128)(2,1)S(1)}, bf16[16,2048]{1,0:T(8,128)(2,1)S(1)}, u32[]{:S(2)}, u32[]{:S(2)}) %collective-permute-start.9) | collective-permute-done | bytes 65568 | tf_op jit(solution)/shard_map/ppermute | solution.py:843
  35.4 1.7 %collective-permute-start.10 = (bf16[1,32,64,128]{3,2,1,0:T(8,128)(2,1)S(1)}, bf16[1,32,64,128]{3,2,1,0:T(8,128)(2,1)S(1)}, u32[]{:S(2)}, u32[]{:S(2)}) collective-permute-start(bf16[1,32,64,128]{3,2,1,0:T(8,128)(2,1)S(1)} %get-tuple-element.92), channel_id=1, source_target_pairs={{0,8},{4,12},{8,0},{12,4},{1,9},{5,13},{9,1},{13,5},{2,10},{6,14},... | collective-permute-start | bytes 1572872 | tf_op jit(solution)/shard_map/ppermute | solution.py:843
  37.1 4.7 %out_proj.1.refs_0_ = bf16[32,2048]{1,0:T(8,128)(2,1)S(1)} custom-call(s32[4]{0:T(128)S(1)} %add_add_fusion.ids_ref, s32[1,32]{1,0:T(1,128)S(1)} %copy-done.13, bf16[16,2048]{1,0:T(8,128)(2,1)S(1)} %get-tuple-element.91.refs_0_, bf16[16,2048]{1,0:T(8,128)(2,1)S(1)} %collective-permute-done.7.refs_1_, bf16[16,2048]{1,0:T(8,128)(2,1)S(1)} %collective-permute-done.8.refs_2_, ...), custom_call_target="tpu_custom_call" | custom-call | tf_op jit(solution)/shard_map/out_proj/pallas_call | solution.py:73
  41.9 3.4 %collective-permute-start.13 = (bf16[32,2048]{1,0:T(8,128)(2,1)S(1)}, bf16[32,2048]{1,0:T(8,128)(2,1)S(1)}, u32[]{:S(2)}, u32[]{:S(2)}) collective-permute-start(bf16[32,2048]{1,0:T(8,128)(2,1)S(1)} %out_proj.1.refs_0_), channel_id=1, source_target_pairs={{0,3},{1,0},{2,1},{3,2},{4,7},{5,4},{6,5},{7,6},{8,11},{9,8},{10,9... | collective-permute-start | bytes 393224 | tf_op jit(solution)/shard_map/ppermute | solution.py:847
  45.7 5.8 %prefetch.1.refs_4_ = bf16[2048,4096]{1,0:T(8,128)(2,1)S(1)} custom-call(bf16[2048,4096]{1,0:T(8,128)(2,1)} %from_ref), custom_call_target="tpu_custom_call" | custom-call | bytes 33554432 | tf_op jit(solution)/shard_map/prefetch/pallas_call | solution.py:73
  52.3 4.3 %collective-permute-done.12.refs_2_ = bf16[32,2048]{1,0:T(8,128)(2,1)S(1)} collective-permute-done((bf16[32,2048]{1,0:T(8,128)(2,1)S(1)}, bf16[32,2048]{1,0:T(8,128)(2,1)S(1)}, u32[]{:S(2)}, u32[]{:S(2)}) %collective-permute-start.12) | collective-permute-done | bytes 131104 | tf_op jit(solution)/shard_map/ppermute | solution.py:847
  56.6 3.0 %up_proj.1 = (f32[32,2048]{1,0:T(8,128)S(1)}, bf16[32,4224]{1,0:T(8,128)(2,1)S(1)}) custom-call(bf16[32,2048]{1,0:T(8,128)(2,1)S(1)} %bitcast.42, f32[2,2048]{1,0:T(2,128)S(1)} %copy-done.10, bf16[32,2048]{1,0:T(8,128)(2,1)S(1)} %out_proj.1.refs_0_, bf16[32,2048]{1,0:T(8,128)(2,1)S(1)} %collective-permute-done.11.refs_1_, ...), custom_call_target="tpu_custom_call" | custom-call | tf_op jit(solution)/shard_map/up_proj/pallas_call | solution.py:73
  59.6 1.5 %collective-permute-start.14 = (bf16[32,4224]{1,0:T(8,128)(2,1)S(1)}, bf16[32,4224]{1,0:T(8,128)(2,1)S(1)}, u32[]{:S(2)}, u32[]{:S(2)}) collective-permute-start(bf16[32,4224]{1,0:T(8,128)(2,1)S(1)} %get-tuple-element.102.own_ref), channel_id=1, source_target_pairs={{0,4},{4,0},{8,12},{12,8},{1,5},{5,1},{9,13},{13,9},{2,6},{6,2},{1... | collective-permute-start | bytes 811016 | tf_op jit(solution)/shard_map/ppermute | solution.py:843
  63.0 1.2 collective-permute-start.19
  64.5 3.9 %collective-permute-done.19.refs_2_ = bf16[8,10240]{1,0:T(8,128)(2,1)S(1)} collective-permute-done((bf16[8,10240]{1,0:T(8,128)(2,1)S(1)}, bf16[8,10240]{1,0:T(8,128)(2,1)S(1)}, u32[]{:S(2)}, u32[]{:S(2)}) %collective-permute-start.19) | collective-permute-done | bytes 163872 | tf_op jit(solution)/shard_map/ppermute | solution.py:843
  68.4 2.0 %collective-permute-start.20 = (bf16[8,10240]{1,0:T(8,128)(2,1)S(1)}, bf16[8,10240]{1,0:T(8,128)(2,1)S(1)}, u32[]{:S(2)}, u32[]{:S(2)}) collective-permute-start(bf16[8,10240]{1,0:T(8,128)(2,1)S(1)} %collective-permute-done.19.refs_2_), channel_id=1, source_target_pairs={{0,4},{4,0},{8,12},{12,8},{1,5},{5,1},{9,13},{13,9},{2,6},{6,2},{1... | collective-permute-start | bytes 491528 | tf_op jit(solution)/shard_map/ppermute | solution.py:843
  70.4 1.3 %collective-permute-done.18.refs_1_ = bf16[4,10240]{1,0:T(4,128)(2,1)S(1)} collective-permute-done((bf16[4,10240]{1,0:T(4,128)(2,1)S(1)}, bf16[4,10240]{1,0:T(4,128)(2,1)S(1)}, u32[]{:S(2)}, u32[]{:S(2)}) %collective-permute-start.18) | collective-permute-done | bytes 81952 | tf_op jit(solution)/shard_map/ppermute | solution.py:843
  71.7 1.7 %collect.1 = (bf16[3,8,2048]{2,1,0:T(8,128)(2,1)}, bf16[8,3,2,256]{3,2,1,0:T(2,128)(2,1)}, f32[8,2048]{1,0:T(8,128)S(1)}, f32[8,256]{1,0:T(8,128)S(1)}, f32[8,128]{1,0:T(8,128)S(1)}) custom-call(s32[4]{0:T(128)S(1)} %add_add_fusion.ids_ref, s32[1,32]{1,0:T(1,128)S(1)} %copy-done.13, bf16[4,10240]{1,0:T(4,128)(2,1)S(1)} %get-tuple-element.110.refs_0_, ...), custom_call_target="tpu_custom_call" | custom-call | tf_op jit(solution)/shard_map/collect/pallas_call | solution.py:73
  77.0 1.2 %collective-permute-start.21 = (s32[32]{0:T(128)S(1)}, s32[32]{0:T(128)S(1)}, u32[]{:S(2)}, u32[]{:S(2)}) collective-permute-start(s32[32]{0:T(128)S(1)} %bitcast.47), channel_id=1, source_target_pairs={{0,16},{16,0},{1,17},{17,1},{2,18},{18,2},{3,19},{19,3},{4,20},{20... | collective-permute-start | bytes 392 | tf_op jit(solution)/shard_map/ppermute | solution.py:959
  84.3 5.9 %update_state.2.refs_8_ = bf16[8,32,64,128]{3,2,1,0:T(8,128)(2,1)} custom-call(s32[8]{0:T(128)S(1)} %fusion.9.table_ref, bf16[8,32,64,128]{3,2,1,0:T(8,128)(2,1)} %refs_0_.5, bf16[8,32,64,128]{3,2,1,0:T(8,128)(2,1)} %collective-permute-done.4.refs_1_, bf16[1,32,64,128]{3,2,1,0:T(8,128)(2,1)S(1)} %collective-permute-done.3.refs_2_, ...), custom_call_target="tpu_custom_call" | custom-call | tf_op jit(solution)/shard_map/update_state/pallas_call | solution.py:625
  90.1 10.1 %collective-permute-done.26.refs_1_ = bf16[2,32,64,128]{3,2,1,0:T(8,128)(2,1)S(1)} collective-permute-done((bf16[2,32,64,128]{3,2,1,0:T(8,128)(2,1)}, bf16[2,32,64,128]{3,2,1,0:T(8,128)(2,1)S(1)}, u32[]{:S(2)}, u32[]{:S(2)}) %collective-permute-start.26) | collective-permute-done | bytes 1048608 | tf_op jit(solution)/shard_map/ppermute | solution.py:843
  100.2 1.3 %collective-permute-start.27 = (bf16[2,32,64,128]{3,2,1,0:T(8,128)(2,1)S(1)}, bf16[2,32,64,128]{3,2,1,0:T(8,128)(2,1)S(1)}, u32[]{:S(2)}, u32[]{:S(2)}) collective-permute-start(bf16[2,32,64,128]{3,2,1,0:T(8,128)(2,1)S(1)} %collective-permute-done.26.refs_1_), channel_id=1, source_target_pairs={{0,4},{4,0},{8,12},{12,8},{1,5},{5,1},{9,13},{13,9},{2,6},{6,2},{1... | collective-permute-start | bytes 3145736 | tf_op jit(solution)/shard_map/ppermute | solution.py:843
  101.5 6.4 %down_proj.1.refs_0_ = bf16[32,2048]{1,0:T(8,128)(2,1)S(1)} custom-call(bf16[32,4224]{1,0:T(8,128)(2,1)S(1)} %chip_sum.1.refs_0_, bf16[32,4224]{1,0:T(8,128)(2,1)S(1)} %copy-done.6, bf16[4096,2048]{1,0:T(8,128)(2,1)} %refs_2_.3), custom_call_target="tpu_custom_call" | custom-call | tf_op jit(solution)/shard_map/down_proj/pallas_call | solution.py:73
  107.9 1.9 %collective-permute-start.25 = (bf16[32,2048]{1,0:T(8,128)(2,1)S(1)}, bf16[32,2048]{1,0:T(8,128)(2,1)S(1)}, u32[]{:S(2)}, u32[]{:S(2)}) collective-permute-start(bf16[32,2048]{1,0:T(8,128)(2,1)S(1)} %down_proj.1.refs_0_), channel_id=1, source_target_pairs={{0,3},{1,0},{2,1},{3,2},{4,7},{5,4},{6,5},{7,6},{8,11},{9,8},{10,9... | collective-permute-start | bytes 393224 | tf_op jit(solution)/shard_map/ppermute | solution.py:847
  109.7 1.4 %collective-permute-start.23 = (bf16[32,2048]{1,0:T(8,128)(2,1)S(1)}, bf16[32,2048]{1,0:T(8,128)(2,1)S(1)}, u32[]{:S(2)}, u32[]{:S(2)}) collective-permute-start(bf16[32,2048]{1,0:T(8,128)(2,1)S(1)} %down_proj.1.refs_0_), channel_id=1, source_target_pairs={{0,1},{1,2},{2,3},{3,0},{4,5},{5,6},{6,7},{7,4},{8,9},{9,10},{10,1... | collective-permute-start | bytes 393224 | tf_op jit(solution)/shard_map/ppermute | solution.py:847
  111.1 1.9 %collective-permute-done.25.refs_3_ = bf16[32,2048]{1,0:T(8,128)(2,1)S(1)} collective-permute-done((bf16[32,2048]{1,0:T(8,128)(2,1)S(1)}, bf16[32,2048]{1,0:T(8,128)(2,1)S(1)}, u32[]{:S(2)}, u32[]{:S(2)}) %collective-permute-start.25) | collective-permute-done | bytes 131104 | tf_op jit(solution)/shard_map/ppermute | solution.py:847
  113.0 8.6 %collective-permute-done.24.refs_2_ = bf16[32,2048]{1,0:T(8,128)(2,1)S(1)} collective-permute-done((bf16[32,2048]{1,0:T(8,128)(2,1)S(1)}, bf16[32,2048]{1,0:T(8,128)(2,1)S(1)}, u32[]{:S(2)}, u32[]{:S(2)}) %collective-permute-start.24) | collective-permute-done | bytes 131104 | tf_op jit(solution)/shard_map/ppermute | solution.py:847
  (124 shorter events, 20.6 us)
Async XLA Ops:
  0.6 21.3 %collective-permute-start.4 = (bf16[8,32,64,128]{3,2,1,0:T(8,128)(2,1)}, bf16[8,32,64,128]{3,2,1,0:T(8,128)(2,1)}, u32[]{:S(2)}, u32[]{:S(2)}) collective-permute-start(bf16[8,32,64,128]{3,2,1,0:T(8,128)(2,1)} %refs_0_.5), channel_id=1, source_target_pairs={{0,4},{4,0},{8,12},{12,8},{1,5},{5,1},{9,13},{13,9},{2,6},{6,2},{1... | collective-permute-start | bytes 12582920 | tf_op jit(solution)/shard_map/ppermute | solution.py:843
  3.2 14.9 %collective-permute-start.3 = (bf16[1,32,64,128]{3,2,1,0:T(8,128)(2,1)S(1)}, bf16[1,32,64,128]{3,2,1,0:T(8,128)(2,1)S(1)}, u32[]{:S(2)}, u32[]{:S(2)}) collective-permute-start(bf16[1,32,64,128]{3,2,1,0:T(8,128)(2,1)S(1)} %first_rows.1), channel_id=1, source_target_pairs={{0,8},{4,12},{8,0},{12,4},{1,9},{5,13},{9,1},{13,5},{2,10},{6,14},... | collective-permute-start | bytes 1572872 | tf_op jit(solution)/shard_map/ppermute | solution.py:843
  16.0 1.7 %collective-permute-start.2 = (bf16[32,4736]{1,0:T(8,128)(2,1)S(1)}, bf16[32,4736]{1,0:T(8,128)(2,1)S(1)}, u32[]{:S(2)}, u32[]{:S(2)}) collective-permute-start(bf16[32,4736]{1,0:T(8,128)(2,1)S(1)} %in_last.1.own_ref), channel_id=1, source_target_pairs={{0,4},{4,0},{8,12},{12,8},{1,5},{5,1},{9,13},{13,9},{2,6},{6,2},{1... | collective-permute-start | bytes 909320 | tf_op jit(solution)/shard_map/ppermute | solution.py:843
  20.3 4.8 %collective-permute-start.5 = (bf16[16,4736]{1,0:T(8,128)(2,1)S(1)}, bf16[16,4736]{1,0:T(8,128)(2,1)S(1)}, u32[]{:S(2)}, u32[]{:S(2)}) collective-permute-start(bf16[16,4736]{1,0:T(8,128)(2,1)S(1)} %get-tuple-element.87), channel_id=1, source_target_pairs={{0,8},{4,12},{8,0},{12,4},{1,9},{5,13},{9,1},{13,5},{2,10},{6,14},... | collective-permute-start | bytes 454664 | tf_op jit(solution)/shard_map/ppermute | solution.py:843
  21.9 3.3 %copy-start.9 = (bf16[8,3,2048]{2,0,1:T(8,128)(2,1)S(1)}, bf16[8,3,2048]{2,0,1:T(8,128)(2,1)}, u32[]{:S(2)}) copy-start(bf16[8,3,2048]{2,0,1:T(8,128)(2,1)} %param.36) | copy-start | bytes 294916
  29.3 3.7 %collective-permute-start.6 = (bf16[1,32,64,128]{3,2,1,0:T(8,128)(2,1)S(1)}, bf16[1,32,64,128]{3,2,1,0:T(8,128)(2,1)S(1)}, u32[]{:S(2)}, u32[]{:S(2)}) collective-permute-start(bf16[1,32,64,128]{3,2,1,0:T(8,128)(2,1)S(1)} %collective-permute-done.3.refs_2_), channel_id=1, source_target_pairs={{0,4},{4,0},{8,12},{12,8},{1,5},{5,1},{9,13},{13,9},{2,6},{6,2},{1... | collective-permute-start | bytes 1572872 | tf_op jit(solution)/shard_map/ppermute | solution.py:843
  30.9 4.0 %collective-permute-start.9 = (bf16[16,2048]{1,0:T(8,128)(2,1)S(1)}, bf16[16,2048]{1,0:T(8,128)(2,1)S(1)}, u32[]{:S(2)}, u32[]{:S(2)}) collective-permute-start(bf16[16,2048]{1,0:T(8,128)(2,1)S(1)} %get-tuple-element.91.refs_0_), channel_id=1, source_target_pairs={{0,12},{4,8},{8,4},{12,0},{1,13},{5,9},{9,5},{13,1},{2,14},{6,10},... | collective-permute-start | bytes 196616 | tf_op jit(solution)/shard_map/ppermute | solution.py:843
  32.1 3.2 %collective-permute-start.8 = (bf16[16,2048]{1,0:T(8,128)(2,1)S(1)}, bf16[16,2048]{1,0:T(8,128)(2,1)S(1)}, u32[]{:S(2)}, u32[]{:S(2)}) collective-permute-start(bf16[16,2048]{1,0:T(8,128)(2,1)S(1)} %get-tuple-element.91.refs_0_), channel_id=1, source_target_pairs={{0,8},{4,12},{8,0},{12,4},{1,9},{5,13},{9,1},{13,5},{2,10},{6,14},... | collective-permute-start | bytes 196616 | tf_op jit(solution)/shard_map/ppermute | solution.py:843
  32.3 3.1 %collective-permute-start.7 = (bf16[16,2048]{1,0:T(8,128)(2,1)S(1)}, bf16[16,2048]{1,0:T(8,128)(2,1)S(1)}, u32[]{:S(2)}, u32[]{:S(2)}) collective-permute-start(bf16[16,2048]{1,0:T(8,128)(2,1)S(1)} %get-tuple-element.91.refs_0_), channel_id=1, source_target_pairs={{0,4},{4,0},{8,12},{12,8},{1,5},{5,1},{9,13},{13,9},{2,6},{6,2},{1... | collective-permute-start | bytes 196616 | tf_op jit(solution)/shard_map/ppermute | solution.py:843
  35.4 16.9 %collective-permute-start.10 = (bf16[1,32,64,128]{3,2,1,0:T(8,128)(2,1)S(1)}, bf16[1,32,64,128]{3,2,1,0:T(8,128)(2,1)S(1)}, u32[]{:S(2)}, u32[]{:S(2)}) collective-permute-start(bf16[1,32,64,128]{3,2,1,0:T(8,128)(2,1)S(1)} %get-tuple-element.92), channel_id=1, source_target_pairs={{0,8},{4,12},{8,0},{12,4},{1,9},{5,13},{9,1},{13,5},{2,10},{6,14},... | collective-permute-start | bytes 1572872 | tf_op jit(solution)/shard_map/ppermute | solution.py:843
  41.8 14.8 %copy-start = (bf16[1,32,2048]{2,1,0:T(8,128)(2,1)S(1)}, bf16[1,32,2048]{2,1,0:T(8,128)(2,1)}, u32[]{:S(2)}) copy-start(bf16[1,32,2048]{2,1,0:T(8,128)(2,1)} %param.20) | copy-start | bytes 393220
  41.8 14.8 %copy-start.10 = (f32[2,2048]{1,0:T(2,128)S(1)}, f32[2,2048]{1,0:T(2,128)}, u32[]{:S(2)}) copy-start(f32[2,2048]{1,0:T(2,128)} %gain_ref.1) | copy-start | bytes 49156
  41.8 19.4 %collective-permute-start.15 = (bf16[1,32,64,128]{3,2,1,0:T(8,128)(2,1)S(1)}, bf16[1,32,64,128]{3,2,1,0:T(8,128)(2,1)S(1)}, u32[]{:S(2)}, u32[]{:S(2)}) collective-permute-start(bf16[1,32,64,128]{3,2,1,0:T(8,128)(2,1)S(1)} %get-tuple-element.104), channel_id=1, source_target_pairs={{0,8},{4,12},{8,0},{12,4},{1,9},{5,13},{9,1},{13,5},{2,10},{6,14},... | collective-permute-start | bytes 1572872 | tf_op jit(solution)/shard_map/ppermute | solution.py:843
  41.9 10.4 %collective-permute-start.13 = (bf16[32,2048]{1,0:T(8,128)(2,1)S(1)}, bf16[32,2048]{1,0:T(8,128)(2,1)S(1)}, u32[]{:S(2)}, u32[]{:S(2)}) collective-permute-start(bf16[32,2048]{1,0:T(8,128)(2,1)S(1)} %out_proj.1.refs_0_), channel_id=1, source_target_pairs={{0,3},{1,0},{2,1},{3,2},{4,7},{5,4},{6,5},{7,6},{8,11},{9,8},{10,9... | collective-permute-start | bytes 393224 | tf_op jit(solution)/shard_map/ppermute | solution.py:847
  45.3 11.3 %collective-permute-start.12 = (bf16[32,2048]{1,0:T(8,128)(2,1)S(1)}, bf16[32,2048]{1,0:T(8,128)(2,1)S(1)}, u32[]{:S(2)}, u32[]{:S(2)}) collective-permute-start(bf16[32,2048]{1,0:T(8,128)(2,1)S(1)} %out_proj.1.refs_0_), channel_id=1, source_target_pairs={{0,2},{1,3},{2,0},{3,1},{4,6},{5,7},{6,4},{7,5},{8,10},{9,11},{10,... | collective-permute-start | bytes 393224 | tf_op jit(solution)/shard_map/ppermute | solution.py:847
  45.3 11.3 %collective-permute-start.11 = (bf16[32,2048]{1,0:T(8,128)(2,1)S(1)}, bf16[32,2048]{1,0:T(8,128)(2,1)S(1)}, u32[]{:S(2)}, u32[]{:S(2)}) collective-permute-start(bf16[32,2048]{1,0:T(8,128)(2,1)S(1)} %out_proj.1.refs_0_), channel_id=1, source_target_pairs={{0,1},{1,2},{2,3},{3,0},{4,5},{5,6},{6,7},{7,4},{8,9},{9,10},{10,1... | collective-permute-start | bytes 393224 | tf_op jit(solution)/shard_map/ppermute | solution.py:847
  59.6 15.4 %copy-start.7 = (f32[32,2048]{1,0:T(8,128)}, f32[32,2048]{1,0:T(8,128)S(1)}, u32[]{:S(2)}) copy-start(f32[32,2048]{1,0:T(8,128)S(1)} %get-tuple-element.124.residual_ref) | copy-start | bytes 786436
  59.6 2.7 %collective-permute-start.14 = (bf16[32,4224]{1,0:T(8,128)(2,1)S(1)}, bf16[32,4224]{1,0:T(8,128)(2,1)S(1)}, u32[]{:S(2)}, u32[]{:S(2)}) collective-permute-start(bf16[32,4224]{1,0:T(8,128)(2,1)S(1)} %get-tuple-element.102.own_ref), channel_id=1, source_target_pairs={{0,4},{4,0},{8,12},{12,8},{1,5},{5,1},{9,13},{13,9},{2,6},{6,2},{1... | collective-permute-start | bytes 811016 | tf_op jit(solution)/shard_map/ppermute | solution.py:843
  62.4 10.9 %collective-permute-start.16 = (bf16[1,32,64,128]{3,2,1,0:T(8,128)(2,1)S(1)}, bf16[1,32,64,128]{3,2,1,0:T(8,128)(2,1)S(1)}, u32[]{:S(2)}, u32[]{:S(2)}) collective-permute-start(bf16[1,32,64,128]{3,2,1,0:T(8,128)(2,1)S(1)} %collective-permute-done.10.refs_3_), channel_id=1, source_target_pairs={{0,4},{4,0},{8,12},{12,8},{1,5},{5,1},{9,13},{13,9},{2,6},{6,2},{1... | collective-permute-start | bytes 1572872 | tf_op jit(solution)/shard_map/ppermute | solution.py:843
  62.9 11.3 %collective-permute-start.17 = (bf16[1,32,64,128]{3,2,1,0:T(8,128)(2,1)S(1)}, bf16[1,32,64,128]{3,2,1,0:T(8,128)(2,1)S(1)}, u32[]{:S(2)}, u32[]{:S(2)}) collective-permute-start(bf16[1,32,64,128]{3,2,1,0:T(8,128)(2,1)S(1)} %collective-permute-done.15.refs_4_), channel_id=1, source_target_pairs={{0,4},{4,0},{8,12},{12,8},{1,5},{5,1},{9,13},{13,9},{2,6},{6,2},{1... | collective-permute-start | bytes 1572872 | tf_op jit(solution)/shard_map/ppermute | solution.py:843
  63.0 5.4 %collective-permute-start.19 = (bf16[8,10240]{1,0:T(8,128)(2,1)S(1)}, bf16[8,10240]{1,0:T(8,128)(2,1)S(1)}, u32[]{:S(2)}, u32[]{:S(2)}) collective-permute-start(bf16[8,10240]{1,0:T(8,128)(2,1)S(1)} %get-tuple-element.114), channel_id=1, source_target_pairs={{0,8},{4,12},{8,0},{12,4},{1,9},{5,13},{9,1},{13,5},{2,10},{6,14},... | collective-permute-start | bytes 491528 | tf_op jit(solution)/shard_map/ppermute | solution.py:843
  64.2 10.8 %collective-permute-start.22 = (bf16[32,4224]{1,0:T(8,128)(2,1)S(1)}, bf16[32,4224]{1,0:T(8,128)(2,1)S(1)}, u32[]{:S(2)}, u32[]{:S(2)}) collective-permute-start(bf16[32,4224]{1,0:T(8,128)(2,1)S(1)} %chip_sum.1.refs_0_), channel_id=1, source_target_pairs={{0,8},{4,12},{8,0},{12,4},{1,9},{5,13},{9,1},{13,5},{2,10},{6,14},... | collective-permute-start | bytes 811016 | tf_op jit(solution)/shard_map/ppermute | solution.py:843
  68.4 3.3 %collective-permute-start.20 = (bf16[8,10240]{1,0:T(8,128)(2,1)S(1)}, bf16[8,10240]{1,0:T(8,128)(2,1)S(1)}, u32[]{:S(2)}, u32[]{:S(2)}) collective-permute-start(bf16[8,10240]{1,0:T(8,128)(2,1)S(1)} %collective-permute-done.19.refs_2_), channel_id=1, source_target_pairs={{0,4},{4,0},{8,12},{12,8},{1,5},{5,1},{9,13},{13,9},{2,6},{6,2},{1... | collective-permute-start | bytes 491528 | tf_op jit(solution)/shard_map/ppermute | solution.py:843
  70.4 1.3 %collective-permute-start.18 = (bf16[4,10240]{1,0:T(4,128)(2,1)S(1)}, bf16[4,10240]{1,0:T(4,128)(2,1)S(1)}, u32[]{:S(2)}, u32[]{:S(2)}) collective-permute-start(bf16[4,10240]{1,0:T(4,128)(2,1)S(1)} %get-tuple-element.112), channel_id=1, source_target_pairs={{0,4},{4,0},{8,12},{12,8},{1,5},{5,1},{9,13},{13,9},{2,6},{6,2},{1... | collective-permute-start | bytes 245768 | tf_op jit(solution)/shard_map/ppermute | solution.py:843
  75.7 24.5 %collective-permute-start.26 = (bf16[2,32,64,128]{3,2,1,0:T(8,128)(2,1)}, bf16[2,32,64,128]{3,2,1,0:T(8,128)(2,1)S(1)}, u32[]{:S(2)}, u32[]{:S(2)}) collective-permute-start(bf16[2,32,64,128]{3,2,1,0:T(8,128)(2,1)} %get-tuple-element.127), channel_id=1, source_target_pairs={{0,8},{4,12},{8,0},{12,4},{1,9},{5,13},{9,1},{13,5},{2,10},{6,14},... | collective-permute-start | bytes 3145736 | tf_op jit(solution)/shard_map/ppermute | solution.py:843
  77.0 2.7 %collective-permute-start.21 = (s32[32]{0:T(128)S(1)}, s32[32]{0:T(128)S(1)}, u32[]{:S(2)}, u32[]{:S(2)}) collective-permute-start(s32[32]{0:T(128)S(1)} %bitcast.47), channel_id=1, source_target_pairs={{0,16},{16,0},{1,17},{17,1},{2,18},{18,2},{3,19},{19,3},{4,20},{20... | collective-permute-start | bytes 392 | tf_op jit(solution)/shard_map/ppermute | solution.py:959
  84.3 17.2 %copy-start.6 = (bf16[32,4224]{1,0:T(8,128)(2,1)S(1)}, bf16[32,4224]{1,0:T(8,128)(2,1)}, u32[]{:S(2)}) copy-start(bf16[32,4224]{1,0:T(8,128)(2,1)} %copy-done.5) | copy-start | bytes 811012
  100.2 22.2 %collective-permute-start.27 = (bf16[2,32,64,128]{3,2,1,0:T(8,128)(2,1)S(1)}, bf16[2,32,64,128]{3,2,1,0:T(8,128)(2,1)S(1)}, u32[]{:S(2)}, u32[]{:S(2)}) collective-permute-start(bf16[2,32,64,128]{3,2,1,0:T(8,128)(2,1)S(1)} %collective-permute-done.26.refs_1_), channel_id=1, source_target_pairs={{0,4},{4,0},{8,12},{12,8},{1,5},{5,1},{9,13},{13,9},{2,6},{6,2},{1... | collective-permute-start | bytes 3145736 | tf_op jit(solution)/shard_map/ppermute | solution.py:843
  107.9 5.2 %collective-permute-start.25 = (bf16[32,2048]{1,0:T(8,128)(2,1)S(1)}, bf16[32,2048]{1,0:T(8,128)(2,1)S(1)}, u32[]{:S(2)}, u32[]{:S(2)}) collective-permute-start(bf16[32,2048]{1,0:T(8,128)(2,1)S(1)} %down_proj.1.refs_0_), channel_id=1, source_target_pairs={{0,3},{1,0},{2,1},{3,2},{4,7},{5,4},{6,5},{7,6},{8,11},{9,8},{10,9... | collective-permute-start | bytes 393224 | tf_op jit(solution)/shard_map/ppermute | solution.py:847
  109.7 11.9 %collective-permute-start.24 = (bf16[32,2048]{1,0:T(8,128)(2,1)S(1)}, bf16[32,2048]{1,0:T(8,128)(2,1)S(1)}, u32[]{:S(2)}, u32[]{:S(2)}) collective-permute-start(bf16[32,2048]{1,0:T(8,128)(2,1)S(1)} %down_proj.1.refs_0_), channel_id=1, source_target_pairs={{0,2},{1,3},{2,0},{3,1},{4,6},{5,7},{6,4},{7,5},{8,10},{9,11},{10,... | collective-permute-start | bytes 393224 | tf_op jit(solution)/shard_map/ppermute | solution.py:847
  109.7 11.9 %collective-permute-start.23 = (bf16[32,2048]{1,0:T(8,128)(2,1)S(1)}, bf16[32,2048]{1,0:T(8,128)(2,1)S(1)}, u32[]{:S(2)}, u32[]{:S(2)}) collective-permute-start(bf16[32,2048]{1,0:T(8,128)(2,1)S(1)} %down_proj.1.refs_0_), channel_id=1, source_target_pairs={{0,1},{1,2},{2,3},{3,0},{4,5},{5,6},{6,7},{7,4},{8,9},{9,10},{10,1... | collective-permute-start | bytes 393224 | tf_op jit(solution)/shard_map/ppermute | solution.py:847
  111.1 10.6 %copy-start.8 = (f32[32,2048]{1,0:T(8,128)S(1)}, f32[32,2048]{1,0:T(8,128)}, u32[]{:S(2)}) copy-start(f32[32,2048]{1,0:T(8,128)} %copy-done.7) | copy-start | bytes 786436
  (14 other events, 27.2 us)
